TPU v7x, 128 devices: a whole 4x4x4 slice. The times are simulated.
128 devices in a mesh: lon: 8 (over y_hi, x), lat: 16 (over y_lo, z, core).
Axes of the slice: x: 4, y: 4 (y_hi: 2, y_lo: 2; y = y_hi * 2 + y_lo), z: 4, core: 2. Of those that a mesh axis runs over, the one named last changes fastest.
Arguments:
- probe: float32 [32, 720, 1440], P(None, 'lat', 'lon'), may hold values from -6 to 6
- residual: float32 [32, 720, 1440], P(None, 'lat', 'lon'), may hold values from -6 to 6
- lon_embed: float32 [1440, 16], replicated, may hold values from -6 to 6
- lat_embed: float32 [720, 16], replicated, may hold values from -6 to 6
- day_embed: float32 [32, 16], replicated, may hold values from -6 to 6
- scales: float32 [3], replicated, may hold values from 3 to 6
Outputs:
- products: float32 [2, 4, 32, 720, 1440], P(None, None, 'lat', 'lon')
All inputs are finite; a program needn't handle non-finite values.
Results may differ from a plain program's by a relative error of at most 0.00014.
Values sent between devices are 32-bit elements; how exact they have to be, the bound alone decides.
No kernel may reach another device: no remote copies, remote signals or barrier semaphores. Data moves between devices by JAX's collectives and lax.ppermute only.
A program may use at most 128 MiB of HBM per device.

v0:
```python
import math

import jax
import jax.numpy as jnp
from jax import lax
from jax.sharding import PartitionSpec as P


def factors(embed, scale):
    count = embed.shape[0]
    squares = jnp.sum(embed * embed, axis=1)
    inner = jnp.dot(
        embed, embed.T, precision=lax.Precision.HIGHEST, preferred_element_type=jnp.float32
    )
    dist = squares[:, None] + squares[None, :] - 2.0 * inner
    kern = jnp.exp(-dist / (2.0 * scale * scale)) / math.sqrt(count)
    deriv = kern * dist / (scale * scale * scale)
    return (kern, deriv)


def along_day(field, mat):
    return jnp.einsum("bdal,de->beal", field, mat, precision=lax.Precision.HIGHEST)


def along_lat(field, mat):
    return jnp.einsum("bdal,ae->bdel", field, mat, precision=lax.Precision.HIGHEST)


def along_lon(field, mat):
    return jnp.einsum("bdal,lm->bdam", field, mat, precision=lax.Precision.HIGHEST)


def local(probe, residual, lon_embed, lat_embed, day_embed, scales):
    lon_k, lon_g = factors(lon_embed, scales[0])
    lat_k, lat_g = factors(lat_embed, scales[1])
    day_k, day_g = factors(day_embed, scales[2])
    fields = jnp.stack([probe, residual])
    plain = along_day(fields, day_k)
    day_part = along_day(fields, day_g)
    stacked = jnp.stack([plain, day_part], axis=1)
    stacked = stacked.reshape((4,) + stacked.shape[2:])
    moved = lax.all_to_all(stacked, "lon", split_axis=1, concat_axis=3, tiled=True)
    lon_all = along_lon(moved, lon_k)
    lon_all = lon_all.reshape((2, 2) + lon_all.shape[1:])
    pairs = moved.reshape((2, 2) + moved.shape[1:])
    lon_der = along_lon(pairs[:, 0], lon_g)
    terms = jnp.stack([lon_all[:, 0], lon_all[:, 1], lon_der], axis=1)
    terms = terms.reshape((6,) + terms.shape[2:])
    sent = lax.all_to_all(terms, "lat", split_axis=3, concat_axis=2, tiled=True)
    lat_all = along_lat(sent, lat_k)
    lat_all = lat_all.reshape((2, 3) + lat_all.shape[1:])
    triples = sent.reshape((2, 3) + sent.shape[1:])
    lat_der = along_lat(triples[:, 0], lat_g)
    final = jnp.stack([lat_all[:, 0], lat_all[:, 1], lat_all[:, 2], lat_der], axis=1)
    final = final.reshape((8,) + final.shape[2:])
    placed = lax.all_to_all(
        lax.all_to_all(final, "lon", split_axis=2, concat_axis=1, tiled=True),
        "lat",
        split_axis=1,
        concat_axis=3,
        tiled=True,
    )
    return placed.reshape((2, 4) + placed.shape[1:])


def solution(mesh):
    placed = (P(None, "lat", "lon"), P(None, "lat", "lon"), P(), P(), P(), P())
    return jax.shard_map(
        local,
        mesh=mesh,
        in_specs=placed,
        out_specs=P(None, None, "lat", "lon", None),
        check_vma=False,
    )
```

profile of v0, /device:TPU:96, one launch (start us, length us, event | category | flops | bytes accessed | tf_op | source)
XLA Modules:
  0.0 846.3 jit_solution(13967362648053991152)
XLA Ops:
  0.0 1.4 fusion.64
  4.9 0.7 multiply_reduce_fusion.2
  5.6 1.0 fusion.33
  6.6 0.0 copy-start
  6.6 0.0 copy-start.1
  6.6 4.7 fusion.26
  11.3 0.0 copy-done
  11.3 0.0 copy-done.1
  11.3 2.8 fusion.27
  14.1 1.1 pad_maximum_fusion.2
  15.2 0.5 copy.83
  15.8 6.3 copy.84
  22.1 7.3 all-to-all-start
  32.7 9.8 %fusion = f32[1440,1440]{1,0:T(8,128)} fusion(f32[1440,16]{0,1:T(8,128)S(1)} %copy-done.3, f32[1440]{0:T(1024)S(1)} %multiply_reduce_fusion), kind=kOutput, calls=%fused_computation.1 | convolution fusion | flops 404352000 | bytes 8392320 | tf_op jit(solution)/shard_map/dot_general | solution.py:12
  42.5 56.2 %all-to-all-done = f32[4,32,45,180]{3,0,2,1:T(4,128)} async-done(((f32[4,32,45,180]{3,0,2,1:T(4,128)}), f32[4,32,45,180]{3,0,2,1:T(4,128)}, u32[]{:S(2)}, u32[]{:S(2)}) %all-to-all-start) | async-done | bytes 4147232 | tf_op jit(solution)/shard_map/all_to_all | solution.py:42
  98.7 8.6 %copy.85 = f32[4,4,45,8,180]{4,3,1,2,0:T(8,128)} copy(f32[4,4,45,8,180]{4,0,2,1,3:T(4,128)} %bitcast.14) | data formatting | bytes 8294400 | tf_op jit(solution)/shard_map/all_to_all | solution.py:42
  107.4 7.8 dot_general.33
  115.2 32.3 %fusion.3 = f32[2,2,4,45,1440]{4,3,2,1,0:T(8,128)S(1)} fusion(f32[1440,1440]{1,0:T(8,128)} %fusion, f32[2,2,4,45,1440]{4,2,3,1,0:T(4,128)} %dot_general.33, f32[]{:T(128)S(6)} %mul.89), kind=kOutput, calls=%fused_computation.5 | convolution fusion | flops 17922125824 | bytes 16588804 | tf_op jit(solution)/shard_map/bdal,lm->bdam/dot_general | solution.py:30
  147.5 0.0 slice-done
  147.5 0.0 slice-done.1
  147.5 0.0 slice-done.2
  147.5 0.0 slice-done.3
  147.6 13.5 %fusion.15 = f32[2,1,4,45,1440]{4,3,2,1,0:T(8,128)S(1)} fusion(f32[1440,1440]{1,0:T(8,128)S(1)} %bitcast.103, f32[]{:T(128)S(6)} %mul.92, f32[]{:T(128)S(6)} %mul.89, f32[2,1,4,45,1440]{4,2,3,1,0:T(4,128)S(1)} %slice-done.3), kind=kOutput, calls=%fused_computation.20 | convolution fusion | flops 8968320000 | bytes 12441608 | tf_op jit(solution)/shard_map/bdal,lm->bdam/dot_general | solution.py:30
  161.0 3.7 pad_maximum_fusion.1
  164.7 16.9 %copy.88 = f32[6,4,45,1440]{2,1,0,3:T(4,128)} copy(f32[6,4,45,1440]{3,2,1,0:T(8,128)} %bitcast.101) | data formatting | bytes 12441600 | tf_op jit(solution)/shard_map/reshape | solution.py:48
  181.6 27.0 %reshape.43 = f32[16,1,97200]{2,1,0:T(1,128)} reshape(f32[1440,6,4,45]{3,2,1,0:T(4,128)} %bitcast.95) | data formatting | bytes 12441600
  208.6 4.8 all-to-all-start.1
  216.2 1.9 fusion.65
  218.2 88.7 %all-to-all-done.1 = f32[16,1,97200]{2,1,0:T(1,128)} async-done(((f32[16,1,97200]{2,1,0:T(1,128)}), f32[16,1,97200]{2,1,0:T(1,128)}, u32[]{:S(2)}, u32[]{:S(2)}) %all-to-all-start.1) | async-done | bytes 6220832 | tf_op jit(solution)/shard_map/all_to_all | solution.py:49
  306.9 0.5 broadcast.9
  307.5 68.6 %reduce = f32[16,97200]{1,0:T(8,128)} reduce(f32[16,1,97200]{2,1,0:T(1,128)} %all-to-all-done.1, f32[]{:T(128)} %broadcast.9), dimensions={1}, to_apply=%all_to_all.51.reduce_sub_computation | reduce | bytes 12441604 | tf_op jit(solution)/shard_map/all_to_all | solution.py:49
  376.0 37.5 %reshape.44 = f32[1440,6,4,45]{3,2,1,0:T(4,128)} reshape(f32[16,97200]{1,0:T(8,128)} %reduce) | data formatting | bytes 12441600
  413.5 16.1 %copy.108 = f32[6,4,45,16,90]{4,3,1,2,0:T(8,128)} copy(f32[6,4,45,16,90]{2,1,0,4,3:T(4,128)} %bitcast.94) | data formatting | bytes 12441600 | tf_op jit(solution)/shard_map/all_to_all | solution.py:49
  429.6 10.3 %copy.90 = f32[6,4,16,45,90]{4,1,3,2,0:T(4,128)} copy(f32[6,4,16,45,90]{4,2,1,3,0:T(8,128)} %bitcast.100) | data formatting | bytes 12441600 | tf_op jit(solution)/shard_map/all_to_all | solution.py:49
  439.9 0.0 copy-done.2
  439.9 28.0 %fusion.5 = f32[720,6,4,90]{0,3,2,1:T(8,128)S(1)} fusion(f32[6,4,720,90]{3,1,2,0:T(4,128)} %bitcast.105, f32[720,720]{1,0:T(8,128)S(1)} %fusion.65, f32[]{:T(128)S(6)} %mul.76, f32[720]{0:T(1024)S(1)} %multiply_reduce_fusion.1), kind=kOutput, calls=%fused_computation.7 | convolution fusion | flops 13440038912 | bytes 14518084 | tf_op jit(solution)/shard_map/bdal,ae->bdel/dot_general | solution.py:26
  468.0 7.1 copy.94
  475.0 2.0 slice.28
  477.0 3.0 copy.112
  480.0 9.3 %fusion.28 = f32[2,1,4,720,90]{3,4,2,0,1:T(8,128)S(1)} fusion(f32[2,1,4,720,90]{3,4,2,0,1:T(8,128)} %copy.112, f32[720,720]{1,0:T(8,128)} %copy-done.2, f32[]{:T(128)S(6)} %mul.95, f32[]{:T(128)S(6)} %mul.76, f32[720]{0:T(1024)S(1)} %multiply_reduce_fusion.1), kind=kOutput, calls=%fused_computation.35 | convolution fusion | flops 4483123200 | bytes 6223688 | tf_op jit(solution)/shard_map/bdal,ae->bdel/dot_general | solution.py:26
  489.3 1.4 copy.95
  490.8 8.5 %pad_maximum_fusion = f32[2,4,4,720,90]{3,2,4,1,0:T(4,128)} fusion(f32[2,1,4,720,90]{3,2,4,1,0:T(4,128)S(1)} %copy.95, f32[2,3,4,720,90]{3,2,4,1,0:T(4,128)} %copy.94), kind=kLoop, calls=%fused_computation.2 | loop fusion | flops 2073600 | bytes 16588800 | tf_op jit(solution)/shard_map/stack | solution.py:54
  499.2 13.1 %copy.96 = f32[8,4,720,90]{3,0,1,2:T(8,128)} copy(f32[8,4,720,90]{2,1,3,0:T(4,128)} %bitcast.99) | data formatting | bytes 16588800 | tf_op jit(solution)/shard_map/reshape | solution.py:55
  512.3 158.3 %all_to_all.66 = f32[8,4,720,90]{3,0,1,2:T(8,128)} all-to-all(f32[8,4,720,90]{3,0,1,2:T(8,128)} %copy.96), channel_id=1, replica_groups=mesh['lon'=8,'lat'=16] {'lon'}, dimensions={2} | all-to-all | bytes 16588800 | tf_op jit(solution)/shard_map/all_to_all | solution.py:57
  670.6 9.6 %copy.98 = f32[8,8,4,90,90]{4,0,3,2,1:T(8,128)} copy(f32[8,8,4,90,90]{4,0,2,3,1:T(8,128)} %bitcast.96) | data formatting | bytes 16588800 | tf_op jit(solution)/shard_map/all_to_all | solution.py:57
  680.1 134.7 %all_to_all.67 = f32[8,32,90,90]{3,0,2,1:T(8,128)} all-to-all(f32[8,32,90,90]{3,0,2,1:T(8,128)} %bitcast.97), channel_id=1, replica_groups=mesh['lon'=8,'lat'=16] {'lat'}, dimensions={1} | all-to-all | bytes 16588800 | tf_op jit(solution)/shard_map/all_to_all | solution.py:56
  814.8 15.4 %copy.99 = f32[8,2,90,16,90]{4,3,1,2,0:T(8,128)} copy(f32[8,2,90,16,90]{4,0,2,1,3:T(8,128)} %bitcast.98) | data formatting | bytes 16588800 | tf_op jit(solution)/shard_map/all_to_all | solution.py:56
  830.3 15.7 %reshape.36 = f32[2,4,2,90,1440]{4,2,3,1,0:T(2,128)} reshape(f32[8,2,90,16,90]{4,3,1,2,0:T(8,128)} %copy.99) | data formatting | bytes 16588800 | tf_op jit(solution)/shard_map/reshape | solution.py:63
  (12 shorter events, 0.1 us)
Async XLA Ops:
  6.6 4.7 copy-start
  6.6 4.7 copy-start.1
  22.1 10.6 %copy-start.3 = (f32[1440,16]{0,1:T(8,128)S(1)}, f32[1440,16]{0,1:T(8,128)}, u32[]{:S(2)}) copy-start(f32[1440,16]{0,1:T(8,128)} %param.8) | copy-start | bytes 276484
  22.1 76.6 %all-to-all-start = ((f32[4,32,45,180]{3,0,2,1:T(4,128)}), f32[4,32,45,180]{3,0,2,1:T(4,128)}, u32[]{:S(2)}, u32[]{:S(2)}) async-start(f32[4,32,45,180]{3,0,2,1:T(4,128)} %copy.84), calls=%async_computation | async-start | bytes 11796480 | tf_op jit(solution)/shard_map/all_to_all | solution.py:42
  115.2 32.3 %slice-start = ((s8[8847360]{0:T(1024)(128)(4,1)}), s8[4194304]{0:T(1024)(128)(4,1)S(1)}, s32[]{:S(2)}) async-start(s8[8847360]{0:T(1024)(128)(4,1)} %bitcast.102), calls=%async_computation.4 | async-start | bytes 8388608
  115.2 32.3 %slice-start.1 = ((s8[8847360]{0:T(1024)(128)(4,1)}), s8[4194304]{0:T(1024)(128)(4,1)S(1)}, s32[]{:S(2)}) async-start(s8[8847360]{0:T(1024)(128)(4,1)} %bitcast.102), calls=%async_computation.5 | async-start | bytes 8388608
  115.2 32.3 %slice-start.2 = ((s8[8847360]{0:T(1024)(128)(4,1)}), s8[458752]{0:T(1024)(128)(4,1)S(1)}, s32[]{:S(2)}) async-start(s8[8847360]{0:T(1024)(128)(4,1)} %bitcast.102), calls=%async_computation.6 | async-start | bytes 917504
  115.2 32.3 %slice-start.3 = ((f32[2,2,4,45,1440]{4,2,3,1,0:T(4,128)}), f32[2,1,4,45,1440]{4,2,3,1,0:T(4,128)S(1)}, s32[]{:S(2)}) async-start(f32[2,2,4,45,1440]{4,2,3,1,0:T(4,128)} %dot_general.33), calls=%async_computation.7 | async-start | bytes 4423680 | tf_op jit(solution)/shard_map/slice | solution.py:46
  208.6 7.6 copy-start.4
  208.6 98.3 %all-to-all-start.1 = ((f32[16,1,97200]{2,1,0:T(1,128)}), f32[16,1,97200]{2,1,0:T(1,128)}, u32[]{:S(2)}, u32[]{:S(2)}) async-start(f32[16,1,97200]{2,1,0:T(1,128)} %reshape.43), calls=%async_computation.1 | async-start | bytes 12451840 | tf_op jit(solution)/shard_map/all_to_all | solution.py:49
  218.2 221.8 %copy-start.2 = (f32[720,720]{1,0:T(8,128)}, f32[720,720]{1,0:T(8,128)S(1)}, u32[]{:S(2)}) copy-start(f32[720,720]{1,0:T(8,128)S(1)} %fusion.65) | copy-start | bytes 6220804
where the time goes:
time: 860 us; the launch traced here: 846 us
  blocking collectives  293 us (34%)
  local copies, waits for them, and re-layouts  200 us (23%)
  waiting for transfers between devices  145 us (17%)
  matrix products  103 us (12%)
  other arithmetic  82.6 us (10%)
  starting transfers between devices  12.1 us (1%)
  between operations  10.1 us (1%)
    all_to_all x1, blocking collectives, local(): lax.all_to_all(final, 'lon', split_axis=2, concat_axis=1, tiled=True)  158 us
    all_to_all x1, blocking collectives, local(): lax.all_to_all(lax.all_to_all(final, 'lon', split_axis=2, concat_axis=1,...  135 us
    all_to_all x1, waiting for transfers between devices, local(): sent = lax.all_to_all(terms, 'lat', split_axis=3, concat_axis=2, tiled=True)  88.7 us
    all_to_all x1, other arithmetic, local(): sent = lax.all_to_all(terms, 'lat', split_axis=3, concat_axis=2, tiled=True)  68.6 us
    unnamed x19, local copies, waits for them, and re-layouts  67.5 us
    all_to_all x1, waiting for transfers between devices, local(): lax.all_to_all(stacked, 'lon', split_axis=1, concat_axis=3, tiled=True)  56.2 us
    dot_general x2, matrix products, along_lon(): jnp.einsum('bdal,lm->bdam', field, mat, precision=lax.Precision.HIGHEST)  45.8 us
    dot_general x2, matrix products, along_lat(): jnp.einsum('bdal,ae->bdel', field, mat, precision=lax.Precision.HIGHEST)  37.3 us
  transfers between devices with their start and end apart: 2, of which 2 were waited for; matrix products, arithmetic and copies ran while one was open for 1% of the time, Pallas kernels for 0%

commit v1 on v0

v1 whole, which is shorter than its diff:
```python
import functools
import math

import jax
import jax.numpy as jnp
from jax import lax
from jax.experimental import pallas as pl
from jax.experimental.pallas import tpu as pltpu
from jax.sharding import PartitionSpec as P

NL = 1440
NA = 720
ND = 32
F32 = jnp.float32
BF16 = jnp.bfloat16
VMEM_LIMIT = 56 * 1024 * 1024

LOCAL_LON = 180
REST = LOCAL_LON - 128
LATS = 45
SLOTS = 46
DAY_ROWS = SLOTS * 12
OUT_LATS = 90
LAT_ROWS = 544


def params(**kw):
    return pltpu.CompilerParams(vmem_limit_bytes=VMEM_LIMIT, **kw)


def dot_high(a, b, dims):
    return lax.dot_general(
        a, b, (dims, ((), ())), precision=lax.Precision.HIGHEST, preferred_element_type=F32
    )


def dot_bf16(a, b):
    return jnp.dot(a, b, preferred_element_type=F32)


def split(x):
    high = x.astype(BF16)
    low = (x - high.astype(F32)).astype(BF16)
    return high, low


def factor_pair(rows, cols, scale, count):
    inner = dot_high(rows, cols, ((1,), (1,)))
    row_sq = jnp.sum(rows * rows, axis=1, keepdims=True)
    ones = jnp.ones((8, rows.shape[1]), F32)
    col_sq = dot_high(ones, cols * cols, ((1,), (1,)))[0:1, :]
    dist = row_sq + col_sq - 2.0 * inner
    kern = jnp.exp(-dist / (2.0 * scale * scale)) * (1.0 / math.sqrt(count))
    deriv = kern * dist / (scale * scale * scale)
    return kern, deriv


def day_kernel(scales, embed, probe, residual, out, weights, rest):
    row = lax.broadcasted_iota(jnp.int32, (128, ND), 0)
    day = lax.broadcasted_iota(jnp.int32, (128, ND), 1)
    pick = (day == (row // 8) * 2 + row % 2).astype(F32)
    rows = dot_high(pick, embed[...], ((1,), (0,)))
    col = lax.broadcasted_iota(jnp.int32, (192, ND), 0)
    day = lax.broadcasted_iota(jnp.int32, (192, ND), 1)
    pick = (day == col % ND).astype(F32)
    cols = dot_high(pick, embed[...], ((1,), (0,)))
    kern, deriv = factor_pair(rows, cols, scales[2], ND)
    row = lax.broadcasted_iota(jnp.int32, (128, 192), 0)
    col = lax.broadcasted_iota(jnp.int32, (128, 192), 1)
    both = jnp.where((row // 2) % 2 == 1, deriv, kern)
    high = both.astype(BF16).astype(F32)
    part = jnp.where((col // ND) % 3 == 2, both - high, high)
    weights[...] = jnp.where((row // 4) % 2 == col // 96, part, 0.0).astype(BF16)
    rest[...] = jnp.zeros((2, ND, 128), F32)

    def operand(lat, at):
        rest[at, :, 0:REST] = probe[lat, :, 128:LOCAL_LON]
        rest[at, :, 64 : 64 + REST] = residual[lat, :, 128:LOCAL_LON]
        x = jnp.concatenate([probe[lat, :, 0:128], residual[lat, :, 0:128], rest[at]], axis=1)
        high, low = split(x)
        return [high, low, high]

    def store(pair, value):
        for dst in range(16):
            for block in range(3):
                out[dst, pl.ds(pair * 24 + block, 8, stride=3), :] = value[
                    dst * 8 : dst * 8 + 8, block * 128 : block * 128 + 128
                ]

    def step(pair, carry):
        stacked = jnp.concatenate(operand(2 * pair, 0) + operand(2 * pair + 1, 1), axis=0)
        store(pair, dot_bf16(weights[...], stacked))
        return carry

    lax.fori_loop(0, LATS // 2, step, 0)
    none = jnp.zeros((96, 384), BF16)
    stacked = jnp.concatenate(operand(LATS - 1, 0) + [none], axis=0)
    store(LATS // 2, dot_bf16(weights[...], stacked))


def day_products(scales, embed, probe, residual):
    return pl.pallas_call(
        day_kernel,
        out_shape=jax.ShapeDtypeStruct((16, DAY_ROWS, 128), F32),
        in_specs=[pl.BlockSpec(memory_space=pltpu.SMEM)]
        + [pl.BlockSpec(memory_space=pltpu.VMEM)] * 3,
        out_specs=pl.BlockSpec(memory_space=pltpu.VMEM),
        scratch_shapes=[pltpu.VMEM((128, 192), BF16), pltpu.VMEM((2, ND, 128), F32)],
        compiler_params=params(),
        name="day_products",
    )(scales, embed, probe, residual)


def factor_kernel(which, count, scales, rows, cols, high, low):
    kern, deriv = factor_pair(rows[...], cols[...], scales[which], count)
    for at, value in enumerate((kern, deriv)):
        high[at], low[at] = split(value)


def factor_halves(scales, which, count, rows, cols):
    nr, nc = rows.shape[0], cols.shape[0]
    shape = jax.ShapeDtypeStruct((2, nr, nc), BF16)
    block = pl.BlockSpec((2, 256, nc), lambda i: (0, i, 0))
    return pl.pallas_call(
        functools.partial(factor_kernel, which, count),
        grid=(nr // 256,),
        out_shape=(shape, shape),
        in_specs=[
            pl.BlockSpec(memory_space=pltpu.SMEM),
            pl.BlockSpec((256, 16), lambda i: (i, 0)),
            pl.BlockSpec((nc, 16), lambda i: (0, 0)),
        ],
        out_specs=(block, block),
        compiler_params=params(),
        cost_estimate=pl.CostEstimate(
            flops=2 * 96 * nr * nc, bytes_accessed=8 * nr * nc, transcendentals=nr * nc
        ),
        name="factors",
    )(scales, rows, cols)


def lat_kernel(op, moved, high, low, out):
    for block in range(3):
        parts = [
            split(moved[pl.ds((op * 2 + day) * 3 + block, 16 * SLOTS, stride=12), :])
            for day in range(2)
        ]
        x_high = jnp.concatenate([p[0] for p in parts], axis=1)
        x_low = jnp.concatenate([p[1] for p in parts], axis=1)
        value = dot_bf16(high[0], x_high) + dot_bf16(high[0], x_low) + dot_bf16(low[0], x_high)
        for dst in range(8):
            for day in range(2):
                out[dst, pl.ds(block * 180 + day, OUT_LATS, stride=2), :] = value[
                    dst * 96 : dst * 96 + OUT_LATS, day * 128 : day * 128 + 128
                ]


def lat_products(moved, high, low, op, which):
    factor = pl.BlockSpec((1, 768, 736), lambda i: (which, 0, 0))
    return pl.pallas_call(
        functools.partial(lat_kernel, op),
        grid=(1,),
        out_shape=jax.ShapeDtypeStruct((8, LAT_ROWS, 128), F32),
        in_specs=[pl.BlockSpec((16 * DAY_ROWS, 128), lambda i: (0, 0)), factor, factor],
        out_specs=pl.BlockSpec((8, LAT_ROWS, 128), lambda i: (0, 0, 0)),
        compiler_params=params(),
        cost_estimate=pl.CostEstimate(
            flops=2 * 3 * 768 * 768 * 768, bytes_accessed=10**7, transcendentals=0
        ),
        name="lat_products",
    )(moved, high, low)


def lon_kernel(moved, high, low, *rest):
    out, z_high, z_low = rest[-3:]

    @pl.when((pl.program_id(0) == 0) & (pl.program_id(1) == 0))
    def _():
        for src in range(8):
            at = pl.ds(src * 128, 128)
            z_high[:, at], z_low[:, at] = split(moved[src, 0:360, :])
        first = lax.broadcasted_iota(jnp.int32, (180, 128), 1) < 64
        for pair in range(4):
            one = moved[2 * pair, 360:540, :]
            two = moved[2 * pair + 1, 360:540, :]
            probe = jnp.where(first, one, pltpu.roll(two, 64, 1))
            residual = jnp.where(first, pltpu.roll(one, 64, 1), two)
            at = pl.ds(1024 + pair * 128, 128)
            z_high[:, at], z_low[:, at] = split(jnp.concatenate([probe, residual], axis=0))

    value = (
        dot_bf16(z_high[...], high[0])
        + dot_bf16(z_high[...], low[0])
        + dot_bf16(z_low[...], high[0])
    )
    out[:, 0] = value.reshape(2, OUT_LATS, 2, value.shape[1])


def lon_products(moved, high, low, operators, so_far=None):
    wide = 512
    factor = pl.BlockSpec((1, 1536, wide), lambda w, n: (w, 0, n))
    first, step = operators[0], operators[-1] - operators[0]
    in_specs = [pl.BlockSpec((8, LAT_ROWS, 128), lambda w, n: (0, 0, 0)), factor, factor]
    args = [moved, high, low]
    aliases = {}
    if so_far is not None:
        in_specs.append(pl.BlockSpec(memory_space=pl.ANY))
        args.append(so_far)
        aliases = {3: 0}
    return pl.pallas_call(
        lon_kernel,
        grid=(len(operators), pl.cdiv(NL, wide)),
        out_shape=jax.ShapeDtypeStruct((2, 4, OUT_LATS, 2, NL), F32),
        in_specs=in_specs,
        out_specs=pl.BlockSpec(
            (2, 1, OUT_LATS, 2, wide), lambda w, n: (0, first + step * w, 0, 0, n)
        ),
        scratch_shapes=[pltpu.VMEM((360, 1536), BF16)] * 2,
        input_output_aliases=aliases,
        compiler_params=params(),
        cost_estimate=pl.CostEstimate(
            flops=2 * 3 * 360 * 1536 * 1536 * len(operators),
            bytes_accessed=2 * 10**7,
            transcendentals=0,
        ),
        name="lon_products",
    )(*args)


def local(probe, residual, lon_embed, lat_embed, day_embed, scales):
    sent = day_products(
        scales, day_embed, jnp.transpose(probe, (1, 0, 2)), jnp.transpose(residual, (1, 0, 2))
    )
    moved = lax.all_to_all(sent, "lat", split_axis=0, concat_axis=0, tiled=True)
    moved = moved.reshape(16 * DAY_ROWS, 128)

    lat_rows = jnp.pad(lat_embed.reshape(8, 90, 16), ((0, 0), (0, 6), (0, 0))).reshape(768, 16)
    lat_cols = jnp.pad(lat_embed.reshape(16, 45, 16), ((0, 0), (0, 1), (0, 0))).reshape(736, 16)
    by_part = lon_embed.reshape(8, LOCAL_LON, 16)
    lon_rest = jnp.pad(by_part[:, 128:], ((0, 0), (0, 64 - REST), (0, 0)))
    lon_rows = jnp.concatenate(
        [by_part[:, :128].reshape(1024, 16), lon_rest.reshape(512, 16)], axis=0
    )
    lat_high, lat_low = factor_halves(scales, 1, NA, lat_rows, lat_cols)
    lon_high, lon_low = factor_halves(scales, 0, NL, lon_rows, lon_embed)

    result = None
    for op, which, operators in ((0, 0, (0, 2)), (1, 0, (1,)), (0, 1, (3,))):
        terms = lat_products(moved, lat_high, lat_low, op, which)
        terms = lax.all_to_all(terms, "lon", split_axis=0, concat_axis=0, tiled=True)
        result = lon_products(terms, lon_high, lon_low, operators, result)
    return jnp.transpose(result, (0, 1, 3, 2, 4))


def solution(mesh):
    placed = (P(None, "lat", "lon"), P(None, "lat", "lon"), P(), P(), P(), P())
    return jax.shard_map(
        local,
        mesh=mesh,
        in_specs=placed,
        out_specs=P(None, None, "lat", "lon", None),
        check_vma=False,
    )
```

time: 860 us -> 233 us (0.27); the launches traced: 846 us -> 232 us
  blocking collectives: 293 us -> 0 us
  local copies, waits for them, and re-layouts: 200 us -> 7.54 us
  matrix products: 103 us -> 0 us
  Pallas kernels: 0 us -> 97.4 us
  other arithmetic: 82.6 us -> 0.01 us
  waiting for transfers between devices: 145 us -> 102 us
  starting transfers between devices: 12.1 us -> 25.4 us
  between operations: 10.1 us -> 0.1 us
    all_to_all x2 -> x0, blocking collectives: 293 us -> none  [the longest x1 158 us: local(): lax.all_to_all(final, 'lon', split_axis=2, concat_axis=1, tiled=True)]
    dot_general x9 -> x0, matrix products: 103 us -> none  [the longest x2 45.8 us: along_lon(): jnp.einsum('bdal,lm->bdam', field, mat, precision=lax.Precision.HIGHEST)]
    pallas_call x0 -> x9, Pallas kernels: none -> 97.4 us  [the longest x3 36.6 us: lon_products(): pl.pallas_call(lon_kernel, grid=(len(operators), pl.cdiv(NL, wide)), out_...]
    all_to_all x1 -> x0, other arithmetic: 68.6 us -> none  [local(): sent = lax.all_to_all(terms, 'lat', split_axis=3, concat_axis=2, tiled=True)]
    unnamed x19 -> x11, local copies, waits for them, and re-layouts: 67.5 us -> 3.94 us
    all_to_all x6 -> x0, local copies, waits for them, and re-layouts: 60.6 us -> none  [the longest x3 26.9 us: local(): sent = lax.all_to_all(terms, 'lat', split_axis=3, concat_axis=2, tiled=True)]
    reshape x5 -> x7, local copies, waits for them, and re-layouts: 59.1 us -> 1.63 us  [the longest x2 1.04 us: local(): jnp.pad(lat_embed.reshape(16, 45, 16), ((0, 0), (0, 1), (0, 0)))]
    all_to_all x2 -> x4, waiting for transfers between devices: 145 us -> 102 us  [the longest x1 57 us: local(): moved = lax.all_to_all(sent, 'lat', split_axis=0, concat_axis=0, tiled=True)]
  transfers between devices with their start and end apart: 2 -> 4, of which waited for: 2 -> 3; matrix products, arithmetic and copies ran while one was open for 1% -> 2% of each run, Pallas kernels for 0% -> 30%
where the time goes in v1:
time: 233 us; the launch traced here: 232 us
  waiting for transfers between devices  102 us (44%)
  Pallas kernels  97.4 us (42%)
  starting transfers between devices  25.4 us (11%)
  local copies, waits for them, and re-layouts  7.54 us (3%)
    all_to_all x1, waiting for transfers between devices, local(): moved = lax.all_to_all(sent, 'lat', split_axis=0, concat_axis=0, tiled=True)  57 us
    all_to_all x3, waiting for transfers between devices, local(): lax.all_to_all(terms, 'lon', split_axis=0, concat_axis=0, tiled=True)  45 us
    pallas_call x3, Pallas kernels, lon_products(): pl.pallas_call(lon_kernel, grid=(len(operators), pl.cdiv(NL, wide)), out_...  36.6 us
    pallas_call x2, Pallas kernels, factor_halves(): pl.pallas_call(functools.partial(factor_kernel, which, count), grid=(nr /...  28.6 us
    pallas_call x3, Pallas kernels, lat_products(): pl.pallas_call(functools.partial(lat_kernel, op), grid=(1,), out_shape=ja...  21.7 us
    all_to_all x3, starting transfers between devices, local(): lax.all_to_all(terms, 'lon', split_axis=0, concat_axis=0, tiled=True)  19.8 us
    pallas_call x1, Pallas kernels, day_products(): pl.pallas_call(day_kernel, out_shape=jax.ShapeDtypeStruct((16, DAY_ROWS,...  10.5 us
    all_to_all x1, starting transfers between devices, local(): moved = lax.all_to_all(sent, 'lat', split_axis=0, concat_axis=0, tiled=True)  5.67 us
  transfers between devices with their start and end apart: 4, of which 3 were waited for; matrix products, arithmetic and copies ran while one was open for 2% of the time, Pallas kernels for 30%

profile of v1, /device:TPU:96, one launch (start us, length us, event | category | flops | bytes accessed | tf_op | source)
XLA Modules:
  0.0 232.4 jit_solution(15801185354658061547)
XLA Ops:
  0.0 1.4 copy.21.embed
  1.4 10.5 %day_products.1 = f32[16,552,128]{2,1,0:T(8,128)} custom-call(f32[3]{0:T(128)} %scales.5, f32[32,16]{1,0:T(8,128)} %copy.21.embed, f32[45,32,180]{2,1,0:T(8,128)} %bitcast.21, f32[45,32,180]{2,1,0:T(8,128)} %bitcast.22), custom_call_target="tpu_custom_call" | custom-call | tf_op jit(solution)/shard_map/day_products/pallas_call | solution.py:102
  11.8 0.0 copy-start.3
  11.8 5.7 %all-to-all-start = ((f32[16,552,128]{2,1,0:T(8,128)}), f32[16,552,128]{2,1,0:T(8,128)}, u32[]{:S(2)}, u32[]{:S(2)}) async-start(f32[16,552,128]{2,1,0:T(8,128)} %day_products.1), calls=%async_computation | async-start | bytes 9043968 | tf_op jit(solution)/shard_map/all_to_all | solution.py:234
  17.5 0.0 copy-done.3
  17.5 0.1 reshape.25
  17.6 0.1 reshape.27
  17.7 0.1 reshape.28
  17.9 0.9 copy.23.cols
  18.8 0.2 copy.22
  19.0 0.8 pad.12
  19.8 7.5 %factors.2 = (bf16[2,768,736]{2,1,0:T(8,128)(2,1)}, bf16[2,768,736]{2,1,0:T(8,128)(2,1)}) custom-call(f32[3]{0:T(128)} %scales.5, f32[768,16]{1,0:T(8,128)} %bitcast.23, f32[736,16]{1,0:T(8,128)} %copy.23.cols), custom_call_target="tpu_custom_call" | custom-call | flops 108527616 | bytes 4521984 | tf_op jit(solution)/shard_map/factors/pallas_call | solution.py:124
  27.2 57.0 %all-to-all-done = f32[16,552,128]{2,1,0:T(8,128)} async-done(((f32[16,552,128]{2,1,0:T(8,128)}), f32[16,552,128]{2,1,0:T(8,128)}, u32[]{:S(2)}, u32[]{:S(2)}) %all-to-all-start) | async-done | bytes 4522016 | tf_op jit(solution)/shard_map/all_to_all | solution.py:234
  84.3 7.2 %lat_products.5 = f32[8,544,128]{2,1,0:T(8,128)} custom-call(f32[8832,128]{1,0:T(8,128)} %bitcast.2.moved, bf16[2,768,736]{2,1,0:T(8,128)(2,1)} %get-tuple-element.9.high, bf16[2,768,736]{2,1,0:T(8,128)(2,1)} %get-tuple-element.10.low), custom_call_target="tpu_custom_call" | custom-call | flops 2717908992 | bytes 10000000 | tf_op jit(solution)/shard_map/lat_products/pallas_call | solution.py:160
  91.5 6.6 %all-to-all-start.3 = ((f32[8,544,128]{2,1,0:T(8,128)}), f32[8,544,128]{2,1,0:T(8,128)S(1)}, u32[]{:S(2)}, u32[]{:S(2)}) async-start(f32[8,544,128]{2,1,0:T(8,128)} %lat_products.5), calls=%async_computation.3 | async-start | bytes 4456448 | tf_op jit(solution)/shard_map/all_to_all | solution.py:250
  98.1 7.2 %lat_products.4 = f32[8,544,128]{2,1,0:T(8,128)} custom-call(f32[8832,128]{1,0:T(8,128)} %bitcast.2.moved, bf16[2,768,736]{2,1,0:T(8,128)(2,1)} %get-tuple-element.9.high, bf16[2,768,736]{2,1,0:T(8,128)(2,1)} %get-tuple-element.10.low), custom_call_target="tpu_custom_call" | custom-call | flops 2717908992 | bytes 10000000 | tf_op jit(solution)/shard_map/lat_products/pallas_call | solution.py:160
  105.4 23.1 %all-to-all-done.3.moved = f32[8,544,128]{2,1,0:T(8,128)S(1)} async-done(((f32[8,544,128]{2,1,0:T(8,128)}), f32[8,544,128]{2,1,0:T(8,128)S(1)}, u32[]{:S(2)}, u32[]{:S(2)}) %all-to-all-start.3) | async-done | bytes 2228256 | tf_op jit(solution)/shard_map/all_to_all | solution.py:250
  128.5 0.0 copy-start.1
  128.5 1.4 copy-done.1
  129.9 8.6 %all-to-all-start.2 = ((f32[8,544,128]{2,1,0:T(8,128)}), f32[8,544,128]{2,1,0:T(8,128)S(1)}, u32[]{:S(2)}, u32[]{:S(2)}) async-start(f32[8,544,128]{2,1,0:T(8,128)} %lat_products.4), calls=%async_computation.2 | async-start | bytes 4456448 | tf_op jit(solution)/shard_map/all_to_all | solution.py:250
  138.5 7.2 %lat_products.3 = f32[8,544,128]{2,1,0:T(8,128)} custom-call(f32[8832,128]{1,0:T(8,128)} %bitcast.2.moved, bf16[2,768,736]{2,1,0:T(8,128)(2,1)} %get-tuple-element.9.high, bf16[2,768,736]{2,1,0:T(8,128)(2,1)} %get-tuple-element.10.low), custom_call_target="tpu_custom_call" | custom-call | flops 2717908992 | bytes 10000000 | tf_op jit(solution)/shard_map/lat_products/pallas_call | solution.py:160
  145.7 0.0 copy-start.2
  145.7 21.9 %all-to-all-done.2.moved = f32[8,544,128]{2,1,0:T(8,128)S(1)} async-done(((f32[8,544,128]{2,1,0:T(8,128)}), f32[8,544,128]{2,1,0:T(8,128)S(1)}, u32[]{:S(2)}, u32[]{:S(2)}) %all-to-all-start.2) | async-done | bytes 2228256 | tf_op jit(solution)/shard_map/all_to_all | solution.py:250
  167.6 0.0 copy-start
  167.6 4.5 %all-to-all-start.1 = ((f32[8,544,128]{2,1,0:T(8,128)}), f32[8,544,128]{2,1,0:T(8,128)}, u32[]{:S(2)}, u32[]{:S(2)}) async-start(f32[8,544,128]{2,1,0:T(8,128)} %lat_products.3), calls=%async_computation.1 | async-start | bytes 4456448 | tf_op jit(solution)/shard_map/all_to_all | solution.py:250
  172.1 0.0 copy-done.2
  172.1 0.1 reshape.29
  172.3 0.0 copy-done
  172.3 1.1 copy.25.cols
  173.5 0.1 reshape.31
  173.6 1.2 copy.24.rows
  174.7 21.2 %factors.3 = (bf16[2,1536,1440]{2,1,0:T(8,128)(2,1)}, bf16[2,1536,1440]{2,1,0:T(8,128)(2,1)}) custom-call(f32[3]{0:T(128)} %scales.5, f32[1536,16]{1,0:T(8,128)} %copy.24.rows, f32[1440,16]{1,0:T(8,128)} %copy.25.cols), custom_call_target="tpu_custom_call" | custom-call | flops 424673280 | bytes 17694720 | tf_op jit(solution)/shard_map/factors/pallas_call | solution.py:124
  195.9 16.3 %lon_products.3.rest_0_ = f32[2,4,90,2,1440]{4,3,2,1,0:T(2,128)} custom-call(f32[8,544,128]{2,1,0:T(8,128)} %copy-done.1, bf16[2,1536,1440]{2,1,0:T(8,128)(2,1)} %get-tuple-element.11.high, bf16[2,1536,1440]{2,1,0:T(8,128)(2,1)} %get-tuple-element.12.low), custom_call_target="tpu_custom_call" | custom-call | flops 10192158720 | bytes 20000000 | tf_op jit(solution)/shard_map/lon_products/pallas_call | solution.py:210
  212.2 10.1 %lon_products.4.rest_0_ = f32[2,4,90,2,1440]{4,3,2,1,0:T(2,128)} custom-call(f32[8,544,128]{2,1,0:T(8,128)} %copy-done, bf16[2,1536,1440]{2,1,0:T(8,128)(2,1)} %get-tuple-element.11.high, bf16[2,1536,1440]{2,1,0:T(8,128)(2,1)} %get-tuple-element.12.low, f32[2,4,90,2,1440]{4,3,2,1,0:T(2,128)} %lon_products.3.rest_0_), custom_call_target="tpu_custom_call", output_to_operand_aliasing={{}: (3, {})} | custom-call | flops 5096079360 | bytes 20000000 | tf_op jit(solution)/shard_map/lon_products/pallas_call | solution.py:210
  222.3 0.0 all-to-all-done.1.moved
  222.3 10.1 %lon_products.5 = f32[2,4,90,2,1440]{4,3,2,1,0:T(2,128)} custom-call(f32[8,544,128]{2,1,0:T(8,128)} %all-to-all-done.1.moved, bf16[2,1536,1440]{2,1,0:T(8,128)(2,1)} %get-tuple-element.11.high, bf16[2,1536,1440]{2,1,0:T(8,128)(2,1)} %get-tuple-element.12.low, f32[2,4,90,2,1440]{4,3,2,1,0:T(2,128)} %lon_products.4.rest_0_), custom_call_target="tpu_custom_call", output_to_operand_aliasing={{}: (3, {})} | custom-call | flops 5096079360 | bytes 20000000 | tf_op jit(solution)/shard_map/lon_products/pallas_call | solution.py:210
  (6 shorter events, 0.1 us)
Async XLA Ops:
  11.8 5.7 %copy-start.3 = (f32[720,16]{0,1:T(8,128)S(1)}, f32[720,16]{0,1:T(8,128)}, u32[]{:S(2)}) copy-start(f32[720,16]{0,1:T(8,128)} %param.9) | copy-start | bytes 138244
  11.8 72.4 %all-to-all-start = ((f32[16,552,128]{2,1,0:T(8,128)}), f32[16,552,128]{2,1,0:T(8,128)}, u32[]{:S(2)}, u32[]{:S(2)}) async-start(f32[16,552,128]{2,1,0:T(8,128)} %day_products.1), calls=%async_computation | async-start | bytes 9043968 | tf_op jit(solution)/shard_map/all_to_all | solution.py:234
  91.5 36.9 %all-to-all-start.3 = ((f32[8,544,128]{2,1,0:T(8,128)}), f32[8,544,128]{2,1,0:T(8,128)S(1)}, u32[]{:S(2)}, u32[]{:S(2)}) async-start(f32[8,544,128]{2,1,0:T(8,128)} %lat_products.5), calls=%async_computation.3 | async-start | bytes 4456448 | tf_op jit(solution)/shard_map/all_to_all | solution.py:250
  128.5 1.4 copy-start.1
  129.9 37.7 %all-to-all-start.2 = ((f32[8,544,128]{2,1,0:T(8,128)}), f32[8,544,128]{2,1,0:T(8,128)S(1)}, u32[]{:S(2)}, u32[]{:S(2)}) async-start(f32[8,544,128]{2,1,0:T(8,128)} %lat_products.4), calls=%async_computation.2 | async-start | bytes 4456448 | tf_op jit(solution)/shard_map/all_to_all | solution.py:250
  145.7 26.4 %copy-start.2 = (f32[1440,16]{0,1:T(8,128)S(1)}, f32[1440,16]{0,1:T(8,128)}, u32[]{:S(2)}) copy-start(f32[1440,16]{0,1:T(8,128)} %param.8) | copy-start | bytes 276484
  167.6 4.7 %copy-start = (f32[8,544,128]{2,1,0:T(8,128)}, f32[8,544,128]{2,1,0:T(8,128)S(1)}, u32[]{:S(2)}) copy-start(f32[8,544,128]{2,1,0:T(8,128)S(1)} %all-to-all-done.2.moved) | copy-start | bytes 6684676
  167.6 54.7 %all-to-all-start.1 = ((f32[8,544,128]{2,1,0:T(8,128)}), f32[8,544,128]{2,1,0:T(8,128)}, u32[]{:S(2)}, u32[]{:S(2)}) async-start(f32[8,544,128]{2,1,0:T(8,128)} %lat_products.3), calls=%async_computation.1 | async-start | bytes 4456448 | tf_op jit(solution)/shard_map/all_to_all | solution.py:250

commit v2 on v1

v2 whole, which is shorter than its diff:
```python
import functools
import math

import jax
import jax.numpy as jnp
from jax import lax
from jax.experimental import pallas as pl
from jax.experimental.pallas import tpu as pltpu
from jax.sharding import PartitionSpec as P

NL = 1440
NA = 720
ND = 32
F32 = jnp.float32
BF16 = jnp.bfloat16
VMEM_LIMIT = 58 * 1024 * 1024

LOCAL_LON = 180
REST = LOCAL_LON - 128
LATS = 45
SLOTS = 46
DAY_ROWS = SLOTS * 12
OUT_LATS = 90
KIND_ROWS = 2 * OUT_LATS


def params(**kw):
    return pltpu.CompilerParams(vmem_limit_bytes=VMEM_LIMIT, **kw)


def dot_high(a, b, dims):
    return lax.dot_general(
        a, b, (dims, ((), ())), precision=lax.Precision.HIGHEST, preferred_element_type=F32
    )


def dot_halves(a_high, a_low, b_high, b_low):
    def dot(a, b):
        return jnp.dot(a, b, preferred_element_type=F32)

    return dot(a_high, b_high) + dot(a_high, b_low) + dot(a_low, b_high)


def split(x):
    high = x.astype(BF16)
    low = (x - high.astype(F32)).astype(BF16)
    return high, low


def factor_pair(rows, cols, scale, count):
    inner = dot_high(rows, cols, ((1,), (1,)))
    row_sq = jnp.sum(rows * rows, axis=1, keepdims=True)
    ones = jnp.ones((8, rows.shape[1]), F32)
    col_sq = dot_high(ones, cols * cols, ((1,), (1,)))[0:1, :]
    dist = row_sq + col_sq - 2.0 * inner
    kern = jnp.exp(-dist / (2.0 * scale * scale)) * (1.0 / math.sqrt(count))
    deriv = kern * dist / (scale * scale * scale)
    return kern, deriv


PAIRS = 4


def day_kernel(scales, embed, probe, residual, out, weights):
    step = pl.program_id(0)

    @pl.when(step == 0)
    def _():
        row = lax.broadcasted_iota(jnp.int32, (128, ND), 0)
        day = lax.broadcasted_iota(jnp.int32, (128, ND), 1)
        pick = (day == (row // 8) * 2 + row % 2).astype(F32)
        rows = dot_high(pick, embed[...], ((1,), (1,)))
        col = lax.broadcasted_iota(jnp.int32, (192, ND), 0)
        day = lax.broadcasted_iota(jnp.int32, (192, ND), 1)
        pick = (day == col % ND).astype(F32)
        cols = dot_high(pick, embed[...], ((1,), (1,)))
        kern, deriv = factor_pair(rows, cols, scales[2], ND)
        row = lax.broadcasted_iota(jnp.int32, (128, 192), 0)
        col = lax.broadcasted_iota(jnp.int32, (128, 192), 1)
        both = jnp.where((row // 2) % 2 == 1, deriv, kern)
        high = both.astype(BF16).astype(F32)
        part = jnp.where((col // ND) % 3 == 2, both - high, high)
        weights[...] = jnp.where((row // 4) % 2 == col // 96, part, 0.0).astype(BF16)

    lane = lax.broadcasted_iota(jnp.int32, (ND, 128), 1)
    none = jnp.zeros((ND, 128 - REST), F32)

    def operand(lat):
        one = jnp.concatenate([probe[lat, :, 128:LOCAL_LON], none], axis=1)
        two = jnp.concatenate([residual[lat, :, 128:LOCAL_LON], none], axis=1)
        rest = jnp.where(lane < 64, one, pltpu.roll(two, 64, 1))
        x = jnp.concatenate([probe[lat, :, 0:128], residual[lat, :, 0:128], rest], axis=1)
        x = jnp.where(step * (2 * PAIRS) + lat < LATS, x, 0.0)
        high, low = split(x)
        return [high, low, high]

    for pair in range(PAIRS):
        stacked = jnp.concatenate(operand(2 * pair) + operand(2 * pair + 1), axis=0)
        value = jnp.dot(weights[...], stacked, preferred_element_type=F32)
        for dst in range(16):
            for block in range(3):
                out[dst, pl.ds(pair * 24 + block, 8, stride=3), :] = value[
                    dst * 8 : dst * 8 + 8, block * 128 : block * 128 + 128
                ]


def day_products(scales, embed, probe, residual):
    field = pl.BlockSpec((2 * PAIRS, ND, LOCAL_LON), lambda i: (i, 0, 0))
    return pl.pallas_call(
        day_kernel,
        grid=(pl.cdiv(SLOTS, 2 * PAIRS),),
        out_shape=jax.ShapeDtypeStruct((16, DAY_ROWS, 128), F32),
        in_specs=[
            pl.BlockSpec(memory_space=pltpu.SMEM),
            pl.BlockSpec((16, ND), lambda i: (0, 0)),
            field,
            field,
        ],
        out_specs=pl.BlockSpec((16, 24 * PAIRS, 128), lambda i: (0, i, 0)),
        scratch_shapes=[pltpu.VMEM((128, 192), BF16)],
        compiler_params=params(),
        name="day_products",
    )(scales, embed, probe, residual)


def factor_kernel(which, count, scales, rows, cols, high, low):
    kern, deriv = factor_pair(rows[...], cols[...], scales[which], count)
    for at, value in enumerate((kern, deriv)):
        high[at], low[at] = split(value)


def factor_halves(scales, which, count, rows, cols):
    nr, nc = rows.shape[0], cols.shape[0]
    shape = jax.ShapeDtypeStruct((2, nr, nc), BF16)
    block = pl.BlockSpec((2, 256, nc), lambda i: (0, i, 0))
    return pl.pallas_call(
        functools.partial(factor_kernel, which, count),
        grid=(nr // 256,),
        out_shape=(shape, shape),
        in_specs=[
            pl.BlockSpec(memory_space=pltpu.SMEM),
            pl.BlockSpec((256, 16), lambda i: (i, 0)),
            pl.BlockSpec((nc, 16), lambda i: (0, 0)),
        ],
        out_specs=(block, block),
        compiler_params=params(),
        cost_estimate=pl.CostEstimate(
            flops=2 * 96 * nr * nc, bytes_accessed=8 * nr * nc, transcendentals=nr * nc
        ),
        name="factors",
    )(scales, rows, cols)


TERM_ROWS = 544


def lat_kernel(kinds, moved, *refs):
    count = len(kinds)
    factors, outs = refs[: 2 * count], refs[2 * count : 10 * count]
    held, sems = refs[10 * count :]
    copies = []
    for at, (op, _) in enumerate(kinds):
        for block in range(3):
            parts = [
                split(moved[pl.ds((op * 2 + day) * 3 + block, 16 * SLOTS, stride=12), :])
                for day in range(2)
            ]
            x_high, x_low = [jnp.concatenate([p[half] for p in parts], axis=1) for half in range(2)]
            value = dot_halves(factors[2 * at][0], factors[2 * at + 1][0], x_high, x_low)
            for step in range(8):
                for day in range(2):
                    held[8 * at + step, pl.ds(block * KIND_ROWS + day, OUT_LATS, stride=2), :] = (
                        value[step * 96 : step * 96 + OUT_LATS, day * 128 : day * 128 + 128]
                    )
        for step in range(8):
            place = 8 * at + step
            copies.append(pltpu.make_async_copy(held.at[place], outs[place], sems.at[place]))
            copies[-1].start()
    for copy in copies:
        copy.wait()


def lat_products(moved, high, low, kinds):
    count = len(kinds)
    in_specs, args = [pl.BlockSpec((16 * DAY_ROWS, 128), lambda i: (0, 0))], [moved]
    for _, which in kinds:
        in_specs += [pl.BlockSpec((1, 768, 16 * SLOTS), lambda i, which=which: (which, 0, 0))] * 2
        args += [high, low]
    terms = pl.pallas_call(
        functools.partial(lat_kernel, kinds),
        grid=(1,),
        out_shape=[jax.ShapeDtypeStruct((TERM_ROWS, 128), F32)] * (8 * count),
        in_specs=in_specs,
        out_specs=[pl.BlockSpec(memory_space=pl.ANY)] * (8 * count),
        scratch_shapes=[
            pltpu.VMEM((8 * count, TERM_ROWS, 128), F32),
            pltpu.SemaphoreType.DMA((8 * count,)),
        ],
        compiler_params=params(),
        cost_estimate=pl.CostEstimate(
            flops=2 * 3 * 768 * 768 * 768 * count, bytes_accessed=10**7, transcendentals=0
        ),
        name="lat_products",
    )(*args)
    return [terms[8 * at : 8 * at + 8] for at in range(count)]


def lay_out(read, put, rows):
    for src in range(8):
        for field in range(2):
            put(field, src, read(src, field))
    first = lax.broadcasted_iota(jnp.int32, (rows, 128), 1) < 64
    for pair in range(4):
        one, two = read(2 * pair, 2), read(2 * pair + 1, 2)
        put(0, 8 + pair, jnp.where(first, one, pltpu.roll(two, 64, 1)))
        put(1, 8 + pair, jnp.where(first, pltpu.roll(one, 64, 1), two))


def by_day(value, start):
    return value[start : start + KIND_ROWS].reshape(OUT_LATS, 2, value.shape[1])


FIELD_ROWS = 192


def lon_kernel(count, *refs):
    terms, factors = refs[:8], refs[8 : 8 + 2 * count]
    out, z_high, z_low = refs[-3:]

    @pl.when(pl.program_id(0) == 0)
    def _():
        def read(step, block):
            return terms[step][block * KIND_ROWS : block * KIND_ROWS + KIND_ROWS, :]

        def put(field, col, value):
            at = pl.ds(col * 128, 128)
            for z, half in zip((z_high, z_low), split(value)):
                z[field * FIELD_ROWS : field * FIELD_ROWS + KIND_ROWS, at] = half

        lay_out(read, put, KIND_ROWS)

    for at in range(count):
        high, low = factors[2 * at : 2 * at + 2]
        value = dot_halves(z_high[...], z_low[...], high[0], low[0])
        for field in range(2):
            out[field, at, 0] = by_day(value, field * FIELD_ROWS)


def lon_products(terms, high, low, operators, so_far=None, wide=512):
    count = len(operators)
    high_at, low_at = divmod(operators[0], 2)
    in_specs = [pl.BlockSpec((TERM_ROWS, 128), lambda n: (0, 0))] * 8
    args = list(terms)
    for which in range(count):
        in_specs += [pl.BlockSpec((1, 1536, wide), lambda n, which=which: (which, 0, n))] * 2
        args += [high, low]
    aliases = {}
    if so_far is not None:
        aliases = {len(args): 0}
        in_specs.append(pl.BlockSpec(memory_space=pl.ANY))
        args.append(so_far)
    return pl.pallas_call(
        functools.partial(lon_kernel, count),
        grid=(pl.cdiv(NL, wide),),
        out_shape=jax.ShapeDtypeStruct((2, 2, 2, OUT_LATS, 2, NL), F32),
        in_specs=in_specs,
        out_specs=pl.BlockSpec(
            (2, count, 1, OUT_LATS, 2, wide), lambda n: (0, high_at, low_at, 0, 0, n)
        ),
        scratch_shapes=[pltpu.VMEM((2 * FIELD_ROWS, 1536), BF16)] * 2,
        input_output_aliases=aliases,
        compiler_params=params(),
        cost_estimate=pl.CostEstimate(
            flops=2 * 3 * 360 * 1536 * 1536 * count, bytes_accessed=2 * 10**7, transcendentals=0
        ),
        name="lon_products",
    )(*args)


ORDER = (1, 6, 4, 3, 2, 5, 7)


def local(probe, residual, lon_embed, lat_embed, day_embed, scales):
    sent = day_products(
        scales, day_embed.T, jnp.transpose(probe, (1, 0, 2)), jnp.transpose(residual, (1, 0, 2))
    )
    moved = lax.all_to_all(sent, "lat", split_axis=0, concat_axis=0, tiled=True)
    moved = moved.reshape(16 * DAY_ROWS, 128)

    order = jnp.bitwise_xor(lax.axis_index("lon"), jnp.arange(8))
    by_block = lat_embed.reshape(8, OUT_LATS, 16)[order]
    lat_rows = jnp.pad(by_block, ((0, 0), (0, 6), (0, 0))).reshape(768, 16)
    lat_cols = jnp.pad(lat_embed.reshape(16, LATS, 16), ((0, 0), (0, SLOTS - LATS), (0, 0)))
    by_block = lon_embed.reshape(8, LOCAL_LON, 16)[order]
    lon_rest = jnp.pad(by_block[:, 128:], ((0, 0), (0, 64 - REST), (0, 0)))
    lon_rows = jnp.concatenate(
        [by_block[:, :128].reshape(1024, 16), lon_rest.reshape(512, 16)], axis=0
    )
    lat_factors = factor_halves(scales, 1, NA, lat_rows, lat_cols.reshape(16 * SLOTS, 16))
    lon_factors = factor_halves(scales, 0, NL, lon_rows, lon_embed)
    moved, lat_factors, lon_factors = lax.optimization_barrier((moved, lat_factors, lon_factors))

    def exchanged(terms):
        there = {0: terms[0]}
        for step in ORDER:
            pairs = [(i, i ^ step) for i in range(8)]
            there[step] = lax.ppermute(terms[step], "lon", pairs)
        return [there[step] for step in range(8)]

    (plain,) = lat_products(moved, *lat_factors, ((0, 0),))
    by_day, by_lat = lat_products(moved, *lat_factors, ((1, 0), (0, 1)))
    result = lon_products(exchanged(plain), *lon_factors, (0, 2))
    result = lon_products(exchanged(by_day), *lon_factors, (1,), result)
    result = lon_products(exchanged(by_lat), *lon_factors, (3,), result)
    result = result.reshape(2, 4, OUT_LATS, 2, NL)
    return jnp.transpose(result, (0, 1, 3, 2, 4))


def solution(mesh):
    placed = (P(None, "lat", "lon"), P(None, "lat", "lon"), P(), P(), P(), P())
    return jax.shard_map(
        local,
        mesh=mesh,
        in_specs=placed,
        out_specs=P(None, None, "lat", "lon", None),
        check_vma=False,
    )
```

time: 233 us -> 200 us (0.86)
  waiting for transfers between devices: 102 us -> 52.7 us
  starting transfers between devices: 25.4 us -> 48.4 us
  Pallas kernels: 97.4 us -> 91.1 us
    all_to_all x3 -> x0, waiting for transfers between devices: 45 us -> none  [local(): lax.all_to_all(terms, 'lon', split_axis=0, concat_axis=0, tiled=True)]
    ppermute x0 -> x21, starting transfers between devices: none -> 42.7 us  [exchanged(): there[step] = lax.ppermute(terms[step], 'lon', pairs)]
    all_to_all x1, waiting for transfers between devices: 57 us -> 32.1 us  [local(): moved = lax.all_to_all(sent, 'lat', split_axis=0, concat_axis=0, tiled=True)]
    ppermute x0 -> x21, waiting for transfers between devices: none -> 20.6 us  [exchanged(): there[step] = lax.ppermute(terms[step], 'lon', pairs)]
    all_to_all x3 -> x0, starting transfers between devices: 19.8 us -> none  [local(): lax.all_to_all(terms, 'lon', split_axis=0, concat_axis=0, tiled=True)]
    pallas_call x7 -> x6, Pallas kernels: 68.7 us -> 62.6 us  [the longest x3 37.3 us: lon_products(): pl.pallas_call(functools.partial(lon_kernel, count), grid=(pl.cdiv(NL, wi...]
  transfers between devices with their start and end apart: 4 -> 22, of which waited for: 3 -> 8; matrix products, arithmetic and copies ran while one was open for 2% -> 3% of each run, Pallas kernels for 30% -> 33%
where the time goes in v2:
time: 200 us
  Pallas kernels  91.1 us (46%)
  waiting for transfers between devices  52.7 us (26%)
  starting transfers between devices  48.4 us (24%)
  local copies, waits for them, and re-layouts  7.07 us (4%)
    ppermute x21, starting transfers between devices, exchanged(): there[step] = lax.ppermute(terms[step], 'lon', pairs)  42.7 us
    pallas_call x3, Pallas kernels, lon_products(): pl.pallas_call(functools.partial(lon_kernel, count), grid=(pl.cdiv(NL, wi...  37.3 us
    all_to_all x1, waiting for transfers between devices, local(): moved = lax.all_to_all(sent, 'lat', split_axis=0, concat_axis=0, tiled=True)  32.1 us
    pallas_call x2, Pallas kernels, factor_halves(): pl.pallas_call(functools.partial(factor_kernel, which, count), grid=(nr /...  28.5 us
    ppermute x21, waiting for transfers between devices, exchanged(): there[step] = lax.ppermute(terms[step], 'lon', pairs)  20.6 us
    pallas_call x2, Pallas kernels, lat_products(): pl.pallas_call(functools.partial(lat_kernel, kinds), grid=(1,), out_shape...  18.2 us
    pallas_call x1, Pallas kernels, day_products(): pl.pallas_call(day_kernel, grid=(pl.cdiv(SLOTS, 2 * PAIRS),), out_shape=j...  7.06 us
    all_to_all x1, starting transfers between devices, local(): moved = lax.all_to_all(sent, 'lat', split_axis=0, concat_axis=0, tiled=True)  5.68 us
  transfers between devices with their start and end apart: 22, of which 8 were waited for; matrix products, arithmetic and copies ran while one was open for 3% of the time, Pallas kernels for 33%

profile of v2, /device:TPU:96, one launch (start us, length us, event | category | flops | bytes accessed | tf_op | source)
XLA Modules:
  0.0 199.6 jit_solution(10123632545643728455)
XLA Ops:
  0.0 7.1 %day_products.1 = f32[16,552,128]{2,1,0:T(8,128)} custom-call(f32[3]{0:T(128)} %scales.5, f32[16,32]{1,0:T(8,128)} %bitcast.28, f32[45,32,180]{2,1,0:T(8,128)} %bitcast.25, f32[45,32,180]{2,1,0:T(8,128)} %bitcast.26), custom_call_target="tpu_custom_call" | custom-call | tf_op jit(solution)/shard_map/day_products/pallas_call | solution.py:109
  7.1 5.7 %all-to-all-start = ((f32[16,552,128]{2,1,0:T(8,128)}), f32[16,552,128]{2,1,0:T(8,128)}, u32[]{:S(2)}, u32[]{:S(2)}) async-start(f32[16,552,128]{2,1,0:T(8,128)} %day_products.1), calls=%async_computation | async-start | bytes 9043968 | tf_op jit(solution)/shard_map/all_to_all | solution.py:287
  12.8 0.1 reshape.46
  13.0 0.1 reshape.48
  13.1 1.2 copy.36.cols
  14.4 0.6 gather_fusion
  15.0 0.6 gather_fusion.1
  15.7 0.1 reshape.47
  15.8 0.9 copy.31.cols
  16.7 0.2 copy.37
  16.9 0.8 pad.12.clone
  17.7 1.2 copy.35.rows
  18.9 7.4 %factors.2 = (bf16[2,768,736]{2,1,0:T(8,128)(2,1)}, bf16[2,768,736]{2,1,0:T(8,128)(2,1)}) custom-call(f32[3]{0:T(128)} %scales.5, f32[768,16]{1,0:T(8,128)} %bitcast.27, f32[736,16]{1,0:T(8,128)} %copy.31.cols), custom_call_target="tpu_custom_call" | custom-call | flops 108527616 | bytes 4521984 | tf_op jit(solution)/shard_map/factors/pallas_call | solution.py:136
  26.3 21.1 %factors.3 = (bf16[2,1536,1440]{2,1,0:T(8,128)(2,1)}, bf16[2,1536,1440]{2,1,0:T(8,128)(2,1)}) custom-call(f32[3]{0:T(128)} %scales.5, f32[1536,16]{1,0:T(8,128)} %copy.35.rows, f32[1440,16]{1,0:T(8,128)} %copy.36.cols), custom_call_target="tpu_custom_call" | custom-call | flops 424673280 | bytes 17694720 | tf_op jit(solution)/shard_map/factors/pallas_call | solution.py:136
  47.4 32.1 %all-to-all-done = f32[16,552,128]{2,1,0:T(8,128)} async-done(((f32[16,552,128]{2,1,0:T(8,128)}), f32[16,552,128]{2,1,0:T(8,128)}, u32[]{:S(2)}, u32[]{:S(2)}) %all-to-all-start) | async-done | bytes 4522016 | tf_op jit(solution)/shard_map/all_to_all | solution.py:287
  79.5 7.3 %lat_products.3 = (f32[544,128]{1,0:T(8,128)}, f32[544,128]{1,0:T(8,128)}, f32[544,128]{1,0:T(8,128)}, f32[544,128]{1,0:T(8,128)}, f32[544,128]{1,0:T(8,128)}, /...) custom-call(f32[8832,128]{1,0:T(8,128)} %bitcast.3.moved, ...), custom_call_target="tpu_custom_call" | custom-call | flops 2717908992 | bytes 10000000 | tf_op jit(solution)/shard_map/lat_products/pallas_call | solution.py:189
  86.8 1.6 collective-permute-start.14
  88.4 2.7 %collective-permute-start.15 = (f32[544,128]{1,0:T(8,128)}, f32[544,128]{1,0:T(8,128)S(1)}, u32[]{:S(2)}, u32[]{:S(2)}) collective-permute-start(f32[544,128]{1,0:T(8,128)} %get-tuple-element.65), channel_id=1, source_target_pairs={{0,32},{16,48},{32,0},{48,16},{64,96},{80,112},{96,64},{112,80},{1... | collective-permute-start | bytes 835592 | tf_op jit(solution)/shard_map/ppermute | solution.py:307
  91.1 0.5 collective-permute-start.16
  91.6 2.9 %collective-permute-start.17 = (f32[544,128]{1,0:T(8,128)}, f32[544,128]{1,0:T(8,128)S(1)}, u32[]{:S(2)}, u32[]{:S(2)}) collective-permute-start(f32[544,128]{1,0:T(8,128)} %get-tuple-element.67), channel_id=1, source_target_pairs={{0,64},{16,80},{32,96},{48,112},{64,0},{80,16},{96,32},{112,48},{1... | collective-permute-start | bytes 835592 | tf_op jit(solution)/shard_map/ppermute | solution.py:307
  94.5 0.3 collective-permute-start.18
  94.9 1.7 collective-permute-done.14.refs_1_
  96.6 5.4 %collective-permute-start.19 = (f32[544,128]{1,0:T(8,128)}, f32[544,128]{1,0:T(8,128)S(1)}, u32[]{:S(2)}, u32[]{:S(2)}) collective-permute-start(f32[544,128]{1,0:T(8,128)} %get-tuple-element.69), channel_id=1, source_target_pairs={{0,96},{16,112},{32,64},{48,80},{64,32},{80,48},{96,0},{112,16},{1... | collective-permute-start | bytes 835592 | tf_op jit(solution)/shard_map/ppermute | solution.py:307
  102.0 10.9 %lat_products.2 = (f32[544,128]{1,0:T(8,128)}, f32[544,128]{1,0:T(8,128)}, f32[544,128]{1,0:T(8,128)}, f32[544,128]{1,0:T(8,128)}, f32[544,128]{1,0:T(8,128)}, /...) custom-call(f32[8832,128]{1,0:T(8,128)} %bitcast.3.moved, ...), custom_call_target="tpu_custom_call" | custom-call | flops 5435817984 | bytes 10000000 | tf_op jit(solution)/shard_map/lat_products/pallas_call | solution.py:189
  112.9 1.3 collective-permute-start.20
  114.2 3.6 %collective-permute-start.1 = (f32[544,128]{1,0:T(8,128)}, f32[544,128]{1,0:T(8,128)S(1)}, u32[]{:S(2)}, u32[]{:S(2)}) collective-permute-start(f32[544,128]{1,0:T(8,128)} %get-tuple-element.47), channel_id=1, source_target_pairs={{0,32},{16,48},{32,0},{48,16},{64,96},{80,112},{96,64},{112,80},{1... | collective-permute-start | bytes 835592 | tf_op jit(solution)/shard_map/ppermute | solution.py:307
  117.8 0.7 collective-permute-done.19.refs_6_
  118.5 1.8 collective-permute-start.8
  120.4 6.1 %collective-permute-done.20.refs_7_ = f32[544,128]{1,0:T(8,128)S(1)} collective-permute-done((f32[544,128]{1,0:T(8,128)S(1)}, f32[544,128]{1,0:T(8,128)S(1)}, u32[]{:S(2)}, u32[]{:S(2)}) %collective-permute-start.20) | collective-permute-done | bytes 278560 | tf_op jit(solution)/shard_map/ppermute | solution.py:307
  126.5 0.8 collective-permute-start.10
  127.3 4.2 %collective-permute-done.1.refs_2_ = f32[544,128]{1,0:T(8,128)S(1)} collective-permute-done((f32[544,128]{1,0:T(8,128)}, f32[544,128]{1,0:T(8,128)S(1)}, u32[]{:S(2)}, u32[]{:S(2)}) %collective-permute-start.1) | collective-permute-done | bytes 278560 | tf_op jit(solution)/shard_map/ppermute | solution.py:307
  131.5 1.7 collective-permute-start.11
  133.2 2.7 %collective-permute-done.7.refs_1_ = f32[544,128]{1,0:T(8,128)S(1)} collective-permute-done((f32[544,128]{1,0:T(8,128)}, f32[544,128]{1,0:T(8,128)S(1)}, u32[]{:S(2)}, u32[]{:S(2)}) %collective-permute-start.7) | collective-permute-done | bytes 278560 | tf_op jit(solution)/shard_map/ppermute | solution.py:307
  135.9 3.9 %collective-permute-start.12 = (f32[544,128]{1,0:T(8,128)}, f32[544,128]{1,0:T(8,128)S(1)}, u32[]{:S(2)}, u32[]{:S(2)}) collective-permute-start(f32[544,128]{1,0:T(8,128)} %get-tuple-element.61), channel_id=1, source_target_pairs={{0,96},{16,112},{32,64},{48,80},{64,32},{80,48},{96,0},{112,16},{1... | collective-permute-start | bytes 835592 | tf_op jit(solution)/shard_map/ppermute | solution.py:307
  139.8 3.6 %collective-permute-done.8.refs_2_ = f32[544,128]{1,0:T(8,128)S(1)} collective-permute-done((f32[544,128]{1,0:T(8,128)}, f32[544,128]{1,0:T(8,128)S(1)}, u32[]{:S(2)}, u32[]{:S(2)}) %collective-permute-start.8) | collective-permute-done | bytes 278560 | tf_op jit(solution)/shard_map/ppermute | solution.py:307
  143.5 3.4 %collective-permute-start.13 = (f32[544,128]{1,0:T(8,128)}, f32[544,128]{1,0:T(8,128)S(1)}, u32[]{:S(2)}, u32[]{:S(2)}) collective-permute-start(f32[544,128]{1,0:T(8,128)} %get-tuple-element.62), channel_id=1, source_target_pairs={{0,112},{16,96},{32,80},{48,64},{64,48},{80,32},{96,16},{112,0},{1... | collective-permute-start | bytes 835592 | tf_op jit(solution)/shard_map/ppermute | solution.py:307
  147.0 17.2 %lon_products.3.refs_10_ = f32[2,2,2,90,2,1440]{5,4,3,2,1,0:T(2,128)} custom-call(f32[544,128]{1,0:T(8,128)} %get-tuple-element.63.refs_0_, f32[544,128]{1,0:T(8,128)} %copy-done.3, f32[544,128]{1,0:T(8,128)} %copy-done.4, f32[544,128]{1,0:T(8,128)} %copy-done.5, f32[544,128]{1,0:T(8,128)} %copy-done.6, f32[544,128]{1,0:T(8,128)} %copy-done.7, ...), custom_call_target="tpu_custom_call" | custom-call | flops 10192158720 | bytes 20000000 | tf_op jit(solution)/shard_map/lon_products/pallas_call | solution.py:262
  164.2 2.2 %collective-permute-start.2 = (f32[544,128]{1,0:T(8,128)S(1)}, f32[544,128]{1,0:T(8,128)S(1)}, u32[]{:S(2)}, u32[]{:S(2)}) collective-permute-start(f32[544,128]{1,0:T(8,128)S(1)} %copy-done.27), channel_id=1, source_target_pairs={{0,48},{16,32},{32,16},{48,0},{64,112},{80,96},{96,80},{112,64},{1... | collective-permute-start | bytes 835592 | tf_op jit(solution)/shard_map/ppermute | solution.py:307
  166.4 0.7 collective-permute-start.3
  167.2 0.6 collective-permute-start.4
  167.8 4.5 %collective-permute-start.5 = (f32[544,128]{1,0:T(8,128)S(1)}, f32[544,128]{1,0:T(8,128)S(1)}, u32[]{:S(2)}, u32[]{:S(2)}) collective-permute-start(f32[544,128]{1,0:T(8,128)S(1)} %copy-done.24), channel_id=1, source_target_pairs={{0,96},{16,112},{32,64},{48,80},{64,32},{80,48},{96,0},{112,16},{1... | collective-permute-start | bytes 835592 | tf_op jit(solution)/shard_map/ppermute | solution.py:307
  172.3 4.7 %collective-permute-start.6 = (f32[544,128]{1,0:T(8,128)S(1)}, f32[544,128]{1,0:T(8,128)S(1)}, u32[]{:S(2)}, u32[]{:S(2)}) collective-permute-start(f32[544,128]{1,0:T(8,128)S(1)} %copy-done.23), channel_id=1, source_target_pairs={{0,112},{16,96},{32,80},{48,64},{64,48},{80,32},{96,16},{112,0},{1... | collective-permute-start | bytes 835592 | tf_op jit(solution)/shard_map/ppermute | solution.py:307
  177.1 10.1 %lon_products.4.refs_10_ = f32[2,2,2,90,2,1440]{5,4,3,2,1,0:T(2,128)} custom-call(f32[544,128]{1,0:T(8,128)} %get-tuple-element.55.refs_0_, f32[544,128]{1,0:T(8,128)} %copy-done.9, f32[544,128]{1,0:T(8,128)} %copy-done.10, f32[544,128]{1,0:T(8,128)} %copy-done.11, f32[544,128]{1,0:T(8,128)} %copy-done.13, ...), custom_call_target="tpu_custom_call", output_to_operand_aliasing={{}: (10, {})} | custom-call | flops 5096079360 | bytes 20000000 | tf_op jit(solution)/shard_map/lon_products/pallas_call | solution.py:262
  187.2 1.4 collective-permute-done.3.refs_4_
  188.6 0.7 copy-done.17
  189.3 0.1 copy-done.19
  189.5 0.1 copy-done.21
  189.6 10.0 %lon_products.5 = f32[2,2,2,90,2,1440]{5,4,3,2,1,0:T(2,128)} custom-call(f32[544,128]{1,0:T(8,128)} %get-tuple-element.45.refs_0_, f32[544,128]{1,0:T(8,128)} %copy-done.1, f32[544,128]{1,0:T(8,128)} %copy-done.2, f32[544,128]{1,0:T(8,128)} %copy-done.15, f32[544,128]{1,0:T(8,128)} %copy-done.17, ...), custom_call_target="tpu_custom_call", output_to_operand_aliasing={{}: (10, {})} | custom-call | flops 5096079360 | bytes 20000000 | tf_op jit(solution)/shard_map/lon_products/pallas_call | solution.py:262
  (84 shorter events, 0.5 us)
Async XLA Ops:
  7.1 5.7 %copy-start.22 = (f32[720,16]{0,1:T(8,128)S(1)}, f32[720,16]{0,1:T(8,128)}, u32[]{:S(2)}) copy-start(f32[720,16]{0,1:T(8,128)} %param.9) | copy-start | bytes 138244
  7.1 5.9 %copy-start = (f32[1440,16]{0,1:T(8,128)S(1)}, f32[1440,16]{0,1:T(8,128)}, u32[]{:S(2)}) copy-start(f32[1440,16]{0,1:T(8,128)} %param.8) | copy-start | bytes 276484
  7.1 72.4 %all-to-all-start = ((f32[16,552,128]{2,1,0:T(8,128)}), f32[16,552,128]{2,1,0:T(8,128)}, u32[]{:S(2)}, u32[]{:S(2)}) async-start(f32[16,552,128]{2,1,0:T(8,128)} %day_products.1), calls=%async_computation | async-start | bytes 9043968 | tf_op jit(solution)/shard_map/all_to_all | solution.py:287
  86.8 9.8 %collective-permute-start.14 = (f32[544,128]{1,0:T(8,128)}, f32[544,128]{1,0:T(8,128)S(1)}, u32[]{:S(2)}, u32[]{:S(2)}) collective-permute-start(f32[544,128]{1,0:T(8,128)} %get-tuple-element.64), channel_id=1, source_target_pairs={{0,16},{16,0},{32,48},{48,32},{64,80},{80,64},{96,112},{112,96},{1... | collective-permute-start | bytes 835592 | tf_op jit(solution)/shard_map/ppermute | solution.py:307
  88.4 24.5 %collective-permute-start.15 = (f32[544,128]{1,0:T(8,128)}, f32[544,128]{1,0:T(8,128)S(1)}, u32[]{:S(2)}, u32[]{:S(2)}) collective-permute-start(f32[544,128]{1,0:T(8,128)} %get-tuple-element.65), channel_id=1, source_target_pairs={{0,32},{16,48},{32,0},{48,16},{64,96},{80,112},{96,64},{112,80},{1... | collective-permute-start | bytes 835592 | tf_op jit(solution)/shard_map/ppermute | solution.py:307
  91.1 23.0 %collective-permute-start.16 = (f32[544,128]{1,0:T(8,128)}, f32[544,128]{1,0:T(8,128)S(1)}, u32[]{:S(2)}, u32[]{:S(2)}) collective-permute-start(f32[544,128]{1,0:T(8,128)} %get-tuple-element.66), channel_id=1, source_target_pairs={{0,48},{16,32},{32,16},{48,0},{64,112},{80,96},{96,80},{112,64},{1... | collective-permute-start | bytes 835592 | tf_op jit(solution)/shard_map/ppermute | solution.py:307
  91.6 22.6 %collective-permute-start.17 = (f32[544,128]{1,0:T(8,128)}, f32[544,128]{1,0:T(8,128)S(1)}, u32[]{:S(2)}, u32[]{:S(2)}) collective-permute-start(f32[544,128]{1,0:T(8,128)} %get-tuple-element.67), channel_id=1, source_target_pairs={{0,64},{16,80},{32,96},{48,112},{64,0},{80,16},{96,32},{112,48},{1... | collective-permute-start | bytes 835592 | tf_op jit(solution)/shard_map/ppermute | solution.py:307
  94.5 23.3 %collective-permute-start.18 = (f32[544,128]{1,0:T(8,128)}, f32[544,128]{1,0:T(8,128)S(1)}, u32[]{:S(2)}, u32[]{:S(2)}) collective-permute-start(f32[544,128]{1,0:T(8,128)} %get-tuple-element.68), channel_id=1, source_target_pairs={{0,80},{16,64},{32,112},{48,96},{64,16},{80,0},{96,48},{112,32},{1... | collective-permute-start | bytes 835592 | tf_op jit(solution)/shard_map/ppermute | solution.py:307
  96.6 16.2 %copy-start.3 = (f32[544,128]{1,0:T(8,128)}, f32[544,128]{1,0:T(8,128)S(1)}, u32[]{:S(2)}) copy-start(f32[544,128]{1,0:T(8,128)S(1)} %collective-permute-done.14.refs_1_) | copy-start | bytes 835588
  96.6 16.3 %copy-start.28 = (f32[544,128]{1,0:T(8,128)S(1)}, f32[544,128]{1,0:T(8,128)}, u32[]{:S(2)}) copy-start(f32[544,128]{1,0:T(8,128)} %get-tuple-element.70) | copy-start | bytes 835588
  96.6 21.9 %collective-permute-start.19 = (f32[544,128]{1,0:T(8,128)}, f32[544,128]{1,0:T(8,128)S(1)}, u32[]{:S(2)}, u32[]{:S(2)}) collective-permute-start(f32[544,128]{1,0:T(8,128)} %get-tuple-element.69), channel_id=1, source_target_pairs={{0,96},{16,112},{32,64},{48,80},{64,32},{80,48},{96,0},{112,16},{1... | collective-permute-start | bytes 835592 | tf_op jit(solution)/shard_map/ppermute | solution.py:307
  112.9 34.0 %copy-start.4 = (f32[544,128]{1,0:T(8,128)}, f32[544,128]{1,0:T(8,128)S(1)}, u32[]{:S(2)}) copy-start(f32[544,128]{1,0:T(8,128)S(1)} %collective-permute-done.15.refs_2_) | copy-start | bytes 835588
  112.9 13.6 %collective-permute-start.20 = (f32[544,128]{1,0:T(8,128)S(1)}, f32[544,128]{1,0:T(8,128)S(1)}, u32[]{:S(2)}, u32[]{:S(2)}) collective-permute-start(f32[544,128]{1,0:T(8,128)S(1)} %copy-done.28), channel_id=1, source_target_pairs={{0,112},{16,96},{32,80},{48,64},{64,48},{80,32},{96,16},{112,0},{1... | collective-permute-start | bytes 835592 | tf_op jit(solution)/shard_map/ppermute | solution.py:307
  114.2 32.7 %copy-start.5 = (f32[544,128]{1,0:T(8,128)}, f32[544,128]{1,0:T(8,128)S(1)}, u32[]{:S(2)}) copy-start(f32[544,128]{1,0:T(8,128)S(1)} %collective-permute-done.16.refs_3_) | copy-start | bytes 835588
  114.2 12.3 %collective-permute-start = (f32[544,128]{1,0:T(8,128)}, f32[544,128]{1,0:T(8,128)S(1)}, u32[]{:S(2)}, u32[]{:S(2)}) collective-permute-start(f32[544,128]{1,0:T(8,128)} %get-tuple-element.46), channel_id=1, source_target_pairs={{0,16},{16,0},{32,48},{48,32},{64,80},{80,64},{96,112},{112,96},{1... | collective-permute-start | bytes 835592 | tf_op jit(solution)/shard_map/ppermute | solution.py:307
  114.2 32.7 %copy-start.6 = (f32[544,128]{1,0:T(8,128)}, f32[544,128]{1,0:T(8,128)S(1)}, u32[]{:S(2)}) copy-start(f32[544,128]{1,0:T(8,128)S(1)} %collective-permute-done.17.refs_4_) | copy-start | bytes 835588
  114.2 17.3 %collective-permute-start.1 = (f32[544,128]{1,0:T(8,128)}, f32[544,128]{1,0:T(8,128)S(1)}, u32[]{:S(2)}, u32[]{:S(2)}) collective-permute-start(f32[544,128]{1,0:T(8,128)} %get-tuple-element.47), channel_id=1, source_target_pairs={{0,32},{16,48},{32,0},{48,16},{64,96},{80,112},{96,64},{112,80},{1... | collective-permute-start | bytes 835592 | tf_op jit(solution)/shard_map/ppermute | solution.py:307
  117.8 29.1 %copy-start.7 = (f32[544,128]{1,0:T(8,128)}, f32[544,128]{1,0:T(8,128)S(1)}, u32[]{:S(2)}) copy-start(f32[544,128]{1,0:T(8,128)S(1)} %collective-permute-done.18.refs_5_) | copy-start | bytes 835588
  117.8 18.1 %collective-permute-start.7 = (f32[544,128]{1,0:T(8,128)}, f32[544,128]{1,0:T(8,128)S(1)}, u32[]{:S(2)}, u32[]{:S(2)}) collective-permute-start(f32[544,128]{1,0:T(8,128)} %get-tuple-element.56), channel_id=1, source_target_pairs={{0,16},{16,0},{32,48},{48,32},{64,80},{80,64},{96,112},{112,96},{1... | collective-permute-start | bytes 835592 | tf_op jit(solution)/shard_map/ppermute | solution.py:307
  118.5 28.4 %copy-start.8 = (f32[544,128]{1,0:T(8,128)}, f32[544,128]{1,0:T(8,128)S(1)}, u32[]{:S(2)}) copy-start(f32[544,128]{1,0:T(8,128)S(1)} %collective-permute-done.19.refs_6_) | copy-start | bytes 835588
  118.5 24.9 %collective-permute-start.8 = (f32[544,128]{1,0:T(8,128)}, f32[544,128]{1,0:T(8,128)S(1)}, u32[]{:S(2)}, u32[]{:S(2)}) collective-permute-start(f32[544,128]{1,0:T(8,128)} %get-tuple-element.57), channel_id=1, source_target_pairs={{0,32},{16,48},{32,0},{48,16},{64,96},{80,112},{96,64},{112,80},{1... | collective-permute-start | bytes 835592 | tf_op jit(solution)/shard_map/ppermute | solution.py:307
  126.5 20.5 %copy-start.12 = (f32[544,128]{1,0:T(8,128)}, f32[544,128]{1,0:T(8,128)S(1)}, u32[]{:S(2)}) copy-start(f32[544,128]{1,0:T(8,128)S(1)} %collective-permute-done.20.refs_7_) | copy-start | bytes 835588
  126.5 37.7 %collective-permute-start.9 = (f32[544,128]{1,0:T(8,128)}, f32[544,128]{1,0:T(8,128)S(1)}, u32[]{:S(2)}, u32[]{:S(2)}) collective-permute-start(f32[544,128]{1,0:T(8,128)} %get-tuple-element.58), channel_id=1, source_target_pairs={{0,48},{16,32},{32,16},{48,0},{64,112},{80,96},{96,80},{112,64},{1... | collective-permute-start | bytes 835592 | tf_op jit(solution)/shard_map/ppermute | solution.py:307
  126.5 37.7 %copy-start.1 = (f32[544,128]{1,0:T(8,128)}, f32[544,128]{1,0:T(8,128)S(1)}, u32[]{:S(2)}) copy-start(f32[544,128]{1,0:T(8,128)S(1)} %collective-permute-done.refs_1_) | copy-start | bytes 835588
  126.5 39.9 %collective-permute-start.10 = (f32[544,128]{1,0:T(8,128)}, f32[544,128]{1,0:T(8,128)S(1)}, u32[]{:S(2)}, u32[]{:S(2)}) collective-permute-start(f32[544,128]{1,0:T(8,128)} %get-tuple-element.59), channel_id=1, source_target_pairs={{0,64},{16,80},{32,96},{48,112},{64,0},{80,16},{96,32},{112,48},{1... | collective-permute-start | bytes 835592 | tf_op jit(solution)/shard_map/ppermute | solution.py:307
  131.5 32.7 %copy-start.2 = (f32[544,128]{1,0:T(8,128)}, f32[544,128]{1,0:T(8,128)S(1)}, u32[]{:S(2)}) copy-start(f32[544,128]{1,0:T(8,128)S(1)} %collective-permute-done.1.refs_2_) | copy-start | bytes 835588
  131.5 35.6 %collective-permute-start.11 = (f32[544,128]{1,0:T(8,128)}, f32[544,128]{1,0:T(8,128)S(1)}, u32[]{:S(2)}, u32[]{:S(2)}) collective-permute-start(f32[544,128]{1,0:T(8,128)} %get-tuple-element.60), channel_id=1, source_target_pairs={{0,80},{16,64},{32,112},{48,96},{64,16},{80,0},{96,48},{112,32},{1... | collective-permute-start | bytes 835592 | tf_op jit(solution)/shard_map/ppermute | solution.py:307
  135.9 28.3 %copy-start.9 = (f32[544,128]{1,0:T(8,128)}, f32[544,128]{1,0:T(8,128)S(1)}, u32[]{:S(2)}) copy-start(f32[544,128]{1,0:T(8,128)S(1)} %collective-permute-done.7.refs_1_) | copy-start | bytes 835588
  135.9 31.8 %collective-permute-start.12 = (f32[544,128]{1,0:T(8,128)}, f32[544,128]{1,0:T(8,128)S(1)}, u32[]{:S(2)}, u32[]{:S(2)}) collective-permute-start(f32[544,128]{1,0:T(8,128)} %get-tuple-element.61), channel_id=1, source_target_pairs={{0,96},{16,112},{32,64},{48,80},{64,32},{80,48},{96,0},{112,16},{1... | collective-permute-start | bytes 835592 | tf_op jit(solution)/shard_map/ppermute | solution.py:307
  143.5 20.7 %copy-start.10 = (f32[544,128]{1,0:T(8,128)}, f32[544,128]{1,0:T(8,128)S(1)}, u32[]{:S(2)}) copy-start(f32[544,128]{1,0:T(8,128)S(1)} %collective-permute-done.8.refs_2_) | copy-start | bytes 835588
  143.5 28.9 %collective-permute-start.13 = (f32[544,128]{1,0:T(8,128)}, f32[544,128]{1,0:T(8,128)S(1)}, u32[]{:S(2)}, u32[]{:S(2)}) collective-permute-start(f32[544,128]{1,0:T(8,128)} %get-tuple-element.62), channel_id=1, source_target_pairs={{0,112},{16,96},{32,80},{48,64},{64,48},{80,32},{96,16},{112,0},{1... | collective-permute-start | bytes 835592 | tf_op jit(solution)/shard_map/ppermute | solution.py:307
  146.9 17.3 %copy-start.27 = (f32[544,128]{1,0:T(8,128)S(1)}, f32[544,128]{1,0:T(8,128)}, u32[]{:S(2)}) copy-start(f32[544,128]{1,0:T(8,128)} %get-tuple-element.48) | copy-start | bytes 835588
  147.0 19.5 %copy-start.26 = (f32[544,128]{1,0:T(8,128)S(1)}, f32[544,128]{1,0:T(8,128)}, u32[]{:S(2)}) copy-start(f32[544,128]{1,0:T(8,128)} %get-tuple-element.49) | copy-start | bytes 835588
  147.0 20.2 %copy-start.25 = (f32[544,128]{1,0:T(8,128)S(1)}, f32[544,128]{1,0:T(8,128)}, u32[]{:S(2)}) copy-start(f32[544,128]{1,0:T(8,128)} %get-tuple-element.50) | copy-start | bytes 835588
  147.0 20.8 %copy-start.24 = (f32[544,128]{1,0:T(8,128)S(1)}, f32[544,128]{1,0:T(8,128)}, u32[]{:S(2)}) copy-start(f32[544,128]{1,0:T(8,128)} %get-tuple-element.51) | copy-start | bytes 835588
  147.0 25.3 %copy-start.23 = (f32[544,128]{1,0:T(8,128)S(1)}, f32[544,128]{1,0:T(8,128)}, u32[]{:S(2)}) copy-start(f32[544,128]{1,0:T(8,128)} %get-tuple-element.52) | copy-start | bytes 835588
  164.2 12.8 %copy-start.11 = (f32[544,128]{1,0:T(8,128)}, f32[544,128]{1,0:T(8,128)S(1)}, u32[]{:S(2)}) copy-start(f32[544,128]{1,0:T(8,128)S(1)} %collective-permute-done.9.refs_3_) | copy-start | bytes 835588
  164.2 22.9 %collective-permute-start.2 = (f32[544,128]{1,0:T(8,128)S(1)}, f32[544,128]{1,0:T(8,128)S(1)}, u32[]{:S(2)}, u32[]{:S(2)}) collective-permute-start(f32[544,128]{1,0:T(8,128)S(1)} %copy-done.27), channel_id=1, source_target_pairs={{0,48},{16,32},{32,16},{48,0},{64,112},{80,96},{96,80},{112,64},{1... | collective-permute-start | bytes 835592 | tf_op jit(solution)/shard_map/ppermute | solution.py:307
  166.4 10.6 %copy-start.13 = (f32[544,128]{1,0:T(8,128)}, f32[544,128]{1,0:T(8,128)S(1)}, u32[]{:S(2)}) copy-start(f32[544,128]{1,0:T(8,128)S(1)} %collective-permute-done.10.refs_4_) | copy-start | bytes 835588
  166.4 22.1 %collective-permute-start.3 = (f32[544,128]{1,0:T(8,128)S(1)}, f32[544,128]{1,0:T(8,128)S(1)}, u32[]{:S(2)}, u32[]{:S(2)}) collective-permute-start(f32[544,128]{1,0:T(8,128)S(1)} %copy-done.26), channel_id=1, source_target_pairs={{0,64},{16,80},{32,96},{48,112},{64,0},{80,16},{96,32},{112,48},{1... | collective-permute-start | bytes 835592 | tf_op jit(solution)/shard_map/ppermute | solution.py:307
  167.2 9.9 %copy-start.14 = (f32[544,128]{1,0:T(8,128)}, f32[544,128]{1,0:T(8,128)S(1)}, u32[]{:S(2)}) copy-start(f32[544,128]{1,0:T(8,128)S(1)} %collective-permute-done.11.refs_5_) | copy-start | bytes 835588
  167.2 21.4 %collective-permute-start.4 = (f32[544,128]{1,0:T(8,128)S(1)}, f32[544,128]{1,0:T(8,128)S(1)}, u32[]{:S(2)}, u32[]{:S(2)}) collective-permute-start(f32[544,128]{1,0:T(8,128)S(1)} %copy-done.25), channel_id=1, source_target_pairs={{0,80},{16,64},{32,112},{48,96},{64,16},{80,0},{96,48},{112,32},{1... | collective-permute-start | bytes 835592 | tf_op jit(solution)/shard_map/ppermute | solution.py:307
  167.8 9.3 %copy-start.16 = (f32[544,128]{1,0:T(8,128)}, f32[544,128]{1,0:T(8,128)S(1)}, u32[]{:S(2)}) copy-start(f32[544,128]{1,0:T(8,128)S(1)} %collective-permute-done.12.refs_6_) | copy-start | bytes 835588
  167.8 20.8 %collective-permute-start.5 = (f32[544,128]{1,0:T(8,128)S(1)}, f32[544,128]{1,0:T(8,128)S(1)}, u32[]{:S(2)}, u32[]{:S(2)}) collective-permute-start(f32[544,128]{1,0:T(8,128)S(1)} %copy-done.24), channel_id=1, source_target_pairs={{0,96},{16,112},{32,64},{48,80},{64,32},{80,48},{96,0},{112,16},{1... | collective-permute-start | bytes 835592 | tf_op jit(solution)/shard_map/ppermute | solution.py:307
  172.3 4.8 %copy-start.18 = (f32[544,128]{1,0:T(8,128)}, f32[544,128]{1,0:T(8,128)S(1)}, u32[]{:S(2)}) copy-start(f32[544,128]{1,0:T(8,128)S(1)} %collective-permute-done.13.refs_7_) | copy-start | bytes 835588
  172.3 16.3 %collective-permute-start.6 = (f32[544,128]{1,0:T(8,128)S(1)}, f32[544,128]{1,0:T(8,128)S(1)}, u32[]{:S(2)}, u32[]{:S(2)}) collective-permute-start(f32[544,128]{1,0:T(8,128)S(1)} %copy-done.23), channel_id=1, source_target_pairs={{0,112},{16,96},{32,80},{48,64},{64,48},{80,32},{96,16},{112,0},{1... | collective-permute-start | bytes 835592 | tf_op jit(solution)/shard_map/ppermute | solution.py:307
  187.2 1.5 copy-start.15
  188.6 1.0 copy-start.21
  (3 other events, 2.4 us)

commit v3 on v2

--- a/solution.py
+++ b/solution.py
@@ -24,8 +24,8 @@
 KIND_ROWS = 2 * OUT_LATS
 
 
-def params(**kw):
-    return pltpu.CompilerParams(vmem_limit_bytes=VMEM_LIMIT, **kw)
+def params(mib=58):
+    return pltpu.CompilerParams(vmem_limit_bytes=mib * 1024 * 1024)
 
 
 def dot_high(a, b, dims):
@@ -129,9 +129,9 @@
         high[at], low[at] = split(value)
 
 
-def factor_halves(scales, which, count, rows, cols):
+def factor_halves(scales, which, count, rows, cols, held=False):
     nr, nc = rows.shape[0], cols.shape[0]
-    shape = jax.ShapeDtypeStruct((2, nr, nc), BF16)
+    shape = (pltpu.VMEM if held else jax.ShapeDtypeStruct)((2, nr, nc), BF16)
     block = pl.BlockSpec((2, 256, nc), lambda i: (0, i, 0))
     return pl.pallas_call(
         functools.partial(factor_kernel, which, count),
@@ -143,7 +143,7 @@
             pl.BlockSpec((nc, 16), lambda i: (0, 0)),
         ],
         out_specs=(block, block),
-        compiler_params=params(),
+        compiler_params=params(30),
         cost_estimate=pl.CostEstimate(
             flops=2 * 96 * nr * nc, bytes_accessed=8 * nr * nc, transcendentals=nr * nc
         ),
@@ -185,7 +185,7 @@
     in_specs, args = [pl.BlockSpec((16 * DAY_ROWS, 128), lambda i: (0, 0))], [moved]
     for _, which in kinds:
         in_specs += [pl.BlockSpec((1, 768, 16 * SLOTS), lambda i, which=which: (which, 0, 0))] * 2
-        args += [high, low]
+        args += [pltpu.with_memory_space_constraint(x, pltpu.HBM) for x in (high, low)]
     terms = pl.pallas_call(
         functools.partial(lat_kernel, kinds),
         grid=(1,),
@@ -196,7 +196,7 @@
             pltpu.VMEM((8 * count, TERM_ROWS, 128), F32),
             pltpu.SemaphoreType.DMA((8 * count,)),
         ],
-        compiler_params=params(),
+        compiler_params=params(28),
         cost_estimate=pl.CostEstimate(
             flops=2 * 3 * 768 * 768 * 768 * count, bytes_accessed=10**7, transcendentals=0
         ),
@@ -220,12 +220,15 @@
     return value[start : start + KIND_ROWS].reshape(OUT_LATS, 2, value.shape[1])
 
 
+WIDE = 1536
 FIELD_ROWS = 192
 
 
 def lon_kernel(count, *refs):
-    terms, factors = refs[:8], refs[8 : 8 + 2 * count]
+    terms, (high, low) = refs[:8], refs[8:10]
     out, z_high, z_low = refs[-3:]
+    wide = out.shape[-1]
+    cols = pl.ds(pl.multiple_of(pl.program_id(0) * wide, wide), wide)
 
     @pl.when(pl.program_id(0) == 0)
     def _():
@@ -240,8 +243,7 @@
         lay_out(read, put, KIND_ROWS)
 
     for at in range(count):
-        high, low = factors[2 * at : 2 * at + 2]
-        value = dot_halves(z_high[...], z_low[...], high[0], low[0])
+        value = dot_halves(z_high[...], z_low[...], high[at, :, cols], low[at, :, cols])
         for field in range(2):
             out[field, at, 0] = by_day(value, field * FIELD_ROWS)
 
@@ -250,10 +252,8 @@
     count = len(operators)
     high_at, low_at = divmod(operators[0], 2)
     in_specs = [pl.BlockSpec((TERM_ROWS, 128), lambda n: (0, 0))] * 8
-    args = list(terms)
-    for which in range(count):
-        in_specs += [pl.BlockSpec((1, 1536, wide), lambda n, which=which: (which, 0, n))] * 2
-        args += [high, low]
+    in_specs += [pl.BlockSpec(memory_space=pltpu.VMEM)] * 2
+    args = [*terms] + [pltpu.with_memory_space_constraint(x, pltpu.VMEM) for x in (high, low)]
     aliases = {}
     if so_far is not None:
         aliases = {len(args): 0}
@@ -269,7 +269,7 @@
         ),
         scratch_shapes=[pltpu.VMEM((2 * FIELD_ROWS, 1536), BF16)] * 2,
         input_output_aliases=aliases,
-        compiler_params=params(),
+        compiler_params=params(18),
         cost_estimate=pl.CostEstimate(
             flops=2 * 3 * 360 * 1536 * 1536 * count, bytes_accessed=2 * 10**7, transcendentals=0
         ),
@@ -277,7 +277,7 @@
     )(*args)
 
 
-ORDER = (1, 6, 4, 3, 2, 5, 7)
+STEPS = (0, 1, 6, 4, 3, 2, 5, 7)
 
 
 def local(probe, residual, lon_embed, lat_embed, day_embed, scales):
@@ -287,7 +287,7 @@
     moved = lax.all_to_all(sent, "lat", split_axis=0, concat_axis=0, tiled=True)
     moved = moved.reshape(16 * DAY_ROWS, 128)
 
-    order = jnp.bitwise_xor(lax.axis_index("lon"), jnp.arange(8))
+    order = jnp.bitwise_xor(lax.axis_index("lon"), jnp.array(STEPS))
     by_block = lat_embed.reshape(8, OUT_LATS, 16)[order]
     lat_rows = jnp.pad(by_block, ((0, 0), (0, 6), (0, 0))).reshape(768, 16)
     lat_cols = jnp.pad(lat_embed.reshape(16, LATS, 16), ((0, 0), (0, SLOTS - LATS), (0, 0)))
@@ -297,15 +297,15 @@
         [by_block[:, :128].reshape(1024, 16), lon_rest.reshape(512, 16)], axis=0
     )
     lat_factors = factor_halves(scales, 1, NA, lat_rows, lat_cols.reshape(16 * SLOTS, 16))
-    lon_factors = factor_halves(scales, 0, NL, lon_rows, lon_embed)
+    lon_cols = jnp.pad(lon_embed, ((0, WIDE - NL), (0, 0)))
+    lon_factors = factor_halves(scales, 0, NL, lon_rows, lon_cols, held=True)
     moved, lat_factors, lon_factors = lax.optimization_barrier((moved, lat_factors, lon_factors))
 
     def exchanged(terms):
-        there = {0: terms[0]}
-        for step in ORDER:
-            pairs = [(i, i ^ step) for i in range(8)]
-            there[step] = lax.ppermute(terms[step], "lon", pairs)
-        return [there[step] for step in range(8)]
+        return [terms[0]] + [
+            lax.ppermute(term, "lon", [(i, i ^ step) for i in range(8)])
+            for term, step in zip(terms[1:], STEPS[1:])
+        ]
 
     (plain,) = lat_products(moved, *lat_factors, ((0, 0),))
     by_day, by_lat = lat_products(moved, *lat_factors, ((1, 0), (0, 1)))

time: 200 us -> 187 us (0.935)
  Pallas kernels: 91.1 us -> 80.7 us
  waiting for transfers between devices: 52.7 us -> 43.5 us
  local copies, waits for them, and re-layouts: 7.07 us -> 12.8 us
    pallas_call x3, Pallas kernels: 37.3 us -> 27.9 us  [lon_products(): pl.pallas_call(functools.partial(lon_kernel, count), grid=(pl.cdiv(NL, wi...]
    unnamed x61 -> x27, local copies, waits for them, and re-layouts: 2.48 us -> 10.6 us
    all_to_all x1, waiting for transfers between devices: 32.1 us -> 27 us  [local(): moved = lax.all_to_all(sent, 'lat', split_axis=0, concat_axis=0, tiled=True)]
    ppermute x21, waiting for transfers between devices: 20.6 us -> 16.5 us  [exchanged(): lax.ppermute(term, 'lon', [(i, i ^ step) for i in range(8)])]
  transfers between devices with their start and end apart: 22 -> 22, of which waited for: 8 -> 6; matrix products, arithmetic and copies ran while one was open for 3% -> 1% of each run, Pallas kernels for 33% -> 32%
where the time goes in v3:
time: 187 us
  Pallas kernels  80.7 us (43%)
  starting transfers between devices  49.4 us (26%)
  waiting for transfers between devices  43.5 us (23%)
  local copies, waits for them, and re-layouts  12.8 us (7%)
    ppermute x21, starting transfers between devices, exchanged(): lax.ppermute(term, 'lon', [(i, i ^ step) for i in range(8)])  43.7 us
    pallas_call x3, Pallas kernels, lon_products(): pl.pallas_call(functools.partial(lon_kernel, count), grid=(pl.cdiv(NL, wi...  27.9 us
    all_to_all x1, waiting for transfers between devices, local(): moved = lax.all_to_all(sent, 'lat', split_axis=0, concat_axis=0, tiled=True)  27 us
    pallas_call x2, Pallas kernels, factor_halves(): pl.pallas_call(functools.partial(factor_kernel, which, count), grid=(nr /...  26.7 us
    pallas_call x2, Pallas kernels, lat_products(): pl.pallas_call(functools.partial(lat_kernel, kinds), grid=(1,), out_shape...  19 us
    ppermute x21, waiting for transfers between devices, exchanged(): lax.ppermute(term, 'lon', [(i, i ^ step) for i in range(8)])  16.5 us
    unnamed x27, local copies, waits for them, and re-layouts  10.6 us
    pallas_call x1, Pallas kernels, day_products(): pl.pallas_call(day_kernel, grid=(pl.cdiv(SLOTS, 2 * PAIRS),), out_shape=j...  7.06 us
  transfers between devices with their start and end apart: 22, of which 6 were waited for; matrix products, arithmetic and copies ran while one was open for 1% of the time, Pallas kernels for 32%

profile of v3, /device:TPU:96, one launch (start us, length us, event | category | flops | bytes accessed | tf_op | source)
XLA Modules:
  0.0 186.8 jit_solution(2808121218054252582)
XLA Ops:
  0.0 7.1 %day_products.1 = f32[16,552,128]{2,1,0:T(8,128)} custom-call(f32[3]{0:T(128)} %scales.5, f32[16,32]{1,0:T(8,128)} %bitcast.28, f32[45,32,180]{2,1,0:T(8,128)} %bitcast.26, f32[45,32,180]{2,1,0:T(8,128)} %bitcast.27), custom_call_target="tpu_custom_call" | custom-call | tf_op jit(solution)/shard_map/day_products/pallas_call | solution.py:109
  7.1 5.7 %all-to-all-start = ((f32[16,552,128]{2,1,0:T(8,128)}), f32[16,552,128]{2,1,0:T(8,128)}, u32[]{:S(2)}, u32[]{:S(2)}) async-start(f32[16,552,128]{2,1,0:T(8,128)} %day_products.1), calls=%async_computation | async-start | bytes 9043968 | tf_op jit(solution)/shard_map/all_to_all | solution.py:287
  12.8 0.1 reshape.28
  12.9 0.1 reshape.30
  13.0 0.1 reshape.32
  13.1 0.3 copy.36
  13.5 0.6 gather_fusion
  14.1 0.6 gather_fusion.1
  14.8 0.1 reshape.31
  14.9 0.2 copy.32.cols
  15.1 0.2 copy.38
  15.3 0.3 copy.37.rows
  15.7 6.0 %factors.2 = (bf16[2,768,736]{2,1,0:T(8,128)(2,1)S(1)}, bf16[2,768,736]{2,1,0:T(8,128)(2,1)S(1)}) custom-call(f32[3]{0:T(128)S(1)} %copy-done.3, f32[768,16]{1,0:T(8,128)S(1)} %bitcast.25, f32[736,16]{1,0:T(8,128)S(1)} %copy.32.cols), custom_call_target="tpu_custom_call" | custom-call | flops 108527616 | bytes 4521984 | tf_op jit(solution)/shard_map/factors/pallas_call | solution.py:136
  21.7 1.5 copy-done.4
  23.2 1.4 copy-done.5
  24.6 20.7 %factors.3 = (bf16[2,1536,1536]{2,1,0:T(8,128)(2,1)S(1)}, bf16[2,1536,1536]{2,1,0:T(8,128)(2,1)S(1)}) custom-call(f32[3]{0:T(128)S(1)} %copy-done.3, f32[1536,16]{1,0:T(8,128)S(1)} %copy.37.rows, f32[1536,16]{1,0:T(8,128)S(1)} %pad.19.cols), custom_call_target="tpu_custom_call" | custom-call | flops 452984832 | bytes 18874368 | tf_op jit(solution)/shard_map/factors/pallas_call | solution.py:136
  45.3 3.6 %copy-done = bf16[2,1536,1536]{2,1,0:T(8,128)(2,1)} copy-done((bf16[2,1536,1536]{2,1,0:T(8,128)(2,1)}, bf16[2,1536,1536]{2,1,0:T(8,128)(2,1)S(1)}, u32[]{:S(2)}) %copy-start) | copy-done | bytes 9437208
  49.0 3.6 %copy-done.1 = bf16[2,1536,1536]{2,1,0:T(8,128)(2,1)} copy-done((bf16[2,1536,1536]{2,1,0:T(8,128)(2,1)}, bf16[2,1536,1536]{2,1,0:T(8,128)(2,1)S(1)}, u32[]{:S(2)}) %copy-start.1) | copy-done | bytes 9437208
  52.6 27.0 %all-to-all-done = f32[16,552,128]{2,1,0:T(8,128)} async-done(((f32[16,552,128]{2,1,0:T(8,128)}), f32[16,552,128]{2,1,0:T(8,128)}, u32[]{:S(2)}, u32[]{:S(2)}) %all-to-all-start) | async-done | bytes 4522016 | tf_op jit(solution)/shard_map/all_to_all | solution.py:287
  79.5 6.3 %lat_products.3 = (f32[544,128]{1,0:T(8,128)S(1)}, f32[544,128]{1,0:T(8,128)S(1)}, f32[544,128]{1,0:T(8,128)S(1)}, f32[544,128]{1,0:T(8,128)S(1)}, f32[544,128]{...) custom-call(f32[8832,128]{1,0:T(8,128)} %bitcast.3.moved, ...), custom_call_target="tpu_custom_call" | custom-call | flops 2717908992 | bytes 10000000 | tf_op jit(solution)/shard_map/lat_products/pallas_call | solution.py:189
  85.8 1.6 collective-permute-start.14
  87.4 5.1 %collective-permute-start.15 = (f32[544,128]{1,0:T(8,128)S(1)}, f32[544,128]{1,0:T(8,128)S(1)}, u32[]{:S(2)}, u32[]{:S(2)}) collective-permute-start(f32[544,128]{1,0:T(8,128)S(1)} %get-tuple-element.65), channel_id=1, source_target_pairs={{0,96},{16,112},{32,64},{48,80},{64,32},{80,48},{96,0},{112,16},{1... | collective-permute-start | bytes 835592 | tf_op jit(solution)/shard_map/ppermute | solution.py:306
  92.4 0.6 collective-permute-start.16
  93.1 0.5 collective-permute-start.17
  93.6 1.8 collective-permute-start.18
  95.4 4.4 %collective-permute-start.19 = (f32[544,128]{1,0:T(8,128)S(1)}, f32[544,128]{1,0:T(8,128)S(1)}, u32[]{:S(2)}, u32[]{:S(2)}) collective-permute-start(f32[544,128]{1,0:T(8,128)S(1)} %get-tuple-element.69), channel_id=1, source_target_pairs={{0,80},{16,64},{32,112},{48,96},{64,16},{80,0},{96,48},{112,32},{1... | collective-permute-start | bytes 835592 | tf_op jit(solution)/shard_map/ppermute | solution.py:306
  99.8 12.8 %lat_products.2 = (f32[544,128]{1,0:T(8,128)S(1)}, f32[544,128]{1,0:T(8,128)S(1)}, f32[544,128]{1,0:T(8,128)S(1)}, f32[544,128]{1,0:T(8,128)S(1)}, f32[544,128]{...) custom-call(f32[8832,128]{1,0:T(8,128)} %bitcast.3.moved, ...), custom_call_target="tpu_custom_call" | custom-call | flops 5435817984 | bytes 10000000 | tf_op jit(solution)/shard_map/lat_products/pallas_call | solution.py:189
  112.6 1.7 collective-permute-start.20
  114.3 0.7 collective-permute-start
  115.0 4.7 %collective-permute-start.1 = (f32[544,128]{1,0:T(8,128)S(1)}, f32[544,128]{1,0:T(8,128)S(1)}, u32[]{:S(2)}, u32[]{:S(2)}) collective-permute-start(f32[544,128]{1,0:T(8,128)S(1)} %get-tuple-element.47), channel_id=1, source_target_pairs={{0,96},{16,112},{32,64},{48,80},{64,32},{80,48},{96,0},{112,16},{1... | collective-permute-start | bytes 835592 | tf_op jit(solution)/shard_map/ppermute | solution.py:306
  119.8 3.1 %collective-permute-start.8 = (f32[544,128]{1,0:T(8,128)S(1)}, f32[544,128]{1,0:T(8,128)S(1)}, u32[]{:S(2)}, u32[]{:S(2)}) collective-permute-start(f32[544,128]{1,0:T(8,128)S(1)} %get-tuple-element.57), channel_id=1, source_target_pairs={{0,96},{16,112},{32,64},{48,80},{64,32},{80,48},{96,0},{112,16},{1... | collective-permute-start | bytes 835592 | tf_op jit(solution)/shard_map/ppermute | solution.py:306
  122.9 2.1 %collective-permute-done.20.refs_7_ = f32[544,128]{1,0:T(8,128)S(1)} collective-permute-done((f32[544,128]{1,0:T(8,128)S(1)}, f32[544,128]{1,0:T(8,128)S(1)}, u32[]{:S(2)}, u32[]{:S(2)}) %collective-permute-start.20) | collective-permute-done | bytes 278560 | tf_op jit(solution)/shard_map/ppermute | solution.py:306
  124.9 1.0 collective-permute-start.9
  126.0 1.5 collective-permute-start.10
  127.4 5.9 %collective-permute-done.1.refs_2_ = f32[544,128]{1,0:T(8,128)S(1)} collective-permute-done((f32[544,128]{1,0:T(8,128)S(1)}, f32[544,128]{1,0:T(8,128)S(1)}, u32[]{:S(2)}, u32[]{:S(2)}) %collective-permute-start.1) | collective-permute-done | bytes 278560 | tf_op jit(solution)/shard_map/ppermute | solution.py:306
  133.3 1.2 collective-permute-start.11
  134.5 1.3 collective-permute-done.7.refs_1_
  135.8 3.1 %collective-permute-start.12 = (f32[544,128]{1,0:T(8,128)S(1)}, f32[544,128]{1,0:T(8,128)S(1)}, u32[]{:S(2)}, u32[]{:S(2)}) collective-permute-start(f32[544,128]{1,0:T(8,128)S(1)} %get-tuple-element.61), channel_id=1, source_target_pairs={{0,80},{16,64},{32,112},{48,96},{64,16},{80,0},{96,48},{112,32},{1... | collective-permute-start | bytes 835592 | tf_op jit(solution)/shard_map/ppermute | solution.py:306
  139.0 6.3 %collective-permute-done.8.refs_2_ = f32[544,128]{1,0:T(8,128)S(1)} collective-permute-done((f32[544,128]{1,0:T(8,128)S(1)}, f32[544,128]{1,0:T(8,128)S(1)}, u32[]{:S(2)}, u32[]{:S(2)}) %collective-permute-start.8) | collective-permute-done | bytes 278560 | tf_op jit(solution)/shard_map/ppermute | solution.py:306
  145.2 1.7 collective-permute-start.13
  147.0 13.1 %lon_products.3.refs_10_ = f32[2,2,2,90,2,1440]{5,4,3,2,1,0:T(2,128)} custom-call(f32[544,128]{1,0:T(8,128)S(1)} %get-tuple-element.63.refs_0_, f32[544,128]{1,0:T(8,128)S(1)} %collective-permute-done.14.refs_1_, f32[544,128]{1,0:T(8,128)S(1)} %collective-permute-done.15.refs_2_, f32[544,128]{1,0:T(8,128)S(1)} %collective-permute-done.16.refs_3_, ...), custom_call_target="tpu_custom_call" | custom-call | flops 10192158720 | bytes 20000000 | tf_op jit(solution)/shard_map/lon_products/pallas_call | solution.py:262
  160.1 3.0 %collective-permute-start.2 = (f32[544,128]{1,0:T(8,128)S(1)}, f32[544,128]{1,0:T(8,128)S(1)}, u32[]{:S(2)}, u32[]{:S(2)}) collective-permute-start(f32[544,128]{1,0:T(8,128)S(1)} %get-tuple-element.48), channel_id=1, source_target_pairs={{0,64},{16,80},{32,96},{48,112},{64,0},{80,16},{96,32},{112,48},{1... | collective-permute-start | bytes 835592 | tf_op jit(solution)/shard_map/ppermute | solution.py:306
  163.1 1.5 collective-permute-start.3
  164.6 2.6 %collective-permute-start.5 = (f32[544,128]{1,0:T(8,128)S(1)}, f32[544,128]{1,0:T(8,128)S(1)}, u32[]{:S(2)}, u32[]{:S(2)}) collective-permute-start(f32[544,128]{1,0:T(8,128)S(1)} %get-tuple-element.51), channel_id=1, source_target_pairs={{0,80},{16,64},{32,112},{48,96},{64,16},{80,0},{96,48},{112,32},{1... | collective-permute-start | bytes 835592 | tf_op jit(solution)/shard_map/ppermute | solution.py:306
  167.2 3.9 %collective-permute-start.6 = (f32[544,128]{1,0:T(8,128)S(1)}, f32[544,128]{1,0:T(8,128)S(1)}, u32[]{:S(2)}, u32[]{:S(2)}) collective-permute-start(f32[544,128]{1,0:T(8,128)S(1)} %get-tuple-element.52), channel_id=1, source_target_pairs={{0,112},{16,96},{32,80},{48,64},{64,48},{80,32},{96,16},{112,0},{1... | collective-permute-start | bytes 835592 | tf_op jit(solution)/shard_map/ppermute | solution.py:306
  171.1 7.4 %lon_products.4.refs_10_ = f32[2,2,2,90,2,1440]{5,4,3,2,1,0:T(2,128)} custom-call(f32[544,128]{1,0:T(8,128)S(1)} %get-tuple-element.55.refs_0_, f32[544,128]{1,0:T(8,128)S(1)} %collective-permute-done.7.refs_1_, f32[544,128]{1,0:T(8,128)S(1)} %collective-permute-done.8.refs_2_, ...), custom_call_target="tpu_custom_call", output_to_operand_aliasing={{}: (10, {})} | custom-call | flops 5096079360 | bytes 20000000 | tf_op jit(solution)/shard_map/lon_products/pallas_call | solution.py:262
  178.5 0.9 collective-permute-done.2.refs_3_
  179.4 7.4 %lon_products.5 = f32[2,2,2,90,2,1440]{5,4,3,2,1,0:T(2,128)} custom-call(f32[544,128]{1,0:T(8,128)S(1)} %get-tuple-element.45.refs_0_, f32[544,128]{1,0:T(8,128)S(1)} %collective-permute-done.refs_1_, f32[544,128]{1,0:T(8,128)S(1)} %collective-permute-done.1.refs_2_, f32[544,128]{1,0:T(8,128)S(1)} %collective-permute-done.2.refs_3_, ...), custom_call_target="tpu_custom_call", output_to_operand_aliasing={{}: (10, {})} | custom-call | flops 5096079360 | bytes 20000000 | tf_op jit(solution)/shard_map/lon_products/pallas_call | solution.py:262
  (52 shorter events, 0.4 us)
Async XLA Ops:
  7.1 5.7 %copy-start.7 = (f32[720,16]{0,1:T(8,128)S(1)}, f32[720,16]{0,1:T(8,128)}, u32[]{:S(2)}) copy-start(f32[720,16]{0,1:T(8,128)} %param.10) | copy-start | bytes 138244
  7.1 5.9 %copy-start.6 = (f32[1440,16]{0,1:T(8,128)S(1)}, f32[1440,16]{0,1:T(8,128)}, u32[]{:S(2)}) copy-start(f32[1440,16]{0,1:T(8,128)} %param.9) | copy-start | bytes 276484
  7.1 6.4 %copy-start.8 = (s32[8]{0:T(128)S(1)}, s32[8]{0:T(128)}, u32[]{:S(2)}) copy-start(s32[8]{0:T(128)} %constant.15.clone) | copy-start | bytes 100
  7.1 72.4 %all-to-all-start = ((f32[16,552,128]{2,1,0:T(8,128)}), f32[16,552,128]{2,1,0:T(8,128)}, u32[]{:S(2)}, u32[]{:S(2)}) async-start(f32[16,552,128]{2,1,0:T(8,128)} %day_products.1), calls=%async_computation | async-start | bytes 9043968 | tf_op jit(solution)/shard_map/all_to_all | solution.py:287
  13.0 2.7 %copy-start.3 = (f32[3]{0:T(128)S(1)}, f32[3]{0:T(128)}, u32[]{:S(2)}) copy-start(f32[3]{0:T(128)} %scales.5) | copy-start | bytes 40
  21.7 1.5 copy-start.4
  23.2 1.4 copy-start.5
  45.3 3.6 %copy-start = (bf16[2,1536,1536]{2,1,0:T(8,128)(2,1)}, bf16[2,1536,1536]{2,1,0:T(8,128)(2,1)S(1)}, u32[]{:S(2)}) copy-start(bf16[2,1536,1536]{2,1,0:T(8,128)(2,1)S(1)} %get-tuple-element.53.refs_8_) | copy-start | bytes 28311556
  48.9 3.6 %copy-start.1 = (bf16[2,1536,1536]{2,1,0:T(8,128)(2,1)}, bf16[2,1536,1536]{2,1,0:T(8,128)(2,1)S(1)}, u32[]{:S(2)}) copy-start(bf16[2,1536,1536]{2,1,0:T(8,128)(2,1)S(1)} %get-tuple-element.54.refs_9_) | copy-start | bytes 28311556
  85.8 9.6 %collective-permute-start.14 = (f32[544,128]{1,0:T(8,128)S(1)}, f32[544,128]{1,0:T(8,128)S(1)}, u32[]{:S(2)}, u32[]{:S(2)}) collective-permute-start(f32[544,128]{1,0:T(8,128)S(1)} %get-tuple-element.64), channel_id=1, source_target_pairs={{0,16},{16,0},{32,48},{48,32},{64,80},{80,64},{96,112},{112,96},{1... | collective-permute-start | bytes 835592 | tf_op jit(solution)/shard_map/ppermute | solution.py:306
  87.4 25.2 %collective-permute-start.15 = (f32[544,128]{1,0:T(8,128)S(1)}, f32[544,128]{1,0:T(8,128)S(1)}, u32[]{:S(2)}, u32[]{:S(2)}) collective-permute-start(f32[544,128]{1,0:T(8,128)S(1)} %get-tuple-element.65), channel_id=1, source_target_pairs={{0,96},{16,112},{32,64},{48,80},{64,32},{80,48},{96,0},{112,16},{1... | collective-permute-start | bytes 835592 | tf_op jit(solution)/shard_map/ppermute | solution.py:306
  92.4 21.8 %collective-permute-start.16 = (f32[544,128]{1,0:T(8,128)S(1)}, f32[544,128]{1,0:T(8,128)S(1)}, u32[]{:S(2)}, u32[]{:S(2)}) collective-permute-start(f32[544,128]{1,0:T(8,128)S(1)} %get-tuple-element.66), channel_id=1, source_target_pairs={{0,64},{16,80},{32,96},{48,112},{64,0},{80,16},{96,32},{112,48},{1... | collective-permute-start | bytes 835592 | tf_op jit(solution)/shard_map/ppermute | solution.py:306
  93.1 21.9 %collective-permute-start.17 = (f32[544,128]{1,0:T(8,128)S(1)}, f32[544,128]{1,0:T(8,128)S(1)}, u32[]{:S(2)}, u32[]{:S(2)}) collective-permute-start(f32[544,128]{1,0:T(8,128)S(1)} %get-tuple-element.67), channel_id=1, source_target_pairs={{0,48},{16,32},{32,16},{48,0},{64,112},{80,96},{96,80},{112,64},{1... | collective-permute-start | bytes 835592 | tf_op jit(solution)/shard_map/ppermute | solution.py:306
  93.6 26.2 %collective-permute-start.18 = (f32[544,128]{1,0:T(8,128)S(1)}, f32[544,128]{1,0:T(8,128)S(1)}, u32[]{:S(2)}, u32[]{:S(2)}) collective-permute-start(f32[544,128]{1,0:T(8,128)S(1)} %get-tuple-element.68), channel_id=1, source_target_pairs={{0,32},{16,48},{32,0},{48,16},{64,96},{80,112},{96,64},{112,80},{1... | collective-permute-start | bytes 835592 | tf_op jit(solution)/shard_map/ppermute | solution.py:306
  95.4 51.6 %slice-start = ((s8[9437184]{0:T(1024)(128)(4,1)}), s8[4194304]{0:T(1024)(128)(4,1)S(1)}, s32[]{:S(2)}) async-start(s8[9437184]{0:T(1024)(128)(4,1)} %bitcast.23), calls=%async_computation.1 | async-start | bytes 8388608
  95.4 51.6 %slice-start.1 = ((s8[9437184]{0:T(1024)(128)(4,1)}), s8[4194304]{0:T(1024)(128)(4,1)S(1)}, s32[]{:S(2)}) async-start(s8[9437184]{0:T(1024)(128)(4,1)} %bitcast.23), calls=%async_computation.2 | async-start | bytes 8388608
  95.4 51.6 %slice-start.2 = ((s8[9437184]{0:T(1024)(128)(4,1)}), s8[1048576]{0:T(1024)(128)(4,1)S(1)}, s32[]{:S(2)}) async-start(s8[9437184]{0:T(1024)(128)(4,1)} %bitcast.23), calls=%async_computation.3 | async-start | bytes 2097152
  95.4 51.6 %copy-start.2 = (bf16[2,1536,1536]{2,1,0:T(8,128)(2,1)S(1)}, bf16[2,1536,1536]{2,1,0:T(8,128)(2,1)}, u32[]{:S(2)}) copy-start(bf16[2,1536,1536]{2,1,0:T(8,128)(2,1)} %copy-done.1) | copy-start | bytes 28311556
  95.4 24.4 %collective-permute-start.19 = (f32[544,128]{1,0:T(8,128)S(1)}, f32[544,128]{1,0:T(8,128)S(1)}, u32[]{:S(2)}, u32[]{:S(2)}) collective-permute-start(f32[544,128]{1,0:T(8,128)S(1)} %get-tuple-element.69), channel_id=1, source_target_pairs={{0,80},{16,64},{32,112},{48,96},{64,16},{80,0},{96,48},{112,32},{1... | collective-permute-start | bytes 835592 | tf_op jit(solution)/shard_map/ppermute | solution.py:306
  112.6 12.4 %collective-permute-start.20 = (f32[544,128]{1,0:T(8,128)S(1)}, f32[544,128]{1,0:T(8,128)S(1)}, u32[]{:S(2)}, u32[]{:S(2)}) collective-permute-start(f32[544,128]{1,0:T(8,128)S(1)} %get-tuple-element.70), channel_id=1, source_target_pairs={{0,112},{16,96},{32,80},{48,64},{64,48},{80,32},{96,16},{112,0},{1... | collective-permute-start | bytes 835592 | tf_op jit(solution)/shard_map/ppermute | solution.py:306
  114.3 11.7 %collective-permute-start = (f32[544,128]{1,0:T(8,128)S(1)}, f32[544,128]{1,0:T(8,128)S(1)}, u32[]{:S(2)}, u32[]{:S(2)}) collective-permute-start(f32[544,128]{1,0:T(8,128)S(1)} %get-tuple-element.46), channel_id=1, source_target_pairs={{0,16},{16,0},{32,48},{48,32},{64,80},{80,64},{96,112},{112,96},{1... | collective-permute-start | bytes 835592 | tf_op jit(solution)/shard_map/ppermute | solution.py:306
  115.0 18.3 %collective-permute-start.1 = (f32[544,128]{1,0:T(8,128)S(1)}, f32[544,128]{1,0:T(8,128)S(1)}, u32[]{:S(2)}, u32[]{:S(2)}) collective-permute-start(f32[544,128]{1,0:T(8,128)S(1)} %get-tuple-element.47), channel_id=1, source_target_pairs={{0,96},{16,112},{32,64},{48,80},{64,32},{80,48},{96,0},{112,16},{1... | collective-permute-start | bytes 835592 | tf_op jit(solution)/shard_map/ppermute | solution.py:306
  119.8 16.1 %collective-permute-start.7 = (f32[544,128]{1,0:T(8,128)S(1)}, f32[544,128]{1,0:T(8,128)S(1)}, u32[]{:S(2)}, u32[]{:S(2)}) collective-permute-start(f32[544,128]{1,0:T(8,128)S(1)} %get-tuple-element.56), channel_id=1, source_target_pairs={{0,16},{16,0},{32,48},{48,32},{64,80},{80,64},{96,112},{112,96},{1... | collective-permute-start | bytes 835592 | tf_op jit(solution)/shard_map/ppermute | solution.py:306
  119.8 25.5 %collective-permute-start.8 = (f32[544,128]{1,0:T(8,128)S(1)}, f32[544,128]{1,0:T(8,128)S(1)}, u32[]{:S(2)}, u32[]{:S(2)}) collective-permute-start(f32[544,128]{1,0:T(8,128)S(1)} %get-tuple-element.57), channel_id=1, source_target_pairs={{0,96},{16,112},{32,64},{48,80},{64,32},{80,48},{96,0},{112,16},{1... | collective-permute-start | bytes 835592 | tf_op jit(solution)/shard_map/ppermute | solution.py:306
  124.9 35.1 %collective-permute-start.9 = (f32[544,128]{1,0:T(8,128)S(1)}, f32[544,128]{1,0:T(8,128)S(1)}, u32[]{:S(2)}, u32[]{:S(2)}) collective-permute-start(f32[544,128]{1,0:T(8,128)S(1)} %get-tuple-element.58), channel_id=1, source_target_pairs={{0,64},{16,80},{32,96},{48,112},{64,0},{80,16},{96,32},{112,48},{1... | collective-permute-start | bytes 835592 | tf_op jit(solution)/shard_map/ppermute | solution.py:306
  126.0 37.1 %collective-permute-start.10 = (f32[544,128]{1,0:T(8,128)S(1)}, f32[544,128]{1,0:T(8,128)S(1)}, u32[]{:S(2)}, u32[]{:S(2)}) collective-permute-start(f32[544,128]{1,0:T(8,128)S(1)} %get-tuple-element.59), channel_id=1, source_target_pairs={{0,48},{16,32},{32,16},{48,0},{64,112},{80,96},{96,80},{112,64},{1... | collective-permute-start | bytes 835592 | tf_op jit(solution)/shard_map/ppermute | solution.py:306
  133.3 31.3 %collective-permute-start.11 = (f32[544,128]{1,0:T(8,128)S(1)}, f32[544,128]{1,0:T(8,128)S(1)}, u32[]{:S(2)}, u32[]{:S(2)}) collective-permute-start(f32[544,128]{1,0:T(8,128)S(1)} %get-tuple-element.60), channel_id=1, source_target_pairs={{0,32},{16,48},{32,0},{48,16},{64,96},{80,112},{96,64},{112,80},{1... | collective-permute-start | bytes 835592 | tf_op jit(solution)/shard_map/ppermute | solution.py:306
  135.8 28.8 %collective-permute-start.12 = (f32[544,128]{1,0:T(8,128)S(1)}, f32[544,128]{1,0:T(8,128)S(1)}, u32[]{:S(2)}, u32[]{:S(2)}) collective-permute-start(f32[544,128]{1,0:T(8,128)S(1)} %get-tuple-element.61), channel_id=1, source_target_pairs={{0,80},{16,64},{32,112},{48,96},{64,16},{80,0},{96,48},{112,32},{1... | collective-permute-start | bytes 835592 | tf_op jit(solution)/shard_map/ppermute | solution.py:306
  145.2 21.9 %collective-permute-start.13 = (f32[544,128]{1,0:T(8,128)S(1)}, f32[544,128]{1,0:T(8,128)S(1)}, u32[]{:S(2)}, u32[]{:S(2)}) collective-permute-start(f32[544,128]{1,0:T(8,128)S(1)} %get-tuple-element.62), channel_id=1, source_target_pairs={{0,112},{16,96},{32,80},{48,64},{64,48},{80,32},{96,16},{112,0},{1... | collective-permute-start | bytes 835592 | tf_op jit(solution)/shard_map/ppermute | solution.py:306
  160.1 19.3 %collective-permute-start.2 = (f32[544,128]{1,0:T(8,128)S(1)}, f32[544,128]{1,0:T(8,128)S(1)}, u32[]{:S(2)}, u32[]{:S(2)}) collective-permute-start(f32[544,128]{1,0:T(8,128)S(1)} %get-tuple-element.48), channel_id=1, source_target_pairs={{0,64},{16,80},{32,96},{48,112},{64,0},{80,16},{96,32},{112,48},{1... | collective-permute-start | bytes 835592 | tf_op jit(solution)/shard_map/ppermute | solution.py:306
  163.1 16.3 %collective-permute-start.3 = (f32[544,128]{1,0:T(8,128)S(1)}, f32[544,128]{1,0:T(8,128)S(1)}, u32[]{:S(2)}, u32[]{:S(2)}) collective-permute-start(f32[544,128]{1,0:T(8,128)S(1)} %get-tuple-element.49), channel_id=1, source_target_pairs={{0,48},{16,32},{32,16},{48,0},{64,112},{80,96},{96,80},{112,64},{1... | collective-permute-start | bytes 835592 | tf_op jit(solution)/shard_map/ppermute | solution.py:306
  164.6 14.8 %collective-permute-start.4 = (f32[544,128]{1,0:T(8,128)S(1)}, f32[544,128]{1,0:T(8,128)S(1)}, u32[]{:S(2)}, u32[]{:S(2)}) collective-permute-start(f32[544,128]{1,0:T(8,128)S(1)} %get-tuple-element.50), channel_id=1, source_target_pairs={{0,32},{16,48},{32,0},{48,16},{64,96},{80,112},{96,64},{112,80},{1... | collective-permute-start | bytes 835592 | tf_op jit(solution)/shard_map/ppermute | solution.py:306
  164.6 14.8 %collective-permute-start.5 = (f32[544,128]{1,0:T(8,128)S(1)}, f32[544,128]{1,0:T(8,128)S(1)}, u32[]{:S(2)}, u32[]{:S(2)}) collective-permute-start(f32[544,128]{1,0:T(8,128)S(1)} %get-tuple-element.51), channel_id=1, source_target_pairs={{0,80},{16,64},{32,112},{48,96},{64,16},{80,0},{96,48},{112,32},{1... | collective-permute-start | bytes 835592 | tf_op jit(solution)/shard_map/ppermute | solution.py:306
  167.2 12.2 %collective-permute-start.6 = (f32[544,128]{1,0:T(8,128)S(1)}, f32[544,128]{1,0:T(8,128)S(1)}, u32[]{:S(2)}, u32[]{:S(2)}) collective-permute-start(f32[544,128]{1,0:T(8,128)S(1)} %get-tuple-element.52), channel_id=1, source_target_pairs={{0,112},{16,96},{32,80},{48,64},{64,48},{80,32},{96,16},{112,0},{1... | collective-permute-start | bytes 835592 | tf_op jit(solution)/shard_map/ppermute | solution.py:306

commit v4 on v3

--- a/solution.py
+++ b/solution.py
@@ -58,7 +58,7 @@
     return kern, deriv
 
 
-PAIRS = 4
+PAIRS = 12
 
 
 def day_kernel(scales, embed, probe, residual, out, weights):
@@ -308,7 +308,8 @@
         ]
 
     (plain,) = lat_products(moved, *lat_factors, ((0, 0),))
-    by_day, by_lat = lat_products(moved, *lat_factors, ((1, 0), (0, 1)))
+    (by_day,) = lat_products(moved, *lat_factors, ((1, 0),))
+    (by_lat,) = lat_products(moved, *lat_factors, ((0, 1),))
     result = lon_products(exchanged(plain), *lon_factors, (0, 2))
     result = lon_products(exchanged(by_day), *lon_factors, (1,), result)
     result = lon_products(exchanged(by_lat), *lon_factors, (3,), result)

time: 187 us -> 185 us (0.989)
  waiting for transfers between devices: 43.5 us -> 46.5 us
  starting transfers between devices: 49.4 us -> 46.7 us
  Pallas kernels: 80.7 us -> 78.5 us
    ppermute x21, waiting for transfers between devices: 16.5 us -> 19.5 us  [exchanged(): lax.ppermute(term, 'lon', [(i, i ^ step) for i in range(8)])]
    ppermute x21, starting transfers between devices: 43.7 us -> 41 us  [exchanged(): lax.ppermute(term, 'lon', [(i, i ^ step) for i in range(8)])]
    pallas_call x1, Pallas kernels: 7.06 us -> 4.93 us  [day_products(): pl.pallas_call(day_kernel, grid=(pl.cdiv(SLOTS, 2 * PAIRS),), out_shape=j...]
    pallas_call x2 -> x3, Pallas kernels: 19 us -> 19 us  [lat_products(): pl.pallas_call(functools.partial(lat_kernel, kinds), grid=(1,), out_shape...]
  transfers between devices with their start and end apart: 22 -> 22, of which waited for: 6 -> 9; matrix products, arithmetic and copies ran while one was open for 1% -> 1% of each run, Pallas kernels for 32% -> 32%
where the time goes in v4:
time: 185 us
  Pallas kernels  78.5 us (42%)
  starting transfers between devices  46.7 us (25%)
  waiting for transfers between devices  46.5 us (25%)
  local copies, waits for them, and re-layouts  12.9 us (7%)
    ppermute x21, starting transfers between devices, exchanged(): lax.ppermute(term, 'lon', [(i, i ^ step) for i in range(8)])  41 us
    pallas_call x3, Pallas kernels, lon_products(): pl.pallas_call(functools.partial(lon_kernel, count), grid=(pl.cdiv(NL, wi...  27.9 us
    all_to_all x1, waiting for transfers between devices, local(): moved = lax.all_to_all(sent, 'lat', split_axis=0, concat_axis=0, tiled=True)  26.9 us
    pallas_call x2, Pallas kernels, factor_halves(): pl.pallas_call(functools.partial(factor_kernel, which, count), grid=(nr /...  26.7 us
    ppermute x21, waiting for transfers between devices, exchanged(): lax.ppermute(term, 'lon', [(i, i ^ step) for i in range(8)])  19.5 us
    pallas_call x3, Pallas kernels, lat_products(): pl.pallas_call(functools.partial(lat_kernel, kinds), grid=(1,), out_shape...  19 us
    unnamed x27, local copies, waits for them, and re-layouts  10.6 us
    all_to_all x1, starting transfers between devices, local(): moved = lax.all_to_all(sent, 'lat', split_axis=0, concat_axis=0, tiled=True)  5.68 us
  transfers between devices with their start and end apart: 22, of which 9 were waited for; matrix products, arithmetic and copies ran while one was open for 1% of the time, Pallas kernels for 32%

profile of v4, /device:TPU:96, one launch (start us, length us, event | category | flops | bytes accessed | tf_op | source)
XLA Modules:
  0.0 184.8 jit_solution(17571104036688624577)
XLA Ops:
  0.0 4.9 %day_products.1 = f32[16,552,128]{2,1,0:T(8,128)} custom-call(f32[3]{0:T(128)} %scales.5, f32[16,32]{1,0:T(8,128)} %bitcast.28, f32[45,32,180]{2,1,0:T(8,128)} %bitcast.26, f32[45,32,180]{2,1,0:T(8,128)} %bitcast.27), custom_call_target="tpu_custom_call" | custom-call | tf_op jit(solution)/shard_map/day_products/pallas_call | solution.py:109
  4.9 5.7 %all-to-all-start = ((f32[16,552,128]{2,1,0:T(8,128)}), f32[16,552,128]{2,1,0:T(8,128)}, u32[]{:S(2)}, u32[]{:S(2)}) async-start(f32[16,552,128]{2,1,0:T(8,128)} %day_products.1), calls=%async_computation | async-start | bytes 9043968 | tf_op jit(solution)/shard_map/all_to_all | solution.py:287
  10.9 0.1 reshape.32
  11.0 0.3 copy.36
  11.4 0.6 gather_fusion
  11.9 0.6 gather_fusion.1
  12.8 0.2 copy.32.cols
  12.9 0.2 copy.38
  13.2 0.3 copy.37.rows
  13.6 6.0 %factors.2 = (bf16[2,768,736]{2,1,0:T(8,128)(2,1)S(1)}, bf16[2,768,736]{2,1,0:T(8,128)(2,1)S(1)}) custom-call(f32[3]{0:T(128)S(1)} %copy-done.3, f32[768,16]{1,0:T(8,128)S(1)} %bitcast.25, f32[736,16]{1,0:T(8,128)S(1)} %copy.32.cols), custom_call_target="tpu_custom_call" | custom-call | flops 108527616 | bytes 4521984 | tf_op jit(solution)/shard_map/factors/pallas_call | solution.py:136
  19.6 1.5 copy-done.4
  21.1 1.4 copy-done.5
  22.5 20.7 %factors.3 = (bf16[2,1536,1536]{2,1,0:T(8,128)(2,1)S(1)}, bf16[2,1536,1536]{2,1,0:T(8,128)(2,1)S(1)}) custom-call(f32[3]{0:T(128)S(1)} %copy-done.3, f32[1536,16]{1,0:T(8,128)S(1)} %copy.37.rows, f32[1536,16]{1,0:T(8,128)S(1)} %pad.19.cols), custom_call_target="tpu_custom_call" | custom-call | flops 452984832 | bytes 18874368 | tf_op jit(solution)/shard_map/factors/pallas_call | solution.py:136
  43.2 3.6 %copy-done = bf16[2,1536,1536]{2,1,0:T(8,128)(2,1)} copy-done((bf16[2,1536,1536]{2,1,0:T(8,128)(2,1)}, bf16[2,1536,1536]{2,1,0:T(8,128)(2,1)S(1)}, u32[]{:S(2)}) %copy-start) | copy-done | bytes 9437208
  46.8 3.6 %copy-done.1 = bf16[2,1536,1536]{2,1,0:T(8,128)(2,1)} copy-done((bf16[2,1536,1536]{2,1,0:T(8,128)(2,1)}, bf16[2,1536,1536]{2,1,0:T(8,128)(2,1)S(1)}, u32[]{:S(2)}) %copy-start.1) | copy-done | bytes 9437208
  50.4 26.9 %all-to-all-done = f32[16,552,128]{2,1,0:T(8,128)} async-done(((f32[16,552,128]{2,1,0:T(8,128)}), f32[16,552,128]{2,1,0:T(8,128)}, u32[]{:S(2)}, u32[]{:S(2)}) %all-to-all-start) | async-done | bytes 4522016 | tf_op jit(solution)/shard_map/all_to_all | solution.py:287
  77.4 6.3 %lat_products.5 = (f32[544,128]{1,0:T(8,128)S(1)}, f32[544,128]{1,0:T(8,128)S(1)}, f32[544,128]{1,0:T(8,128)S(1)}, f32[544,128]{1,0:T(8,128)S(1)}, f32[544,128]{...) custom-call(f32[8832,128]{1,0:T(8,128)} %bitcast.3.moved, ...), custom_call_target="tpu_custom_call" | custom-call | flops 2717908992 | bytes 10000000 | tf_op jit(solution)/shard_map/lat_products/pallas_call | solution.py:189
  83.7 1.6 collective-permute-start.14
  85.2 5.1 %collective-permute-start.15 = (f32[544,128]{1,0:T(8,128)S(1)}, f32[544,128]{1,0:T(8,128)S(1)}, u32[]{:S(2)}, u32[]{:S(2)}) collective-permute-start(f32[544,128]{1,0:T(8,128)S(1)} %get-tuple-element.65), channel_id=1, source_target_pairs={{0,96},{16,112},{32,64},{48,80},{64,32},{80,48},{96,0},{112,16},{1... | collective-permute-start | bytes 835592 | tf_op jit(solution)/shard_map/ppermute | solution.py:306
  90.3 0.6 collective-permute-start.16
  90.9 0.5 collective-permute-start.17
  91.4 1.8 collective-permute-start.18
  93.2 4.1 %collective-permute-start.19 = (f32[544,128]{1,0:T(8,128)S(1)}, f32[544,128]{1,0:T(8,128)S(1)}, u32[]{:S(2)}, u32[]{:S(2)}) collective-permute-start(f32[544,128]{1,0:T(8,128)S(1)} %get-tuple-element.69), channel_id=1, source_target_pairs={{0,80},{16,64},{32,112},{48,96},{64,16},{80,0},{96,48},{112,32},{1... | collective-permute-start | bytes 835592 | tf_op jit(solution)/shard_map/ppermute | solution.py:306
  97.4 6.4 %lat_products.4 = (f32[544,128]{1,0:T(8,128)S(1)}, f32[544,128]{1,0:T(8,128)S(1)}, f32[544,128]{1,0:T(8,128)S(1)}, f32[544,128]{1,0:T(8,128)S(1)}, f32[544,128]{...) custom-call(f32[8832,128]{1,0:T(8,128)} %bitcast.3.moved, ...), custom_call_target="tpu_custom_call" | custom-call | flops 2717908992 | bytes 10000000 | tf_op jit(solution)/shard_map/lat_products/pallas_call | solution.py:189
  103.8 1.9 %collective-permute-start.20 = (f32[544,128]{1,0:T(8,128)S(1)}, f32[544,128]{1,0:T(8,128)S(1)}, u32[]{:S(2)}, u32[]{:S(2)}) collective-permute-start(f32[544,128]{1,0:T(8,128)S(1)} %get-tuple-element.70), channel_id=1, source_target_pairs={{0,112},{16,96},{32,80},{48,64},{64,48},{80,32},{96,16},{112,0},{1... | collective-permute-start | bytes 835592 | tf_op jit(solution)/shard_map/ppermute | solution.py:306
  105.7 0.3 collective-permute-done.16.refs_3_
  106.1 0.3 collective-permute-start.7
  106.4 6.5 %collective-permute-done.17.refs_4_ = f32[544,128]{1,0:T(8,128)S(1)} collective-permute-done((f32[544,128]{1,0:T(8,128)S(1)}, f32[544,128]{1,0:T(8,128)S(1)}, u32[]{:S(2)}, u32[]{:S(2)}) %collective-permute-start.17) | collective-permute-done | bytes 278560 | tf_op jit(solution)/shard_map/ppermute | solution.py:306
  112.9 2.6 %collective-permute-start.8 = (f32[544,128]{1,0:T(8,128)S(1)}, f32[544,128]{1,0:T(8,128)S(1)}, u32[]{:S(2)}, u32[]{:S(2)}) collective-permute-start(f32[544,128]{1,0:T(8,128)S(1)} %get-tuple-element.57), channel_id=1, source_target_pairs={{0,96},{16,112},{32,64},{48,80},{64,32},{80,48},{96,0},{112,16},{1... | collective-permute-start | bytes 835592 | tf_op jit(solution)/shard_map/ppermute | solution.py:306
  115.5 0.6 collective-permute-start.9
  116.1 2.1 %collective-permute-start.10 = (f32[544,128]{1,0:T(8,128)S(1)}, f32[544,128]{1,0:T(8,128)S(1)}, u32[]{:S(2)}, u32[]{:S(2)}) collective-permute-start(f32[544,128]{1,0:T(8,128)S(1)} %get-tuple-element.59), channel_id=1, source_target_pairs={{0,48},{16,32},{32,16},{48,0},{64,112},{80,96},{96,80},{112,64},{1... | collective-permute-start | bytes 835592 | tf_op jit(solution)/shard_map/ppermute | solution.py:306
  118.2 6.3 %lat_products.3 = (f32[544,128]{1,0:T(8,128)S(1)}, f32[544,128]{1,0:T(8,128)S(1)}, f32[544,128]{1,0:T(8,128)S(1)}, f32[544,128]{1,0:T(8,128)S(1)}, f32[544,128]{...) custom-call(f32[8832,128]{1,0:T(8,128)} %bitcast.3.moved, ...), custom_call_target="tpu_custom_call" | custom-call | flops 2717908992 | bytes 10000000 | tf_op jit(solution)/shard_map/lat_products/pallas_call | solution.py:189
  124.5 2.7 %collective-permute-done.20.refs_7_ = f32[544,128]{1,0:T(8,128)S(1)} collective-permute-done((f32[544,128]{1,0:T(8,128)S(1)}, f32[544,128]{1,0:T(8,128)S(1)}, u32[]{:S(2)}, u32[]{:S(2)}) %collective-permute-start.20) | collective-permute-done | bytes 278560 | tf_op jit(solution)/shard_map/ppermute | solution.py:306
  127.2 1.7 collective-permute-start.12
  128.9 4.8 %collective-permute-start.13 = (f32[544,128]{1,0:T(8,128)S(1)}, f32[544,128]{1,0:T(8,128)S(1)}, u32[]{:S(2)}, u32[]{:S(2)}) collective-permute-start(f32[544,128]{1,0:T(8,128)S(1)} %get-tuple-element.62), channel_id=1, source_target_pairs={{0,112},{16,96},{32,80},{48,64},{64,48},{80,32},{96,16},{112,0},{1... | collective-permute-start | bytes 835592 | tf_op jit(solution)/shard_map/ppermute | solution.py:306
  133.7 1.6 collective-permute-done.9.refs_3_
  135.3 1.5 collective-permute-done.10.refs_4_
  136.8 3.5 %collective-permute-start.1 = (f32[544,128]{1,0:T(8,128)S(1)}, f32[544,128]{1,0:T(8,128)S(1)}, u32[]{:S(2)}, u32[]{:S(2)}) collective-permute-start(f32[544,128]{1,0:T(8,128)S(1)} %get-tuple-element.47), channel_id=1, source_target_pairs={{0,96},{16,112},{32,64},{48,80},{64,32},{80,48},{96,0},{112,16},{1... | collective-permute-start | bytes 835592 | tf_op jit(solution)/shard_map/ppermute | solution.py:306
  140.3 13.1 %lon_products.3.refs_10_ = f32[2,2,2,90,2,1440]{5,4,3,2,1,0:T(2,128)} custom-call(f32[544,128]{1,0:T(8,128)S(1)} %get-tuple-element.63.refs_0_, f32[544,128]{1,0:T(8,128)S(1)} %collective-permute-done.14.refs_1_, f32[544,128]{1,0:T(8,128)S(1)} %collective-permute-done.15.refs_2_, f32[544,128]{1,0:T(8,128)S(1)} %collective-permute-done.16.refs_3_, ...), custom_call_target="tpu_custom_call" | custom-call | flops 10192158720 | bytes 20000000 | tf_op jit(solution)/shard_map/lon_products/pallas_call | solution.py:262
  153.5 0.7 collective-permute-start.2
  154.1 2.6 %collective-permute-start.3 = (f32[544,128]{1,0:T(8,128)S(1)}, f32[544,128]{1,0:T(8,128)S(1)}, u32[]{:S(2)}, u32[]{:S(2)}) collective-permute-start(f32[544,128]{1,0:T(8,128)S(1)} %get-tuple-element.49), channel_id=1, source_target_pairs={{0,48},{16,32},{32,16},{48,0},{64,112},{80,96},{96,80},{112,64},{1... | collective-permute-start | bytes 835592 | tf_op jit(solution)/shard_map/ppermute | solution.py:306
  156.8 3.8 %collective-permute-start.5 = (f32[544,128]{1,0:T(8,128)S(1)}, f32[544,128]{1,0:T(8,128)S(1)}, u32[]{:S(2)}, u32[]{:S(2)}) collective-permute-start(f32[544,128]{1,0:T(8,128)S(1)} %get-tuple-element.51), channel_id=1, source_target_pairs={{0,80},{16,64},{32,112},{48,96},{64,16},{80,0},{96,48},{112,32},{1... | collective-permute-start | bytes 835592 | tf_op jit(solution)/shard_map/ppermute | solution.py:306
  160.5 2.7 %collective-permute-start.6 = (f32[544,128]{1,0:T(8,128)S(1)}, f32[544,128]{1,0:T(8,128)S(1)}, u32[]{:S(2)}, u32[]{:S(2)}) collective-permute-start(f32[544,128]{1,0:T(8,128)S(1)} %get-tuple-element.52), channel_id=1, source_target_pairs={{0,112},{16,96},{32,80},{48,64},{64,48},{80,32},{96,16},{112,0},{1... | collective-permute-start | bytes 835592 | tf_op jit(solution)/shard_map/ppermute | solution.py:306
  163.3 7.4 %lon_products.4.refs_10_ = f32[2,2,2,90,2,1440]{5,4,3,2,1,0:T(2,128)} custom-call(f32[544,128]{1,0:T(8,128)S(1)} %get-tuple-element.55.refs_0_, f32[544,128]{1,0:T(8,128)S(1)} %collective-permute-done.7.refs_1_, f32[544,128]{1,0:T(8,128)S(1)} %collective-permute-done.8.refs_2_, ...), custom_call_target="tpu_custom_call", output_to_operand_aliasing={{}: (10, {})} | custom-call | flops 5096079360 | bytes 20000000 | tf_op jit(solution)/shard_map/lon_products/pallas_call | solution.py:262
  170.7 0.2 collective-permute-done.3.refs_4_
  170.8 1.4 collective-permute-done.5.refs_6_
  172.2 5.2 %collective-permute-done.6.refs_7_ = f32[544,128]{1,0:T(8,128)S(1)} collective-permute-done((f32[544,128]{1,0:T(8,128)S(1)}, f32[544,128]{1,0:T(8,128)S(1)}, u32[]{:S(2)}, u32[]{:S(2)}) %collective-permute-start.6) | collective-permute-done | bytes 278560 | tf_op jit(solution)/shard_map/ppermute | solution.py:306
  177.4 7.4 %lon_products.5 = f32[2,2,2,90,2,1440]{5,4,3,2,1,0:T(2,128)} custom-call(f32[544,128]{1,0:T(8,128)S(1)} %get-tuple-element.45.refs_0_, f32[544,128]{1,0:T(8,128)S(1)} %collective-permute-done.refs_1_, f32[544,128]{1,0:T(8,128)S(1)} %collective-permute-done.1.refs_2_, f32[544,128]{1,0:T(8,128)S(1)} %collective-permute-done.2.refs_3_, ...), custom_call_target="tpu_custom_call", output_to_operand_aliasing={{}: (10, {})} | custom-call | flops 5096079360 | bytes 20000000 | tf_op jit(solution)/shard_map/lon_products/pallas_call | solution.py:262
  (53 shorter events, 0.7 us)
Async XLA Ops:
  4.9 5.7 %copy-start.7 = (f32[720,16]{0,1:T(8,128)S(1)}, f32[720,16]{0,1:T(8,128)}, u32[]{:S(2)}) copy-start(f32[720,16]{0,1:T(8,128)} %param.10) | copy-start | bytes 138244
  4.9 5.9 %copy-start.6 = (f32[1440,16]{0,1:T(8,128)S(1)}, f32[1440,16]{0,1:T(8,128)}, u32[]{:S(2)}) copy-start(f32[1440,16]{0,1:T(8,128)} %param.9) | copy-start | bytes 276484
  4.9 6.4 %copy-start.8 = (s32[8]{0:T(128)S(1)}, s32[8]{0:T(128)}, u32[]{:S(2)}) copy-start(s32[8]{0:T(128)} %constant.15.clone) | copy-start | bytes 100
  4.9 72.4 %all-to-all-start = ((f32[16,552,128]{2,1,0:T(8,128)}), f32[16,552,128]{2,1,0:T(8,128)}, u32[]{:S(2)}, u32[]{:S(2)}) async-start(f32[16,552,128]{2,1,0:T(8,128)} %day_products.1), calls=%async_computation | async-start | bytes 9043968 | tf_op jit(solution)/shard_map/all_to_all | solution.py:287
  10.9 2.7 %copy-start.3 = (f32[3]{0:T(128)S(1)}, f32[3]{0:T(128)}, u32[]{:S(2)}) copy-start(f32[3]{0:T(128)} %scales.5) | copy-start | bytes 40
  19.6 1.5 copy-start.4
  21.1 1.4 copy-start.5
  43.2 3.6 %copy-start = (bf16[2,1536,1536]{2,1,0:T(8,128)(2,1)}, bf16[2,1536,1536]{2,1,0:T(8,128)(2,1)S(1)}, u32[]{:S(2)}) copy-start(bf16[2,1536,1536]{2,1,0:T(8,128)(2,1)S(1)} %get-tuple-element.53.refs_8_) | copy-start | bytes 28311556
  46.8 3.6 %copy-start.1 = (bf16[2,1536,1536]{2,1,0:T(8,128)(2,1)}, bf16[2,1536,1536]{2,1,0:T(8,128)(2,1)S(1)}, u32[]{:S(2)}) copy-start(bf16[2,1536,1536]{2,1,0:T(8,128)(2,1)S(1)} %get-tuple-element.54.refs_9_) | copy-start | bytes 28311556
  83.7 9.6 %collective-permute-start.14 = (f32[544,128]{1,0:T(8,128)S(1)}, f32[544,128]{1,0:T(8,128)S(1)}, u32[]{:S(2)}, u32[]{:S(2)}) collective-permute-start(f32[544,128]{1,0:T(8,128)S(1)} %get-tuple-element.64), channel_id=1, source_target_pairs={{0,16},{16,0},{32,48},{48,32},{64,80},{80,64},{96,112},{112,96},{1... | collective-permute-start | bytes 835592 | tf_op jit(solution)/shard_map/ppermute | solution.py:306
  85.2 18.6 %collective-permute-start.15 = (f32[544,128]{1,0:T(8,128)S(1)}, f32[544,128]{1,0:T(8,128)S(1)}, u32[]{:S(2)}, u32[]{:S(2)}) collective-permute-start(f32[544,128]{1,0:T(8,128)S(1)} %get-tuple-element.65), channel_id=1, source_target_pairs={{0,96},{16,112},{32,64},{48,80},{64,32},{80,48},{96,0},{112,16},{1... | collective-permute-start | bytes 835592 | tf_op jit(solution)/shard_map/ppermute | solution.py:306
  90.3 15.8 %collective-permute-start.16 = (f32[544,128]{1,0:T(8,128)S(1)}, f32[544,128]{1,0:T(8,128)S(1)}, u32[]{:S(2)}, u32[]{:S(2)}) collective-permute-start(f32[544,128]{1,0:T(8,128)S(1)} %get-tuple-element.66), channel_id=1, source_target_pairs={{0,64},{16,80},{32,96},{48,112},{64,0},{80,16},{96,32},{112,48},{1... | collective-permute-start | bytes 835592 | tf_op jit(solution)/shard_map/ppermute | solution.py:306
  90.9 21.9 %collective-permute-start.17 = (f32[544,128]{1,0:T(8,128)S(1)}, f32[544,128]{1,0:T(8,128)S(1)}, u32[]{:S(2)}, u32[]{:S(2)}) collective-permute-start(f32[544,128]{1,0:T(8,128)S(1)} %get-tuple-element.67), channel_id=1, source_target_pairs={{0,48},{16,32},{32,16},{48,0},{64,112},{80,96},{96,80},{112,64},{1... | collective-permute-start | bytes 835592 | tf_op jit(solution)/shard_map/ppermute | solution.py:306
  91.4 24.1 %collective-permute-start.18 = (f32[544,128]{1,0:T(8,128)S(1)}, f32[544,128]{1,0:T(8,128)S(1)}, u32[]{:S(2)}, u32[]{:S(2)}) collective-permute-start(f32[544,128]{1,0:T(8,128)S(1)} %get-tuple-element.68), channel_id=1, source_target_pairs={{0,32},{16,48},{32,0},{48,16},{64,96},{80,112},{96,64},{112,80},{1... | collective-permute-start | bytes 835592 | tf_op jit(solution)/shard_map/ppermute | solution.py:306
  93.2 22.9 %collective-permute-start.19 = (f32[544,128]{1,0:T(8,128)S(1)}, f32[544,128]{1,0:T(8,128)S(1)}, u32[]{:S(2)}, u32[]{:S(2)}) collective-permute-start(f32[544,128]{1,0:T(8,128)S(1)} %get-tuple-element.69), channel_id=1, source_target_pairs={{0,80},{16,64},{32,112},{48,96},{64,16},{80,0},{96,48},{112,32},{1... | collective-permute-start | bytes 835592 | tf_op jit(solution)/shard_map/ppermute | solution.py:306
  97.4 42.9 %slice-start = ((s8[9437184]{0:T(1024)(128)(4,1)}), s8[4194304]{0:T(1024)(128)(4,1)S(1)}, s32[]{:S(2)}) async-start(s8[9437184]{0:T(1024)(128)(4,1)} %bitcast.23), calls=%async_computation.1 | async-start | bytes 8388608
  97.4 42.9 %slice-start.1 = ((s8[9437184]{0:T(1024)(128)(4,1)}), s8[4194304]{0:T(1024)(128)(4,1)S(1)}, s32[]{:S(2)}) async-start(s8[9437184]{0:T(1024)(128)(4,1)} %bitcast.23), calls=%async_computation.2 | async-start | bytes 8388608
  97.4 42.9 %copy-start.2 = (bf16[2,1536,1536]{2,1,0:T(8,128)(2,1)S(1)}, bf16[2,1536,1536]{2,1,0:T(8,128)(2,1)}, u32[]{:S(2)}) copy-start(bf16[2,1536,1536]{2,1,0:T(8,128)(2,1)} %copy-done.1) | copy-start | bytes 28311556
  103.8 23.3 %collective-permute-start.20 = (f32[544,128]{1,0:T(8,128)S(1)}, f32[544,128]{1,0:T(8,128)S(1)}, u32[]{:S(2)}, u32[]{:S(2)}) collective-permute-start(f32[544,128]{1,0:T(8,128)S(1)} %get-tuple-element.70), channel_id=1, source_target_pairs={{0,112},{16,96},{32,80},{48,64},{64,48},{80,32},{96,16},{112,0},{1... | collective-permute-start | bytes 835592 | tf_op jit(solution)/shard_map/ppermute | solution.py:306
  106.1 21.1 %collective-permute-start.7 = (f32[544,128]{1,0:T(8,128)S(1)}, f32[544,128]{1,0:T(8,128)S(1)}, u32[]{:S(2)}, u32[]{:S(2)}) collective-permute-start(f32[544,128]{1,0:T(8,128)S(1)} %get-tuple-element.56), channel_id=1, source_target_pairs={{0,16},{16,0},{32,48},{48,32},{64,80},{80,64},{96,112},{112,96},{1... | collective-permute-start | bytes 835592 | tf_op jit(solution)/shard_map/ppermute | solution.py:306
  112.9 16.1 %collective-permute-start.8 = (f32[544,128]{1,0:T(8,128)S(1)}, f32[544,128]{1,0:T(8,128)S(1)}, u32[]{:S(2)}, u32[]{:S(2)}) collective-permute-start(f32[544,128]{1,0:T(8,128)S(1)} %get-tuple-element.57), channel_id=1, source_target_pairs={{0,96},{16,112},{32,64},{48,80},{64,32},{80,48},{96,0},{112,16},{1... | collective-permute-start | bytes 835592 | tf_op jit(solution)/shard_map/ppermute | solution.py:306
  115.5 19.8 %collective-permute-start.9 = (f32[544,128]{1,0:T(8,128)S(1)}, f32[544,128]{1,0:T(8,128)S(1)}, u32[]{:S(2)}, u32[]{:S(2)}) collective-permute-start(f32[544,128]{1,0:T(8,128)S(1)} %get-tuple-element.58), channel_id=1, source_target_pairs={{0,64},{16,80},{32,96},{48,112},{64,0},{80,16},{96,32},{112,48},{1... | collective-permute-start | bytes 835592 | tf_op jit(solution)/shard_map/ppermute | solution.py:306
  116.1 24.2 %slice-start.2 = ((s8[9437184]{0:T(1024)(128)(4,1)}), s8[1048576]{0:T(1024)(128)(4,1)S(1)}, s32[]{:S(2)}) async-start(s8[9437184]{0:T(1024)(128)(4,1)} %bitcast.23), calls=%async_computation.3 | async-start | bytes 2097152
  116.1 20.7 %collective-permute-start.10 = (f32[544,128]{1,0:T(8,128)S(1)}, f32[544,128]{1,0:T(8,128)S(1)}, u32[]{:S(2)}, u32[]{:S(2)}) collective-permute-start(f32[544,128]{1,0:T(8,128)S(1)} %get-tuple-element.59), channel_id=1, source_target_pairs={{0,48},{16,32},{32,16},{48,0},{64,112},{80,96},{96,80},{112,64},{1... | collective-permute-start | bytes 835592 | tf_op jit(solution)/shard_map/ppermute | solution.py:306
  127.2 26.3 %collective-permute-start.11 = (f32[544,128]{1,0:T(8,128)S(1)}, f32[544,128]{1,0:T(8,128)S(1)}, u32[]{:S(2)}, u32[]{:S(2)}) collective-permute-start(f32[544,128]{1,0:T(8,128)S(1)} %get-tuple-element.60), channel_id=1, source_target_pairs={{0,32},{16,48},{32,0},{48,16},{64,96},{80,112},{96,64},{112,80},{1... | collective-permute-start | bytes 835592 | tf_op jit(solution)/shard_map/ppermute | solution.py:306
  127.2 26.9 %collective-permute-start.12 = (f32[544,128]{1,0:T(8,128)S(1)}, f32[544,128]{1,0:T(8,128)S(1)}, u32[]{:S(2)}, u32[]{:S(2)}) collective-permute-start(f32[544,128]{1,0:T(8,128)S(1)} %get-tuple-element.61), channel_id=1, source_target_pairs={{0,80},{16,64},{32,112},{48,96},{64,16},{80,0},{96,48},{112,32},{1... | collective-permute-start | bytes 835592 | tf_op jit(solution)/shard_map/ppermute | solution.py:306
  128.9 27.8 %collective-permute-start.13 = (f32[544,128]{1,0:T(8,128)S(1)}, f32[544,128]{1,0:T(8,128)S(1)}, u32[]{:S(2)}, u32[]{:S(2)}) collective-permute-start(f32[544,128]{1,0:T(8,128)S(1)} %get-tuple-element.62), channel_id=1, source_target_pairs={{0,112},{16,96},{32,80},{48,64},{64,48},{80,32},{96,16},{112,0},{1... | collective-permute-start | bytes 835592 | tf_op jit(solution)/shard_map/ppermute | solution.py:306
  135.3 21.4 %collective-permute-start = (f32[544,128]{1,0:T(8,128)S(1)}, f32[544,128]{1,0:T(8,128)S(1)}, u32[]{:S(2)}, u32[]{:S(2)}) collective-permute-start(f32[544,128]{1,0:T(8,128)S(1)} %get-tuple-element.46), channel_id=1, source_target_pairs={{0,16},{16,0},{32,48},{48,32},{64,80},{80,64},{96,112},{112,96},{1... | collective-permute-start | bytes 835592 | tf_op jit(solution)/shard_map/ppermute | solution.py:306
  136.8 23.7 %collective-permute-start.1 = (f32[544,128]{1,0:T(8,128)S(1)}, f32[544,128]{1,0:T(8,128)S(1)}, u32[]{:S(2)}, u32[]{:S(2)}) collective-permute-start(f32[544,128]{1,0:T(8,128)S(1)} %get-tuple-element.47), channel_id=1, source_target_pairs={{0,96},{16,112},{32,64},{48,80},{64,32},{80,48},{96,0},{112,16},{1... | collective-permute-start | bytes 835592 | tf_op jit(solution)/shard_map/ppermute | solution.py:306
  153.5 17.2 %collective-permute-start.2 = (f32[544,128]{1,0:T(8,128)S(1)}, f32[544,128]{1,0:T(8,128)S(1)}, u32[]{:S(2)}, u32[]{:S(2)}) collective-permute-start(f32[544,128]{1,0:T(8,128)S(1)} %get-tuple-element.48), channel_id=1, source_target_pairs={{0,64},{16,80},{32,96},{48,112},{64,0},{80,16},{96,32},{112,48},{1... | collective-permute-start | bytes 835592 | tf_op jit(solution)/shard_map/ppermute | solution.py:306
  154.1 16.7 %collective-permute-start.3 = (f32[544,128]{1,0:T(8,128)S(1)}, f32[544,128]{1,0:T(8,128)S(1)}, u32[]{:S(2)}, u32[]{:S(2)}) collective-permute-start(f32[544,128]{1,0:T(8,128)S(1)} %get-tuple-element.49), channel_id=1, source_target_pairs={{0,48},{16,32},{32,16},{48,0},{64,112},{80,96},{96,80},{112,64},{1... | collective-permute-start | bytes 835592 | tf_op jit(solution)/shard_map/ppermute | solution.py:306
  156.8 14.0 %collective-permute-start.4 = (f32[544,128]{1,0:T(8,128)S(1)}, f32[544,128]{1,0:T(8,128)S(1)}, u32[]{:S(2)}, u32[]{:S(2)}) collective-permute-start(f32[544,128]{1,0:T(8,128)S(1)} %get-tuple-element.50), channel_id=1, source_target_pairs={{0,32},{16,48},{32,0},{48,16},{64,96},{80,112},{96,64},{112,80},{1... | collective-permute-start | bytes 835592 | tf_op jit(solution)/shard_map/ppermute | solution.py:306
  156.8 15.5 %collective-permute-start.5 = (f32[544,128]{1,0:T(8,128)S(1)}, f32[544,128]{1,0:T(8,128)S(1)}, u32[]{:S(2)}, u32[]{:S(2)}) collective-permute-start(f32[544,128]{1,0:T(8,128)S(1)} %get-tuple-element.51), channel_id=1, source_target_pairs={{0,80},{16,64},{32,112},{48,96},{64,16},{80,0},{96,48},{112,32},{1... | collective-permute-start | bytes 835592 | tf_op jit(solution)/shard_map/ppermute | solution.py:306
  160.5 16.9 %collective-permute-start.6 = (f32[544,128]{1,0:T(8,128)S(1)}, f32[544,128]{1,0:T(8,128)S(1)}, u32[]{:S(2)}, u32[]{:S(2)}) collective-permute-start(f32[544,128]{1,0:T(8,128)S(1)} %get-tuple-element.52), channel_id=1, source_target_pairs={{0,112},{16,96},{32,80},{48,64},{64,48},{80,32},{96,16},{112,0},{1... | collective-permute-start | bytes 835592 | tf_op jit(solution)/shard_map/ppermute | solution.py:306

commit v5 on v4

--- a/solution.py
+++ b/solution.py
@@ -307,11 +307,11 @@
             for term, step in zip(terms[1:], STEPS[1:])
         ]
 
+    (by_day,) = lat_products(moved, *lat_factors, ((1, 0),))
     (plain,) = lat_products(moved, *lat_factors, ((0, 0),))
-    (by_day,) = lat_products(moved, *lat_factors, ((1, 0),))
     (by_lat,) = lat_products(moved, *lat_factors, ((0, 1),))
-    result = lon_products(exchanged(plain), *lon_factors, (0, 2))
-    result = lon_products(exchanged(by_day), *lon_factors, (1,), result)
+    result = lon_products(exchanged(by_day), *lon_factors, (1,))
+    result = lon_products(exchanged(plain), *lon_factors, (0, 2), result)
     result = lon_products(exchanged(by_lat), *lon_factors, (3,), result)
     result = result.reshape(2, 4, OUT_LATS, 2, NL)
     return jnp.transpose(result, (0, 1, 3, 2, 4))

time: 185 us -> 179 us (0.968)
  waiting for transfers between devices: 46.5 us -> 40.7 us
    ppermute x21, waiting for transfers between devices: 19.5 us -> 13.8 us  [exchanged(): lax.ppermute(term, 'lon', [(i, i ^ step) for i in range(8)])]
  transfers between devices with their start and end apart: 22 -> 22, of which waited for: 9 -> 7; matrix products, arithmetic and copies ran while one was open for 1% -> 2% of each run, Pallas kernels for 32% -> 33%
where the time goes in v5:
time: 179 us
  Pallas kernels  78.5 us (44%)
  starting transfers between devices  46.7 us (26%)
  waiting for transfers between devices  40.7 us (23%)
  local copies, waits for them, and re-layouts  12.9 us (7%)
    ppermute x21, starting transfers between devices, exchanged(): lax.ppermute(term, 'lon', [(i, i ^ step) for i in range(8)])  41 us
    pallas_call x3, Pallas kernels, lon_products(): pl.pallas_call(functools.partial(lon_kernel, count), grid=(pl.cdiv(NL, wi...  27.9 us
    all_to_all x1, waiting for transfers between devices, local(): moved = lax.all_to_all(sent, 'lat', split_axis=0, concat_axis=0, tiled=True)  26.9 us
    pallas_call x2, Pallas kernels, factor_halves(): pl.pallas_call(functools.partial(factor_kernel, which, count), grid=(nr /...  26.7 us
    pallas_call x3, Pallas kernels, lat_products(): pl.pallas_call(functools.partial(lat_kernel, kinds), grid=(1,), out_shape...  19 us
    ppermute x21, waiting for transfers between devices, exchanged(): lax.ppermute(term, 'lon', [(i, i ^ step) for i in range(8)])  13.8 us
    unnamed x27, local copies, waits for them, and re-layouts  10.6 us
    all_to_all x1, starting transfers between devices, local(): moved = lax.all_to_all(sent, 'lat', split_axis=0, concat_axis=0, tiled=True)  5.68 us
  transfers between devices with their start and end apart: 22, of which 7 were waited for; matrix products, arithmetic and copies ran while one was open for 2% of the time, Pallas kernels for 33%

profile of v5, /device:TPU:96, one launch (start us, length us, event | category | flops | bytes accessed | tf_op | source)
XLA Modules:
  0.0 179.1 jit_solution(11730223437574464758)
XLA Ops:
  0.0 4.9 %day_products.1 = f32[16,552,128]{2,1,0:T(8,128)} custom-call(f32[3]{0:T(128)} %scales.5, f32[16,32]{1,0:T(8,128)} %bitcast.28, f32[45,32,180]{2,1,0:T(8,128)} %bitcast.26, f32[45,32,180]{2,1,0:T(8,128)} %bitcast.27), custom_call_target="tpu_custom_call" | custom-call | tf_op jit(solution)/shard_map/day_products/pallas_call | solution.py:109
  4.9 5.7 %all-to-all-start = ((f32[16,552,128]{2,1,0:T(8,128)}), f32[16,552,128]{2,1,0:T(8,128)}, u32[]{:S(2)}, u32[]{:S(2)}) async-start(f32[16,552,128]{2,1,0:T(8,128)} %day_products.1), calls=%async_computation | async-start | bytes 9043968 | tf_op jit(solution)/shard_map/all_to_all | solution.py:287
  10.7 0.1 reshape.30
  10.9 0.1 reshape.32
  11.0 0.3 copy.36
  11.4 0.6 gather_fusion
  11.9 0.6 gather_fusion.1
  12.7 0.1 reshape.31
  12.8 0.2 copy.32.cols
  12.9 0.2 copy.38
  13.2 0.3 copy.37.rows
  13.6 6.0 %factors.2 = (bf16[2,768,736]{2,1,0:T(8,128)(2,1)S(1)}, bf16[2,768,736]{2,1,0:T(8,128)(2,1)S(1)}) custom-call(f32[3]{0:T(128)S(1)} %copy-done.3, f32[768,16]{1,0:T(8,128)S(1)} %bitcast.25, f32[736,16]{1,0:T(8,128)S(1)} %copy.32.cols), custom_call_target="tpu_custom_call" | custom-call | flops 108527616 | bytes 4521984 | tf_op jit(solution)/shard_map/factors/pallas_call | solution.py:136
  19.6 1.5 copy-done.4
  21.1 1.4 copy-done.5
  22.5 20.7 %factors.3 = (bf16[2,1536,1536]{2,1,0:T(8,128)(2,1)S(1)}, bf16[2,1536,1536]{2,1,0:T(8,128)(2,1)S(1)}) custom-call(f32[3]{0:T(128)S(1)} %copy-done.3, f32[1536,16]{1,0:T(8,128)S(1)} %copy.37.rows, f32[1536,16]{1,0:T(8,128)S(1)} %pad.19.cols), custom_call_target="tpu_custom_call" | custom-call | flops 452984832 | bytes 18874368 | tf_op jit(solution)/shard_map/factors/pallas_call | solution.py:136
  43.2 3.6 %copy-done = bf16[2,1536,1536]{2,1,0:T(8,128)(2,1)} copy-done((bf16[2,1536,1536]{2,1,0:T(8,128)(2,1)}, bf16[2,1536,1536]{2,1,0:T(8,128)(2,1)S(1)}, u32[]{:S(2)}) %copy-start) | copy-done | bytes 9437208
  46.8 3.6 %copy-done.1 = bf16[2,1536,1536]{2,1,0:T(8,128)(2,1)} copy-done((bf16[2,1536,1536]{2,1,0:T(8,128)(2,1)}, bf16[2,1536,1536]{2,1,0:T(8,128)(2,1)S(1)}, u32[]{:S(2)}) %copy-start.1) | copy-done | bytes 9437208
  50.4 26.9 %all-to-all-done = f32[16,552,128]{2,1,0:T(8,128)} async-done(((f32[16,552,128]{2,1,0:T(8,128)}), f32[16,552,128]{2,1,0:T(8,128)}, u32[]{:S(2)}, u32[]{:S(2)}) %all-to-all-start) | async-done | bytes 4522016 | tf_op jit(solution)/shard_map/all_to_all | solution.py:287
  77.4 6.3 %lat_products.5 = (f32[544,128]{1,0:T(8,128)S(1)}, f32[544,128]{1,0:T(8,128)S(1)}, f32[544,128]{1,0:T(8,128)S(1)}, f32[544,128]{1,0:T(8,128)S(1)}, f32[544,128]{...) custom-call(f32[8832,128]{1,0:T(8,128)} %bitcast.3.moved, ...), custom_call_target="tpu_custom_call" | custom-call | flops 2717908992 | bytes 10000000 | tf_op jit(solution)/shard_map/lat_products/pallas_call | solution.py:189
  83.7 1.6 collective-permute-start.14
  85.2 5.1 %collective-permute-start.15 = (f32[544,128]{1,0:T(8,128)S(1)}, f32[544,128]{1,0:T(8,128)S(1)}, u32[]{:S(2)}, u32[]{:S(2)}) collective-permute-start(f32[544,128]{1,0:T(8,128)S(1)} %get-tuple-element.65), channel_id=1, source_target_pairs={{0,96},{16,112},{32,64},{48,80},{64,32},{80,48},{96,0},{112,16},{1... | collective-permute-start | bytes 835592 | tf_op jit(solution)/shard_map/ppermute | solution.py:306
  90.3 0.6 collective-permute-start.16
  90.9 0.5 collective-permute-start.17
  91.4 1.8 %collective-permute-start.18 = (f32[544,128]{1,0:T(8,128)S(1)}, f32[544,128]{1,0:T(8,128)S(1)}, u32[]{:S(2)}, u32[]{:S(2)}) collective-permute-start(f32[544,128]{1,0:T(8,128)S(1)} %get-tuple-element.68), channel_id=1, source_target_pairs={{0,32},{16,48},{32,0},{48,16},{64,96},{80,112},{96,64},{112,80},{1... | collective-permute-start | bytes 835592 | tf_op jit(solution)/shard_map/ppermute | solution.py:306
  93.2 4.1 %collective-permute-start.19 = (f32[544,128]{1,0:T(8,128)S(1)}, f32[544,128]{1,0:T(8,128)S(1)}, u32[]{:S(2)}, u32[]{:S(2)}) collective-permute-start(f32[544,128]{1,0:T(8,128)S(1)} %get-tuple-element.69), channel_id=1, source_target_pairs={{0,80},{16,64},{32,112},{48,96},{64,16},{80,0},{96,48},{112,32},{1... | collective-permute-start | bytes 835592 | tf_op jit(solution)/shard_map/ppermute | solution.py:306
  97.4 6.4 %lat_products.4 = (f32[544,128]{1,0:T(8,128)S(1)}, f32[544,128]{1,0:T(8,128)S(1)}, f32[544,128]{1,0:T(8,128)S(1)}, f32[544,128]{1,0:T(8,128)S(1)}, f32[544,128]{...) custom-call(f32[8832,128]{1,0:T(8,128)} %bitcast.3.moved, ...), custom_call_target="tpu_custom_call" | custom-call | flops 2717908992 | bytes 10000000 | tf_op jit(solution)/shard_map/lat_products/pallas_call | solution.py:189
  103.8 1.9 %collective-permute-start.20 = (f32[544,128]{1,0:T(8,128)S(1)}, f32[544,128]{1,0:T(8,128)S(1)}, u32[]{:S(2)}, u32[]{:S(2)}) collective-permute-start(f32[544,128]{1,0:T(8,128)S(1)} %get-tuple-element.70), channel_id=1, source_target_pairs={{0,112},{16,96},{32,80},{48,64},{64,48},{80,32},{96,16},{112,0},{1... | collective-permute-start | bytes 835592 | tf_op jit(solution)/shard_map/ppermute | solution.py:306
  105.7 0.3 collective-permute-done.16.refs_3_
  106.1 0.3 collective-permute-start.7
  106.4 6.5 %collective-permute-done.17.refs_4_ = f32[544,128]{1,0:T(8,128)S(1)} collective-permute-done((f32[544,128]{1,0:T(8,128)S(1)}, f32[544,128]{1,0:T(8,128)S(1)}, u32[]{:S(2)}, u32[]{:S(2)}) %collective-permute-start.17) | collective-permute-done | bytes 278560 | tf_op jit(solution)/shard_map/ppermute | solution.py:306
  112.9 2.6 %collective-permute-start.8 = (f32[544,128]{1,0:T(8,128)S(1)}, f32[544,128]{1,0:T(8,128)S(1)}, u32[]{:S(2)}, u32[]{:S(2)}) collective-permute-start(f32[544,128]{1,0:T(8,128)S(1)} %get-tuple-element.57), channel_id=1, source_target_pairs={{0,96},{16,112},{32,64},{48,80},{64,32},{80,48},{96,0},{112,16},{1... | collective-permute-start | bytes 835592 | tf_op jit(solution)/shard_map/ppermute | solution.py:306
  115.5 0.6 collective-permute-start.9
  116.1 2.1 %collective-permute-start.10 = (f32[544,128]{1,0:T(8,128)S(1)}, f32[544,128]{1,0:T(8,128)S(1)}, u32[]{:S(2)}, u32[]{:S(2)}) collective-permute-start(f32[544,128]{1,0:T(8,128)S(1)} %get-tuple-element.59), channel_id=1, source_target_pairs={{0,48},{16,32},{32,16},{48,0},{64,112},{80,96},{96,80},{112,64},{1... | collective-permute-start | bytes 835592 | tf_op jit(solution)/shard_map/ppermute | solution.py:306
  118.2 6.3 %lat_products.3 = (f32[544,128]{1,0:T(8,128)S(1)}, f32[544,128]{1,0:T(8,128)S(1)}, f32[544,128]{1,0:T(8,128)S(1)}, f32[544,128]{1,0:T(8,128)S(1)}, f32[544,128]{...) custom-call(f32[8832,128]{1,0:T(8,128)} %bitcast.3.moved, ...), custom_call_target="tpu_custom_call" | custom-call | flops 2717908992 | bytes 10000000 | tf_op jit(solution)/shard_map/lat_products/pallas_call | solution.py:189
  124.5 2.7 %collective-permute-done.20.refs_7_ = f32[544,128]{1,0:T(8,128)S(1)} collective-permute-done((f32[544,128]{1,0:T(8,128)S(1)}, f32[544,128]{1,0:T(8,128)S(1)}, u32[]{:S(2)}, u32[]{:S(2)}) %collective-permute-start.20) | collective-permute-done | bytes 278560 | tf_op jit(solution)/shard_map/ppermute | solution.py:306
  127.2 1.7 collective-permute-start.12
  128.9 4.8 %collective-permute-start.13 = (f32[544,128]{1,0:T(8,128)S(1)}, f32[544,128]{1,0:T(8,128)S(1)}, u32[]{:S(2)}, u32[]{:S(2)}) collective-permute-start(f32[544,128]{1,0:T(8,128)S(1)} %get-tuple-element.62), channel_id=1, source_target_pairs={{0,112},{16,96},{32,80},{48,64},{64,48},{80,32},{96,16},{112,0},{1... | collective-permute-start | bytes 835592 | tf_op jit(solution)/shard_map/ppermute | solution.py:306
  133.7 1.6 collective-permute-done.9.refs_3_
  135.3 1.5 collective-permute-done.10.refs_4_
  136.8 3.5 %collective-permute-start.1 = (f32[544,128]{1,0:T(8,128)S(1)}, f32[544,128]{1,0:T(8,128)S(1)}, u32[]{:S(2)}, u32[]{:S(2)}) collective-permute-start(f32[544,128]{1,0:T(8,128)S(1)} %get-tuple-element.47), channel_id=1, source_target_pairs={{0,96},{16,112},{32,64},{48,80},{64,32},{80,48},{96,0},{112,16},{1... | collective-permute-start | bytes 835592 | tf_op jit(solution)/shard_map/ppermute | solution.py:306
  140.3 7.4 %lon_products.3.refs_10_ = f32[2,2,2,90,2,1440]{5,4,3,2,1,0:T(2,128)} custom-call(f32[544,128]{1,0:T(8,128)S(1)} %get-tuple-element.63.refs_0_, f32[544,128]{1,0:T(8,128)S(1)} %collective-permute-done.14.refs_1_, f32[544,128]{1,0:T(8,128)S(1)} %collective-permute-done.15.refs_2_, f32[544,128]{1,0:T(8,128)S(1)} %collective-permute-done.16.refs_3_, ...), custom_call_target="tpu_custom_call" | custom-call | flops 5096079360 | bytes 20000000 | tf_op jit(solution)/shard_map/lon_products/pallas_call | solution.py:262
  147.7 0.7 collective-permute-start.2
  148.4 2.6 %collective-permute-start.3 = (f32[544,128]{1,0:T(8,128)S(1)}, f32[544,128]{1,0:T(8,128)S(1)}, u32[]{:S(2)}, u32[]{:S(2)}) collective-permute-start(f32[544,128]{1,0:T(8,128)S(1)} %get-tuple-element.49), channel_id=1, source_target_pairs={{0,48},{16,32},{32,16},{48,0},{64,112},{80,96},{96,80},{112,64},{1... | collective-permute-start | bytes 835592 | tf_op jit(solution)/shard_map/ppermute | solution.py:306
  151.1 3.8 %collective-permute-start.5 = (f32[544,128]{1,0:T(8,128)S(1)}, f32[544,128]{1,0:T(8,128)S(1)}, u32[]{:S(2)}, u32[]{:S(2)}) collective-permute-start(f32[544,128]{1,0:T(8,128)S(1)} %get-tuple-element.51), channel_id=1, source_target_pairs={{0,80},{16,64},{32,112},{48,96},{64,16},{80,0},{96,48},{112,32},{1... | collective-permute-start | bytes 835592 | tf_op jit(solution)/shard_map/ppermute | solution.py:306
  154.8 2.7 %collective-permute-start.6 = (f32[544,128]{1,0:T(8,128)S(1)}, f32[544,128]{1,0:T(8,128)S(1)}, u32[]{:S(2)}, u32[]{:S(2)}) collective-permute-start(f32[544,128]{1,0:T(8,128)S(1)} %get-tuple-element.52), channel_id=1, source_target_pairs={{0,112},{16,96},{32,80},{48,64},{64,48},{80,32},{96,16},{112,0},{1... | collective-permute-start | bytes 835592 | tf_op jit(solution)/shard_map/ppermute | solution.py:306
  157.6 13.1 %lon_products.4.refs_10_ = f32[2,2,2,90,2,1440]{5,4,3,2,1,0:T(2,128)} custom-call(f32[544,128]{1,0:T(8,128)S(1)} %get-tuple-element.55.refs_0_, f32[544,128]{1,0:T(8,128)S(1)} %collective-permute-done.7.refs_1_, f32[544,128]{1,0:T(8,128)S(1)} %collective-permute-done.8.refs_2_, ...), custom_call_target="tpu_custom_call", output_to_operand_aliasing={{}: (10, {})} | custom-call | flops 10192158720 | bytes 20000000 | tf_op jit(solution)/shard_map/lon_products/pallas_call | solution.py:262
  170.7 1.1 collective-permute-done.6.refs_7_
  171.7 7.4 %lon_products.5 = f32[2,2,2,90,2,1440]{5,4,3,2,1,0:T(2,128)} custom-call(f32[544,128]{1,0:T(8,128)S(1)} %get-tuple-element.45.refs_0_, f32[544,128]{1,0:T(8,128)S(1)} %collective-permute-done.refs_1_, f32[544,128]{1,0:T(8,128)S(1)} %collective-permute-done.1.refs_2_, f32[544,128]{1,0:T(8,128)S(1)} %collective-permute-done.2.refs_3_, ...), custom_call_target="tpu_custom_call", output_to_operand_aliasing={{}: (10, {})} | custom-call | flops 5096079360 | bytes 20000000 | tf_op jit(solution)/shard_map/lon_products/pallas_call | solution.py:262
  (53 shorter events, 0.5 us)
Async XLA Ops:
  4.9 5.7 %copy-start.7 = (f32[720,16]{0,1:T(8,128)S(1)}, f32[720,16]{0,1:T(8,128)}, u32[]{:S(2)}) copy-start(f32[720,16]{0,1:T(8,128)} %param.10) | copy-start | bytes 138244
  4.9 5.9 %copy-start.6 = (f32[1440,16]{0,1:T(8,128)S(1)}, f32[1440,16]{0,1:T(8,128)}, u32[]{:S(2)}) copy-start(f32[1440,16]{0,1:T(8,128)} %param.9) | copy-start | bytes 276484
  4.9 6.4 %copy-start.8 = (s32[8]{0:T(128)S(1)}, s32[8]{0:T(128)}, u32[]{:S(2)}) copy-start(s32[8]{0:T(128)} %constant.15.clone) | copy-start | bytes 100
  4.9 72.4 %all-to-all-start = ((f32[16,552,128]{2,1,0:T(8,128)}), f32[16,552,128]{2,1,0:T(8,128)}, u32[]{:S(2)}, u32[]{:S(2)}) async-start(f32[16,552,128]{2,1,0:T(8,128)} %day_products.1), calls=%async_computation | async-start | bytes 9043968 | tf_op jit(solution)/shard_map/all_to_all | solution.py:287
  10.9 2.7 %copy-start.3 = (f32[3]{0:T(128)S(1)}, f32[3]{0:T(128)}, u32[]{:S(2)}) copy-start(f32[3]{0:T(128)} %scales.5) | copy-start | bytes 40
  19.6 1.5 copy-start.4
  21.1 1.4 copy-start.5
  43.2 3.6 %copy-start = (bf16[2,1536,1536]{2,1,0:T(8,128)(2,1)}, bf16[2,1536,1536]{2,1,0:T(8,128)(2,1)S(1)}, u32[]{:S(2)}) copy-start(bf16[2,1536,1536]{2,1,0:T(8,128)(2,1)S(1)} %get-tuple-element.53.refs_8_) | copy-start | bytes 28311556
  46.8 3.6 %copy-start.1 = (bf16[2,1536,1536]{2,1,0:T(8,128)(2,1)}, bf16[2,1536,1536]{2,1,0:T(8,128)(2,1)S(1)}, u32[]{:S(2)}) copy-start(bf16[2,1536,1536]{2,1,0:T(8,128)(2,1)S(1)} %get-tuple-element.54.refs_9_) | copy-start | bytes 28311556
  83.7 9.6 %collective-permute-start.14 = (f32[544,128]{1,0:T(8,128)S(1)}, f32[544,128]{1,0:T(8,128)S(1)}, u32[]{:S(2)}, u32[]{:S(2)}) collective-permute-start(f32[544,128]{1,0:T(8,128)S(1)} %get-tuple-element.64), channel_id=1, source_target_pairs={{0,16},{16,0},{32,48},{48,32},{64,80},{80,64},{96,112},{112,96},{1... | collective-permute-start | bytes 835592 | tf_op jit(solution)/shard_map/ppermute | solution.py:306
  85.2 18.6 %collective-permute-start.15 = (f32[544,128]{1,0:T(8,128)S(1)}, f32[544,128]{1,0:T(8,128)S(1)}, u32[]{:S(2)}, u32[]{:S(2)}) collective-permute-start(f32[544,128]{1,0:T(8,128)S(1)} %get-tuple-element.65), channel_id=1, source_target_pairs={{0,96},{16,112},{32,64},{48,80},{64,32},{80,48},{96,0},{112,16},{1... | collective-permute-start | bytes 835592 | tf_op jit(solution)/shard_map/ppermute | solution.py:306
  90.3 15.8 %collective-permute-start.16 = (f32[544,128]{1,0:T(8,128)S(1)}, f32[544,128]{1,0:T(8,128)S(1)}, u32[]{:S(2)}, u32[]{:S(2)}) collective-permute-start(f32[544,128]{1,0:T(8,128)S(1)} %get-tuple-element.66), channel_id=1, source_target_pairs={{0,64},{16,80},{32,96},{48,112},{64,0},{80,16},{96,32},{112,48},{1... | collective-permute-start | bytes 835592 | tf_op jit(solution)/shard_map/ppermute | solution.py:306
  90.9 21.9 %collective-permute-start.17 = (f32[544,128]{1,0:T(8,128)S(1)}, f32[544,128]{1,0:T(8,128)S(1)}, u32[]{:S(2)}, u32[]{:S(2)}) collective-permute-start(f32[544,128]{1,0:T(8,128)S(1)} %get-tuple-element.67), channel_id=1, source_target_pairs={{0,48},{16,32},{32,16},{48,0},{64,112},{80,96},{96,80},{112,64},{1... | collective-permute-start | bytes 835592 | tf_op jit(solution)/shard_map/ppermute | solution.py:306
  91.4 24.1 %collective-permute-start.18 = (f32[544,128]{1,0:T(8,128)S(1)}, f32[544,128]{1,0:T(8,128)S(1)}, u32[]{:S(2)}, u32[]{:S(2)}) collective-permute-start(f32[544,128]{1,0:T(8,128)S(1)} %get-tuple-element.68), channel_id=1, source_target_pairs={{0,32},{16,48},{32,0},{48,16},{64,96},{80,112},{96,64},{112,80},{1... | collective-permute-start | bytes 835592 | tf_op jit(solution)/shard_map/ppermute | solution.py:306
  93.2 22.9 %collective-permute-start.19 = (f32[544,128]{1,0:T(8,128)S(1)}, f32[544,128]{1,0:T(8,128)S(1)}, u32[]{:S(2)}, u32[]{:S(2)}) collective-permute-start(f32[544,128]{1,0:T(8,128)S(1)} %get-tuple-element.69), channel_id=1, source_target_pairs={{0,80},{16,64},{32,112},{48,96},{64,16},{80,0},{96,48},{112,32},{1... | collective-permute-start | bytes 835592 | tf_op jit(solution)/shard_map/ppermute | solution.py:306
  97.4 42.9 %slice-start = ((s8[9437184]{0:T(1024)(128)(4,1)}), s8[4194304]{0:T(1024)(128)(4,1)S(1)}, s32[]{:S(2)}) async-start(s8[9437184]{0:T(1024)(128)(4,1)} %bitcast.23), calls=%async_computation.1 | async-start | bytes 8388608
  97.4 42.9 %slice-start.1 = ((s8[9437184]{0:T(1024)(128)(4,1)}), s8[4194304]{0:T(1024)(128)(4,1)S(1)}, s32[]{:S(2)}) async-start(s8[9437184]{0:T(1024)(128)(4,1)} %bitcast.23), calls=%async_computation.2 | async-start | bytes 8388608
  97.4 42.9 %copy-start.2 = (bf16[2,1536,1536]{2,1,0:T(8,128)(2,1)S(1)}, bf16[2,1536,1536]{2,1,0:T(8,128)(2,1)}, u32[]{:S(2)}) copy-start(bf16[2,1536,1536]{2,1,0:T(8,128)(2,1)} %copy-done.1) | copy-start | bytes 28311556
  103.8 23.3 %collective-permute-start.20 = (f32[544,128]{1,0:T(8,128)S(1)}, f32[544,128]{1,0:T(8,128)S(1)}, u32[]{:S(2)}, u32[]{:S(2)}) collective-permute-start(f32[544,128]{1,0:T(8,128)S(1)} %get-tuple-element.70), channel_id=1, source_target_pairs={{0,112},{16,96},{32,80},{48,64},{64,48},{80,32},{96,16},{112,0},{1... | collective-permute-start | bytes 835592 | tf_op jit(solution)/shard_map/ppermute | solution.py:306
  106.1 21.1 %collective-permute-start.7 = (f32[544,128]{1,0:T(8,128)S(1)}, f32[544,128]{1,0:T(8,128)S(1)}, u32[]{:S(2)}, u32[]{:S(2)}) collective-permute-start(f32[544,128]{1,0:T(8,128)S(1)} %get-tuple-element.56), channel_id=1, source_target_pairs={{0,16},{16,0},{32,48},{48,32},{64,80},{80,64},{96,112},{112,96},{1... | collective-permute-start | bytes 835592 | tf_op jit(solution)/shard_map/ppermute | solution.py:306
  112.9 16.1 %collective-permute-start.8 = (f32[544,128]{1,0:T(8,128)S(1)}, f32[544,128]{1,0:T(8,128)S(1)}, u32[]{:S(2)}, u32[]{:S(2)}) collective-permute-start(f32[544,128]{1,0:T(8,128)S(1)} %get-tuple-element.57), channel_id=1, source_target_pairs={{0,96},{16,112},{32,64},{48,80},{64,32},{80,48},{96,0},{112,16},{1... | collective-permute-start | bytes 835592 | tf_op jit(solution)/shard_map/ppermute | solution.py:306
  115.5 19.8 %collective-permute-start.9 = (f32[544,128]{1,0:T(8,128)S(1)}, f32[544,128]{1,0:T(8,128)S(1)}, u32[]{:S(2)}, u32[]{:S(2)}) collective-permute-start(f32[544,128]{1,0:T(8,128)S(1)} %get-tuple-element.58), channel_id=1, source_target_pairs={{0,64},{16,80},{32,96},{48,112},{64,0},{80,16},{96,32},{112,48},{1... | collective-permute-start | bytes 835592 | tf_op jit(solution)/shard_map/ppermute | solution.py:306
  116.1 24.2 %slice-start.2 = ((s8[9437184]{0:T(1024)(128)(4,1)}), s8[1048576]{0:T(1024)(128)(4,1)S(1)}, s32[]{:S(2)}) async-start(s8[9437184]{0:T(1024)(128)(4,1)} %bitcast.23), calls=%async_computation.3 | async-start | bytes 2097152
  116.1 20.7 %collective-permute-start.10 = (f32[544,128]{1,0:T(8,128)S(1)}, f32[544,128]{1,0:T(8,128)S(1)}, u32[]{:S(2)}, u32[]{:S(2)}) collective-permute-start(f32[544,128]{1,0:T(8,128)S(1)} %get-tuple-element.59), channel_id=1, source_target_pairs={{0,48},{16,32},{32,16},{48,0},{64,112},{80,96},{96,80},{112,64},{1... | collective-permute-start | bytes 835592 | tf_op jit(solution)/shard_map/ppermute | solution.py:306
  127.2 20.6 %collective-permute-start.11 = (f32[544,128]{1,0:T(8,128)S(1)}, f32[544,128]{1,0:T(8,128)S(1)}, u32[]{:S(2)}, u32[]{:S(2)}) collective-permute-start(f32[544,128]{1,0:T(8,128)S(1)} %get-tuple-element.60), channel_id=1, source_target_pairs={{0,32},{16,48},{32,0},{48,16},{64,96},{80,112},{96,64},{112,80},{1... | collective-permute-start | bytes 835592 | tf_op jit(solution)/shard_map/ppermute | solution.py:306
  127.2 21.2 %collective-permute-start.12 = (f32[544,128]{1,0:T(8,128)S(1)}, f32[544,128]{1,0:T(8,128)S(1)}, u32[]{:S(2)}, u32[]{:S(2)}) collective-permute-start(f32[544,128]{1,0:T(8,128)S(1)} %get-tuple-element.61), channel_id=1, source_target_pairs={{0,80},{16,64},{32,112},{48,96},{64,16},{80,0},{96,48},{112,32},{1... | collective-permute-start | bytes 835592 | tf_op jit(solution)/shard_map/ppermute | solution.py:306
  128.9 22.1 %collective-permute-start.13 = (f32[544,128]{1,0:T(8,128)S(1)}, f32[544,128]{1,0:T(8,128)S(1)}, u32[]{:S(2)}, u32[]{:S(2)}) collective-permute-start(f32[544,128]{1,0:T(8,128)S(1)} %get-tuple-element.62), channel_id=1, source_target_pairs={{0,112},{16,96},{32,80},{48,64},{64,48},{80,32},{96,16},{112,0},{1... | collective-permute-start | bytes 835592 | tf_op jit(solution)/shard_map/ppermute | solution.py:306
  135.3 15.7 %collective-permute-start = (f32[544,128]{1,0:T(8,128)S(1)}, f32[544,128]{1,0:T(8,128)S(1)}, u32[]{:S(2)}, u32[]{:S(2)}) collective-permute-start(f32[544,128]{1,0:T(8,128)S(1)} %get-tuple-element.46), channel_id=1, source_target_pairs={{0,16},{16,0},{32,48},{48,32},{64,80},{80,64},{96,112},{112,96},{1... | collective-permute-start | bytes 835592 | tf_op jit(solution)/shard_map/ppermute | solution.py:306
  136.8 18.0 %collective-permute-start.1 = (f32[544,128]{1,0:T(8,128)S(1)}, f32[544,128]{1,0:T(8,128)S(1)}, u32[]{:S(2)}, u32[]{:S(2)}) collective-permute-start(f32[544,128]{1,0:T(8,128)S(1)} %get-tuple-element.47), channel_id=1, source_target_pairs={{0,96},{16,112},{32,64},{48,80},{64,32},{80,48},{96,0},{112,16},{1... | collective-permute-start | bytes 835592 | tf_op jit(solution)/shard_map/ppermute | solution.py:306
  147.7 22.9 %collective-permute-start.2 = (f32[544,128]{1,0:T(8,128)S(1)}, f32[544,128]{1,0:T(8,128)S(1)}, u32[]{:S(2)}, u32[]{:S(2)}) collective-permute-start(f32[544,128]{1,0:T(8,128)S(1)} %get-tuple-element.48), channel_id=1, source_target_pairs={{0,64},{16,80},{32,96},{48,112},{64,0},{80,16},{96,32},{112,48},{1... | collective-permute-start | bytes 835592 | tf_op jit(solution)/shard_map/ppermute | solution.py:306
  148.4 22.2 %collective-permute-start.3 = (f32[544,128]{1,0:T(8,128)S(1)}, f32[544,128]{1,0:T(8,128)S(1)}, u32[]{:S(2)}, u32[]{:S(2)}) collective-permute-start(f32[544,128]{1,0:T(8,128)S(1)} %get-tuple-element.49), channel_id=1, source_target_pairs={{0,48},{16,32},{32,16},{48,0},{64,112},{80,96},{96,80},{112,64},{1... | collective-permute-start | bytes 835592 | tf_op jit(solution)/shard_map/ppermute | solution.py:306
  151.1 19.6 %collective-permute-start.4 = (f32[544,128]{1,0:T(8,128)S(1)}, f32[544,128]{1,0:T(8,128)S(1)}, u32[]{:S(2)}, u32[]{:S(2)}) collective-permute-start(f32[544,128]{1,0:T(8,128)S(1)} %get-tuple-element.50), channel_id=1, source_target_pairs={{0,32},{16,48},{32,0},{48,16},{64,96},{80,112},{96,64},{112,80},{1... | collective-permute-start | bytes 835592 | tf_op jit(solution)/shard_map/ppermute | solution.py:306
  151.1 19.6 %collective-permute-start.5 = (f32[544,128]{1,0:T(8,128)S(1)}, f32[544,128]{1,0:T(8,128)S(1)}, u32[]{:S(2)}, u32[]{:S(2)}) collective-permute-start(f32[544,128]{1,0:T(8,128)S(1)} %get-tuple-element.51), channel_id=1, source_target_pairs={{0,80},{16,64},{32,112},{48,96},{64,16},{80,0},{96,48},{112,32},{1... | collective-permute-start | bytes 835592 | tf_op jit(solution)/shard_map/ppermute | solution.py:306
  154.8 16.9 %collective-permute-start.6 = (f32[544,128]{1,0:T(8,128)S(1)}, f32[544,128]{1,0:T(8,128)S(1)}, u32[]{:S(2)}, u32[]{:S(2)}) collective-permute-start(f32[544,128]{1,0:T(8,128)S(1)} %get-tuple-element.52), channel_id=1, source_target_pairs={{0,112},{16,96},{32,80},{48,64},{64,48},{80,32},{96,16},{112,0},{1... | collective-permute-start | bytes 835592 | tf_op jit(solution)/shard_map/ppermute | solution.py:306

commit v6 on v5

--- a/solution.py
+++ b/solution.py
@@ -224,8 +224,8 @@
 FIELD_ROWS = 192
 
 
-def lon_kernel(count, *refs):
-    terms, (high, low) = refs[:8], refs[8:10]
+def lon_kernel(count, order, *refs):
+    terms, (high, low) = [refs[order.index(at)] for at in range(8)], refs[8:10]
     out, z_high, z_low = refs[-3:]
     wide = out.shape[-1]
     cols = pl.ds(pl.multiple_of(pl.program_id(0) * wide, wide), wide)
@@ -248,19 +248,19 @@
             out[field, at, 0] = by_day(value, field * FIELD_ROWS)
 
 
-def lon_products(terms, high, low, operators, so_far=None, wide=512):
+def lon_products(terms, high, low, operators, so_far=None, wide=512, order=tuple(range(8))):
     count = len(operators)
     high_at, low_at = divmod(operators[0], 2)
     in_specs = [pl.BlockSpec((TERM_ROWS, 128), lambda n: (0, 0))] * 8
     in_specs += [pl.BlockSpec(memory_space=pltpu.VMEM)] * 2
-    args = [*terms] + [pltpu.with_memory_space_constraint(x, pltpu.VMEM) for x in (high, low)]
+    args = [terms[at] for at in order] + [pltpu.with_memory_space_constraint(x, pltpu.VMEM) for x in (high, low)]
     aliases = {}
     if so_far is not None:
         aliases = {len(args): 0}
         in_specs.append(pl.BlockSpec(memory_space=pl.ANY))
         args.append(so_far)
     return pl.pallas_call(
-        functools.partial(lon_kernel, count),
+        functools.partial(lon_kernel, count, order),
         grid=(pl.cdiv(NL, wide),),
         out_shape=jax.ShapeDtypeStruct((2, 2, 2, OUT_LATS, 2, NL), F32),
         in_specs=in_specs,
@@ -312,7 +312,9 @@
     (by_lat,) = lat_products(moved, *lat_factors, ((0, 1),))
     result = lon_products(exchanged(by_day), *lon_factors, (1,))
     result = lon_products(exchanged(plain), *lon_factors, (0, 2), result)
-    result = lon_products(exchanged(by_lat), *lon_factors, (3,), result)
+    result = lon_products(
+        exchanged(by_lat), *lon_factors, (3,), result, order=(0, 1, 2, 3, 6, 7, 4, 5)
+    )
     result = result.reshape(2, 4, OUT_LATS, 2, NL)
     return jnp.transpose(result, (0, 1, 3, 2, 4))
 

time: 179 us -> 179 us (level)
  transfers between devices with their start and end apart: 22 -> 22, of which waited for: 7 -> 8; matrix products, arithmetic and copies ran while one was open for 2% -> 2% of each run, Pallas kernels for 33% -> 33%
where the time goes in v6:
time: 179 us
  Pallas kernels  78.5 us (44%)
  starting transfers between devices  46.1 us (26%)
  waiting for transfers between devices  41.2 us (23%)
  local copies, waits for them, and re-layouts  12.9 us (7%)
    ppermute x21, starting transfers between devices, exchanged(): lax.ppermute(term, 'lon', [(i, i ^ step) for i in range(8)])  40.4 us
    pallas_call x3, Pallas kernels, lon_products(): pl.pallas_call(functools.partial(lon_kernel, count, order), grid=(pl.cdiv...  27.9 us
    all_to_all x1, waiting for transfers between devices, local(): moved = lax.all_to_all(sent, 'lat', split_axis=0, concat_axis=0, tiled=True)  26.9 us
    pallas_call x2, Pallas kernels, factor_halves(): pl.pallas_call(functools.partial(factor_kernel, which, count), grid=(nr /...  26.7 us
    pallas_call x3, Pallas kernels, lat_products(): pl.pallas_call(functools.partial(lat_kernel, kinds), grid=(1,), out_shape...  19 us
    ppermute x21, waiting for transfers between devices, exchanged(): lax.ppermute(term, 'lon', [(i, i ^ step) for i in range(8)])  14.3 us
    unnamed x27, local copies, waits for them, and re-layouts  10.6 us
    all_to_all x1, starting transfers between devices, local(): moved = lax.all_to_all(sent, 'lat', split_axis=0, concat_axis=0, tiled=True)  5.68 us
  transfers between devices with their start and end apart: 22, of which 8 were waited for; matrix products, arithmetic and copies ran while one was open for 2% of the time, Pallas kernels for 33%

profile of v6, /device:TPU:96, one launch (start us, length us, event | category | flops | bytes accessed | tf_op | source)
XLA Modules:
  0.0 179.0 jit_solution(8645436851924894014)
XLA Ops:
  0.0 4.9 %day_products.1 = f32[16,552,128]{2,1,0:T(8,128)} custom-call(f32[3]{0:T(128)} %scales.5, f32[16,32]{1,0:T(8,128)} %bitcast.28, f32[45,32,180]{2,1,0:T(8,128)} %bitcast.26, f32[45,32,180]{2,1,0:T(8,128)} %bitcast.27), custom_call_target="tpu_custom_call" | custom-call | tf_op jit(solution)/shard_map/day_products/pallas_call | solution.py:109
  4.9 5.7 %all-to-all-start = ((f32[16,552,128]{2,1,0:T(8,128)}), f32[16,552,128]{2,1,0:T(8,128)}, u32[]{:S(2)}, u32[]{:S(2)}) async-start(f32[16,552,128]{2,1,0:T(8,128)} %day_products.1), calls=%async_computation | async-start | bytes 9043968 | tf_op jit(solution)/shard_map/all_to_all | solution.py:287
  10.9 0.1 reshape.32
  11.0 0.3 copy.36
  11.4 0.6 gather_fusion
  11.9 0.6 gather_fusion.1
  12.8 0.2 copy.32.cols
  12.9 0.2 copy.38
  13.2 0.3 copy.37.rows
  13.6 6.0 %factors.2 = (bf16[2,768,736]{2,1,0:T(8,128)(2,1)S(1)}, bf16[2,768,736]{2,1,0:T(8,128)(2,1)S(1)}) custom-call(f32[3]{0:T(128)S(1)} %copy-done.3, f32[768,16]{1,0:T(8,128)S(1)} %bitcast.25, f32[736,16]{1,0:T(8,128)S(1)} %copy.32.cols), custom_call_target="tpu_custom_call" | custom-call | flops 108527616 | bytes 4521984 | tf_op jit(solution)/shard_map/factors/pallas_call | solution.py:136
  19.6 1.5 copy-done.4
  21.1 1.4 copy-done.5
  22.5 20.7 %factors.3 = (bf16[2,1536,1536]{2,1,0:T(8,128)(2,1)S(1)}, bf16[2,1536,1536]{2,1,0:T(8,128)(2,1)S(1)}) custom-call(f32[3]{0:T(128)S(1)} %copy-done.3, f32[1536,16]{1,0:T(8,128)S(1)} %copy.37.rows, f32[1536,16]{1,0:T(8,128)S(1)} %pad.19.cols), custom_call_target="tpu_custom_call" | custom-call | flops 452984832 | bytes 18874368 | tf_op jit(solution)/shard_map/factors/pallas_call | solution.py:136
  43.2 3.6 %copy-done = bf16[2,1536,1536]{2,1,0:T(8,128)(2,1)} copy-done((bf16[2,1536,1536]{2,1,0:T(8,128)(2,1)}, bf16[2,1536,1536]{2,1,0:T(8,128)(2,1)S(1)}, u32[]{:S(2)}) %copy-start) | copy-done | bytes 9437208
  46.8 3.6 %copy-done.1 = bf16[2,1536,1536]{2,1,0:T(8,128)(2,1)} copy-done((bf16[2,1536,1536]{2,1,0:T(8,128)(2,1)}, bf16[2,1536,1536]{2,1,0:T(8,128)(2,1)S(1)}, u32[]{:S(2)}) %copy-start.1) | copy-done | bytes 9437208
  50.4 26.9 %all-to-all-done = f32[16,552,128]{2,1,0:T(8,128)} async-done(((f32[16,552,128]{2,1,0:T(8,128)}), f32[16,552,128]{2,1,0:T(8,128)}, u32[]{:S(2)}, u32[]{:S(2)}) %all-to-all-start) | async-done | bytes 4522016 | tf_op jit(solution)/shard_map/all_to_all | solution.py:287
  77.4 6.3 %lat_products.5 = (f32[544,128]{1,0:T(8,128)S(1)}, f32[544,128]{1,0:T(8,128)S(1)}, f32[544,128]{1,0:T(8,128)S(1)}, f32[544,128]{1,0:T(8,128)S(1)}, f32[544,128]{...) custom-call(f32[8832,128]{1,0:T(8,128)} %bitcast.3.moved, ...), custom_call_target="tpu_custom_call" | custom-call | flops 2717908992 | bytes 10000000 | tf_op jit(solution)/shard_map/lat_products/pallas_call | solution.py:189
  83.7 1.6 collective-permute-start.14
  85.2 5.1 %collective-permute-start.15 = (f32[544,128]{1,0:T(8,128)S(1)}, f32[544,128]{1,0:T(8,128)S(1)}, u32[]{:S(2)}, u32[]{:S(2)}) collective-permute-start(f32[544,128]{1,0:T(8,128)S(1)} %get-tuple-element.65), channel_id=1, source_target_pairs={{0,96},{16,112},{32,64},{48,80},{64,32},{80,48},{96,0},{112,16},{1... | collective-permute-start | bytes 835592 | tf_op jit(solution)/shard_map/ppermute | solution.py:306
  90.3 0.6 collective-permute-start.16
  90.9 0.5 collective-permute-start.17
  91.4 1.8 %collective-permute-start.18 = (f32[544,128]{1,0:T(8,128)S(1)}, f32[544,128]{1,0:T(8,128)S(1)}, u32[]{:S(2)}, u32[]{:S(2)}) collective-permute-start(f32[544,128]{1,0:T(8,128)S(1)} %get-tuple-element.68), channel_id=1, source_target_pairs={{0,32},{16,48},{32,0},{48,16},{64,96},{80,112},{96,64},{112,80},{1... | collective-permute-start | bytes 835592 | tf_op jit(solution)/shard_map/ppermute | solution.py:306
  93.2 4.1 %collective-permute-start.19 = (f32[544,128]{1,0:T(8,128)S(1)}, f32[544,128]{1,0:T(8,128)S(1)}, u32[]{:S(2)}, u32[]{:S(2)}) collective-permute-start(f32[544,128]{1,0:T(8,128)S(1)} %get-tuple-element.69), channel_id=1, source_target_pairs={{0,80},{16,64},{32,112},{48,96},{64,16},{80,0},{96,48},{112,32},{1... | collective-permute-start | bytes 835592 | tf_op jit(solution)/shard_map/ppermute | solution.py:306
  97.4 6.4 %lat_products.4 = (f32[544,128]{1,0:T(8,128)S(1)}, f32[544,128]{1,0:T(8,128)S(1)}, f32[544,128]{1,0:T(8,128)S(1)}, f32[544,128]{1,0:T(8,128)S(1)}, f32[544,128]{...) custom-call(f32[8832,128]{1,0:T(8,128)} %bitcast.3.moved, ...), custom_call_target="tpu_custom_call" | custom-call | flops 2717908992 | bytes 10000000 | tf_op jit(solution)/shard_map/lat_products/pallas_call | solution.py:189
  103.8 1.9 %collective-permute-start.20 = (f32[544,128]{1,0:T(8,128)S(1)}, f32[544,128]{1,0:T(8,128)S(1)}, u32[]{:S(2)}, u32[]{:S(2)}) collective-permute-start(f32[544,128]{1,0:T(8,128)S(1)} %get-tuple-element.70), channel_id=1, source_target_pairs={{0,112},{16,96},{32,80},{48,64},{64,48},{80,32},{96,16},{112,0},{1... | collective-permute-start | bytes 835592 | tf_op jit(solution)/shard_map/ppermute | solution.py:306
  105.7 0.3 collective-permute-done.16.refs_3_
  106.1 0.3 collective-permute-start.7
  106.4 6.5 %collective-permute-done.17.refs_4_ = f32[544,128]{1,0:T(8,128)S(1)} collective-permute-done((f32[544,128]{1,0:T(8,128)S(1)}, f32[544,128]{1,0:T(8,128)S(1)}, u32[]{:S(2)}, u32[]{:S(2)}) %collective-permute-start.17) | collective-permute-done | bytes 278560 | tf_op jit(solution)/shard_map/ppermute | solution.py:306
  112.9 2.6 %collective-permute-start.8 = (f32[544,128]{1,0:T(8,128)S(1)}, f32[544,128]{1,0:T(8,128)S(1)}, u32[]{:S(2)}, u32[]{:S(2)}) collective-permute-start(f32[544,128]{1,0:T(8,128)S(1)} %get-tuple-element.57), channel_id=1, source_target_pairs={{0,96},{16,112},{32,64},{48,80},{64,32},{80,48},{96,0},{112,16},{1... | collective-permute-start | bytes 835592 | tf_op jit(solution)/shard_map/ppermute | solution.py:306
  115.5 0.6 collective-permute-start.9
  116.1 2.1 %collective-permute-start.10 = (f32[544,128]{1,0:T(8,128)S(1)}, f32[544,128]{1,0:T(8,128)S(1)}, u32[]{:S(2)}, u32[]{:S(2)}) collective-permute-start(f32[544,128]{1,0:T(8,128)S(1)} %get-tuple-element.59), channel_id=1, source_target_pairs={{0,48},{16,32},{32,16},{48,0},{64,112},{80,96},{96,80},{112,64},{1... | collective-permute-start | bytes 835592 | tf_op jit(solution)/shard_map/ppermute | solution.py:306
  118.2 6.3 %lat_products.3 = (f32[544,128]{1,0:T(8,128)S(1)}, f32[544,128]{1,0:T(8,128)S(1)}, f32[544,128]{1,0:T(8,128)S(1)}, f32[544,128]{1,0:T(8,128)S(1)}, f32[544,128]{...) custom-call(f32[8832,128]{1,0:T(8,128)} %bitcast.3.moved, ...), custom_call_target="tpu_custom_call" | custom-call | flops 2717908992 | bytes 10000000 | tf_op jit(solution)/shard_map/lat_products/pallas_call | solution.py:189
  124.5 2.7 %collective-permute-done.20.refs_7_ = f32[544,128]{1,0:T(8,128)S(1)} collective-permute-done((f32[544,128]{1,0:T(8,128)S(1)}, f32[544,128]{1,0:T(8,128)S(1)}, u32[]{:S(2)}, u32[]{:S(2)}) %collective-permute-start.20) | collective-permute-done | bytes 278560 | tf_op jit(solution)/shard_map/ppermute | solution.py:306
  127.2 1.7 collective-permute-start.12
  128.9 4.8 %collective-permute-start.13 = (f32[544,128]{1,0:T(8,128)S(1)}, f32[544,128]{1,0:T(8,128)S(1)}, u32[]{:S(2)}, u32[]{:S(2)}) collective-permute-start(f32[544,128]{1,0:T(8,128)S(1)} %get-tuple-element.62), channel_id=1, source_target_pairs={{0,112},{16,96},{32,80},{48,64},{64,48},{80,32},{96,16},{112,0},{1... | collective-permute-start | bytes 835592 | tf_op jit(solution)/shard_map/ppermute | solution.py:306
  133.7 1.6 collective-permute-done.9.refs_3_
  135.3 1.5 collective-permute-done.10.refs_4_
  136.8 3.5 %collective-permute-start.1 = (f32[544,128]{1,0:T(8,128)S(1)}, f32[544,128]{1,0:T(8,128)S(1)}, u32[]{:S(2)}, u32[]{:S(2)}) collective-permute-start(f32[544,128]{1,0:T(8,128)S(1)} %get-tuple-element.47), channel_id=1, source_target_pairs={{0,96},{16,112},{32,64},{48,80},{64,32},{80,48},{96,0},{112,16},{1... | collective-permute-start | bytes 835592 | tf_op jit(solution)/shard_map/ppermute | solution.py:306
  140.3 7.4 %lon_products.3.refs_10_ = f32[2,2,2,90,2,1440]{5,4,3,2,1,0:T(2,128)} custom-call(f32[544,128]{1,0:T(8,128)S(1)} %get-tuple-element.63.refs_0_, f32[544,128]{1,0:T(8,128)S(1)} %collective-permute-done.14.refs_1_, f32[544,128]{1,0:T(8,128)S(1)} %collective-permute-done.15.refs_2_, f32[544,128]{1,0:T(8,128)S(1)} %collective-permute-done.16.refs_3_, ...), custom_call_target="tpu_custom_call" | custom-call | flops 5096079360 | bytes 20000000 | tf_op jit(solution)/shard_map/lon_products/pallas_call | solution.py:262
  147.7 0.7 collective-permute-start.2
  148.4 2.9 %collective-permute-start.3 = (f32[544,128]{1,0:T(8,128)S(1)}, f32[544,128]{1,0:T(8,128)S(1)}, u32[]{:S(2)}, u32[]{:S(2)}) collective-permute-start(f32[544,128]{1,0:T(8,128)S(1)} %get-tuple-element.49), channel_id=1, source_target_pairs={{0,80},{16,64},{32,112},{48,96},{64,16},{80,0},{96,48},{112,32},{1... | collective-permute-start | bytes 835592 | tf_op jit(solution)/shard_map/ppermute | solution.py:306
  151.3 2.4 %collective-permute-start.4 = (f32[544,128]{1,0:T(8,128)S(1)}, f32[544,128]{1,0:T(8,128)S(1)}, u32[]{:S(2)}, u32[]{:S(2)}) collective-permute-start(f32[544,128]{1,0:T(8,128)S(1)} %get-tuple-element.50), channel_id=1, source_target_pairs={{0,112},{16,96},{32,80},{48,64},{64,48},{80,32},{96,16},{112,0},{1... | collective-permute-start | bytes 835592 | tf_op jit(solution)/shard_map/ppermute | solution.py:306
  153.7 0.8 collective-permute-start.5
  154.5 2.5 %collective-permute-start.6 = (f32[544,128]{1,0:T(8,128)S(1)}, f32[544,128]{1,0:T(8,128)S(1)}, u32[]{:S(2)}, u32[]{:S(2)}) collective-permute-start(f32[544,128]{1,0:T(8,128)S(1)} %get-tuple-element.52), channel_id=1, source_target_pairs={{0,32},{16,48},{32,0},{48,16},{64,96},{80,112},{96,64},{112,80},{1... | collective-permute-start | bytes 835592 | tf_op jit(solution)/shard_map/ppermute | solution.py:306
  157.0 13.1 %lon_products.4.refs_10_ = f32[2,2,2,90,2,1440]{5,4,3,2,1,0:T(2,128)} custom-call(f32[544,128]{1,0:T(8,128)S(1)} %get-tuple-element.55.refs_0_, f32[544,128]{1,0:T(8,128)S(1)} %collective-permute-done.7.refs_1_, f32[544,128]{1,0:T(8,128)S(1)} %collective-permute-done.8.refs_2_, ...), custom_call_target="tpu_custom_call", output_to_operand_aliasing={{}: (10, {})} | custom-call | flops 10192158720 | bytes 20000000 | tf_op jit(solution)/shard_map/lon_products/pallas_call | solution.py:262
  170.1 0.6 collective-permute-done.4.refs_5_
  170.7 0.9 collective-permute-done.5.refs_6_
  171.6 7.4 %lon_products.5 = f32[2,2,2,90,2,1440]{5,4,3,2,1,0:T(2,128)} custom-call(f32[544,128]{1,0:T(8,128)S(1)} %get-tuple-element.45.refs_0_, f32[544,128]{1,0:T(8,128)S(1)} %collective-permute-done.refs_1_, f32[544,128]{1,0:T(8,128)S(1)} %collective-permute-done.1.refs_2_, f32[544,128]{1,0:T(8,128)S(1)} %collective-permute-done.2.refs_3_, ...), custom_call_target="tpu_custom_call", output_to_operand_aliasing={{}: (10, {})} | custom-call | flops 5096079360 | bytes 20000000 | tf_op jit(solution)/shard_map/lon_products/pallas_call | solution.py:262
  (53 shorter events, 0.7 us)
Async XLA Ops:
  4.9 5.7 %copy-start.7 = (f32[720,16]{0,1:T(8,128)S(1)}, f32[720,16]{0,1:T(8,128)}, u32[]{:S(2)}) copy-start(f32[720,16]{0,1:T(8,128)} %param.10) | copy-start | bytes 138244
  4.9 5.9 %copy-start.6 = (f32[1440,16]{0,1:T(8,128)S(1)}, f32[1440,16]{0,1:T(8,128)}, u32[]{:S(2)}) copy-start(f32[1440,16]{0,1:T(8,128)} %param.9) | copy-start | bytes 276484
  4.9 6.4 %copy-start.8 = (s32[8]{0:T(128)S(1)}, s32[8]{0:T(128)}, u32[]{:S(2)}) copy-start(s32[8]{0:T(128)} %constant.15.clone) | copy-start | bytes 100
  4.9 72.4 %all-to-all-start = ((f32[16,552,128]{2,1,0:T(8,128)}), f32[16,552,128]{2,1,0:T(8,128)}, u32[]{:S(2)}, u32[]{:S(2)}) async-start(f32[16,552,128]{2,1,0:T(8,128)} %day_products.1), calls=%async_computation | async-start | bytes 9043968 | tf_op jit(solution)/shard_map/all_to_all | solution.py:287
  10.9 2.7 %copy-start.3 = (f32[3]{0:T(128)S(1)}, f32[3]{0:T(128)}, u32[]{:S(2)}) copy-start(f32[3]{0:T(128)} %scales.5) | copy-start | bytes 40
  19.6 1.5 copy-start.4
  21.1 1.4 copy-start.5
  43.2 3.6 %copy-start = (bf16[2,1536,1536]{2,1,0:T(8,128)(2,1)}, bf16[2,1536,1536]{2,1,0:T(8,128)(2,1)S(1)}, u32[]{:S(2)}) copy-start(bf16[2,1536,1536]{2,1,0:T(8,128)(2,1)S(1)} %get-tuple-element.53.refs_8_) | copy-start | bytes 28311556
  46.8 3.6 %copy-start.1 = (bf16[2,1536,1536]{2,1,0:T(8,128)(2,1)}, bf16[2,1536,1536]{2,1,0:T(8,128)(2,1)S(1)}, u32[]{:S(2)}) copy-start(bf16[2,1536,1536]{2,1,0:T(8,128)(2,1)S(1)} %get-tuple-element.54.refs_9_) | copy-start | bytes 28311556
  83.7 9.6 %collective-permute-start.14 = (f32[544,128]{1,0:T(8,128)S(1)}, f32[544,128]{1,0:T(8,128)S(1)}, u32[]{:S(2)}, u32[]{:S(2)}) collective-permute-start(f32[544,128]{1,0:T(8,128)S(1)} %get-tuple-element.64), channel_id=1, source_target_pairs={{0,16},{16,0},{32,48},{48,32},{64,80},{80,64},{96,112},{112,96},{1... | collective-permute-start | bytes 835592 | tf_op jit(solution)/shard_map/ppermute | solution.py:306
  85.2 18.6 %collective-permute-start.15 = (f32[544,128]{1,0:T(8,128)S(1)}, f32[544,128]{1,0:T(8,128)S(1)}, u32[]{:S(2)}, u32[]{:S(2)}) collective-permute-start(f32[544,128]{1,0:T(8,128)S(1)} %get-tuple-element.65), channel_id=1, source_target_pairs={{0,96},{16,112},{32,64},{48,80},{64,32},{80,48},{96,0},{112,16},{1... | collective-permute-start | bytes 835592 | tf_op jit(solution)/shard_map/ppermute | solution.py:306
  90.3 15.8 %collective-permute-start.16 = (f32[544,128]{1,0:T(8,128)S(1)}, f32[544,128]{1,0:T(8,128)S(1)}, u32[]{:S(2)}, u32[]{:S(2)}) collective-permute-start(f32[544,128]{1,0:T(8,128)S(1)} %get-tuple-element.66), channel_id=1, source_target_pairs={{0,64},{16,80},{32,96},{48,112},{64,0},{80,16},{96,32},{112,48},{1... | collective-permute-start | bytes 835592 | tf_op jit(solution)/shard_map/ppermute | solution.py:306
  90.9 21.9 %collective-permute-start.17 = (f32[544,128]{1,0:T(8,128)S(1)}, f32[544,128]{1,0:T(8,128)S(1)}, u32[]{:S(2)}, u32[]{:S(2)}) collective-permute-start(f32[544,128]{1,0:T(8,128)S(1)} %get-tuple-element.67), channel_id=1, source_target_pairs={{0,48},{16,32},{32,16},{48,0},{64,112},{80,96},{96,80},{112,64},{1... | collective-permute-start | bytes 835592 | tf_op jit(solution)/shard_map/ppermute | solution.py:306
  91.4 24.1 %collective-permute-start.18 = (f32[544,128]{1,0:T(8,128)S(1)}, f32[544,128]{1,0:T(8,128)S(1)}, u32[]{:S(2)}, u32[]{:S(2)}) collective-permute-start(f32[544,128]{1,0:T(8,128)S(1)} %get-tuple-element.68), channel_id=1, source_target_pairs={{0,32},{16,48},{32,0},{48,16},{64,96},{80,112},{96,64},{112,80},{1... | collective-permute-start | bytes 835592 | tf_op jit(solution)/shard_map/ppermute | solution.py:306
  93.2 22.9 %collective-permute-start.19 = (f32[544,128]{1,0:T(8,128)S(1)}, f32[544,128]{1,0:T(8,128)S(1)}, u32[]{:S(2)}, u32[]{:S(2)}) collective-permute-start(f32[544,128]{1,0:T(8,128)S(1)} %get-tuple-element.69), channel_id=1, source_target_pairs={{0,80},{16,64},{32,112},{48,96},{64,16},{80,0},{96,48},{112,32},{1... | collective-permute-start | bytes 835592 | tf_op jit(solution)/shard_map/ppermute | solution.py:306
  97.4 42.9 %slice-start = ((s8[9437184]{0:T(1024)(128)(4,1)}), s8[4194304]{0:T(1024)(128)(4,1)S(1)}, s32[]{:S(2)}) async-start(s8[9437184]{0:T(1024)(128)(4,1)} %bitcast.23), calls=%async_computation.1 | async-start | bytes 8388608
  97.4 42.9 %slice-start.1 = ((s8[9437184]{0:T(1024)(128)(4,1)}), s8[4194304]{0:T(1024)(128)(4,1)S(1)}, s32[]{:S(2)}) async-start(s8[9437184]{0:T(1024)(128)(4,1)} %bitcast.23), calls=%async_computation.2 | async-start | bytes 8388608
  97.4 42.9 %copy-start.2 = (bf16[2,1536,1536]{2,1,0:T(8,128)(2,1)S(1)}, bf16[2,1536,1536]{2,1,0:T(8,128)(2,1)}, u32[]{:S(2)}) copy-start(bf16[2,1536,1536]{2,1,0:T(8,128)(2,1)} %copy-done.1) | copy-start | bytes 28311556
  103.8 23.3 %collective-permute-start.20 = (f32[544,128]{1,0:T(8,128)S(1)}, f32[544,128]{1,0:T(8,128)S(1)}, u32[]{:S(2)}, u32[]{:S(2)}) collective-permute-start(f32[544,128]{1,0:T(8,128)S(1)} %get-tuple-element.70), channel_id=1, source_target_pairs={{0,112},{16,96},{32,80},{48,64},{64,48},{80,32},{96,16},{112,0},{1... | collective-permute-start | bytes 835592 | tf_op jit(solution)/shard_map/ppermute | solution.py:306
  106.1 21.1 %collective-permute-start.7 = (f32[544,128]{1,0:T(8,128)S(1)}, f32[544,128]{1,0:T(8,128)S(1)}, u32[]{:S(2)}, u32[]{:S(2)}) collective-permute-start(f32[544,128]{1,0:T(8,128)S(1)} %get-tuple-element.56), channel_id=1, source_target_pairs={{0,16},{16,0},{32,48},{48,32},{64,80},{80,64},{96,112},{112,96},{1... | collective-permute-start | bytes 835592 | tf_op jit(solution)/shard_map/ppermute | solution.py:306
  112.9 16.1 %collective-permute-start.8 = (f32[544,128]{1,0:T(8,128)S(1)}, f32[544,128]{1,0:T(8,128)S(1)}, u32[]{:S(2)}, u32[]{:S(2)}) collective-permute-start(f32[544,128]{1,0:T(8,128)S(1)} %get-tuple-element.57), channel_id=1, source_target_pairs={{0,96},{16,112},{32,64},{48,80},{64,32},{80,48},{96,0},{112,16},{1... | collective-permute-start | bytes 835592 | tf_op jit(solution)/shard_map/ppermute | solution.py:306
  115.5 19.8 %collective-permute-start.9 = (f32[544,128]{1,0:T(8,128)S(1)}, f32[544,128]{1,0:T(8,128)S(1)}, u32[]{:S(2)}, u32[]{:S(2)}) collective-permute-start(f32[544,128]{1,0:T(8,128)S(1)} %get-tuple-element.58), channel_id=1, source_target_pairs={{0,64},{16,80},{32,96},{48,112},{64,0},{80,16},{96,32},{112,48},{1... | collective-permute-start | bytes 835592 | tf_op jit(solution)/shard_map/ppermute | solution.py:306
  116.1 24.2 %slice-start.2 = ((s8[9437184]{0:T(1024)(128)(4,1)}), s8[1048576]{0:T(1024)(128)(4,1)S(1)}, s32[]{:S(2)}) async-start(s8[9437184]{0:T(1024)(128)(4,1)} %bitcast.23), calls=%async_computation.3 | async-start | bytes 2097152
  116.1 20.7 %collective-permute-start.10 = (f32[544,128]{1,0:T(8,128)S(1)}, f32[544,128]{1,0:T(8,128)S(1)}, u32[]{:S(2)}, u32[]{:S(2)}) collective-permute-start(f32[544,128]{1,0:T(8,128)S(1)} %get-tuple-element.59), channel_id=1, source_target_pairs={{0,48},{16,32},{32,16},{48,0},{64,112},{80,96},{96,80},{112,64},{1... | collective-permute-start | bytes 835592 | tf_op jit(solution)/shard_map/ppermute | solution.py:306
  127.2 20.6 %collective-permute-start.11 = (f32[544,128]{1,0:T(8,128)S(1)}, f32[544,128]{1,0:T(8,128)S(1)}, u32[]{:S(2)}, u32[]{:S(2)}) collective-permute-start(f32[544,128]{1,0:T(8,128)S(1)} %get-tuple-element.60), channel_id=1, source_target_pairs={{0,32},{16,48},{32,0},{48,16},{64,96},{80,112},{96,64},{112,80},{1... | collective-permute-start | bytes 835592 | tf_op jit(solution)/shard_map/ppermute | solution.py:306
  127.2 21.2 %collective-permute-start.12 = (f32[544,128]{1,0:T(8,128)S(1)}, f32[544,128]{1,0:T(8,128)S(1)}, u32[]{:S(2)}, u32[]{:S(2)}) collective-permute-start(f32[544,128]{1,0:T(8,128)S(1)} %get-tuple-element.61), channel_id=1, source_target_pairs={{0,80},{16,64},{32,112},{48,96},{64,16},{80,0},{96,48},{112,32},{1... | collective-permute-start | bytes 835592 | tf_op jit(solution)/shard_map/ppermute | solution.py:306
  128.9 22.3 %collective-permute-start.13 = (f32[544,128]{1,0:T(8,128)S(1)}, f32[544,128]{1,0:T(8,128)S(1)}, u32[]{:S(2)}, u32[]{:S(2)}) collective-permute-start(f32[544,128]{1,0:T(8,128)S(1)} %get-tuple-element.62), channel_id=1, source_target_pairs={{0,112},{16,96},{32,80},{48,64},{64,48},{80,32},{96,16},{112,0},{1... | collective-permute-start | bytes 835592 | tf_op jit(solution)/shard_map/ppermute | solution.py:306
  135.3 18.4 %collective-permute-start = (f32[544,128]{1,0:T(8,128)S(1)}, f32[544,128]{1,0:T(8,128)S(1)}, u32[]{:S(2)}, u32[]{:S(2)}) collective-permute-start(f32[544,128]{1,0:T(8,128)S(1)} %get-tuple-element.46), channel_id=1, source_target_pairs={{0,16},{16,0},{32,48},{48,32},{64,80},{80,64},{96,112},{112,96},{1... | collective-permute-start | bytes 835592 | tf_op jit(solution)/shard_map/ppermute | solution.py:306
  136.8 17.7 %collective-permute-start.1 = (f32[544,128]{1,0:T(8,128)S(1)}, f32[544,128]{1,0:T(8,128)S(1)}, u32[]{:S(2)}, u32[]{:S(2)}) collective-permute-start(f32[544,128]{1,0:T(8,128)S(1)} %get-tuple-element.47), channel_id=1, source_target_pairs={{0,96},{16,112},{32,64},{48,80},{64,32},{80,48},{96,0},{112,16},{1... | collective-permute-start | bytes 835592 | tf_op jit(solution)/shard_map/ppermute | solution.py:306
  147.7 22.3 %collective-permute-start.2 = (f32[544,128]{1,0:T(8,128)S(1)}, f32[544,128]{1,0:T(8,128)S(1)}, u32[]{:S(2)}, u32[]{:S(2)}) collective-permute-start(f32[544,128]{1,0:T(8,128)S(1)} %get-tuple-element.48), channel_id=1, source_target_pairs={{0,64},{16,80},{32,96},{48,112},{64,0},{80,16},{96,32},{112,48},{1... | collective-permute-start | bytes 835592 | tf_op jit(solution)/shard_map/ppermute | solution.py:306
  148.4 21.6 %collective-permute-start.3 = (f32[544,128]{1,0:T(8,128)S(1)}, f32[544,128]{1,0:T(8,128)S(1)}, u32[]{:S(2)}, u32[]{:S(2)}) collective-permute-start(f32[544,128]{1,0:T(8,128)S(1)} %get-tuple-element.49), channel_id=1, source_target_pairs={{0,80},{16,64},{32,112},{48,96},{64,16},{80,0},{96,48},{112,32},{1... | collective-permute-start | bytes 835592 | tf_op jit(solution)/shard_map/ppermute | solution.py:306
  151.3 19.4 %collective-permute-start.4 = (f32[544,128]{1,0:T(8,128)S(1)}, f32[544,128]{1,0:T(8,128)S(1)}, u32[]{:S(2)}, u32[]{:S(2)}) collective-permute-start(f32[544,128]{1,0:T(8,128)S(1)} %get-tuple-element.50), channel_id=1, source_target_pairs={{0,112},{16,96},{32,80},{48,64},{64,48},{80,32},{96,16},{112,0},{1... | collective-permute-start | bytes 835592 | tf_op jit(solution)/shard_map/ppermute | solution.py:306
  153.7 17.9 %collective-permute-start.5 = (f32[544,128]{1,0:T(8,128)S(1)}, f32[544,128]{1,0:T(8,128)S(1)}, u32[]{:S(2)}, u32[]{:S(2)}) collective-permute-start(f32[544,128]{1,0:T(8,128)S(1)} %get-tuple-element.51), channel_id=1, source_target_pairs={{0,48},{16,32},{32,16},{48,0},{64,112},{80,96},{96,80},{112,64},{1... | collective-permute-start | bytes 835592 | tf_op jit(solution)/shard_map/ppermute | solution.py:306
  154.5 17.1 %collective-permute-start.6 = (f32[544,128]{1,0:T(8,128)S(1)}, f32[544,128]{1,0:T(8,128)S(1)}, u32[]{:S(2)}, u32[]{:S(2)}) collective-permute-start(f32[544,128]{1,0:T(8,128)S(1)} %get-tuple-element.52), channel_id=1, source_target_pairs={{0,32},{16,48},{32,0},{48,16},{64,96},{80,112},{96,64},{112,80},{1... | collective-permute-start | bytes 835592 | tf_op jit(solution)/shard_map/ppermute | solution.py:306
